TPU v7x, 32 devices: a whole 2x2x4 slice. The times are simulated.
32 devices in a mesh: row: 8 (over y, x, core), col: 4 (over z).
Axes of the slice: x: 2, y: 2, z: 4, core: 2. Of those that a mesh axis runs over, the one named last changes fastest.
Arguments:
- token_ids: int32 [8192], P('row'), may hold values from 0 to 31999
- target_ids: int32 [1024], P('row'), may hold values from 0 to 31999
- loss_slots: int32 [1024], P('row'), may hold values from 0 to 1023
- valid_mask: int32 [1024], replicated, may hold values 0 or 1
- prefix_lens: int32 [8], replicated, may hold values from 0 to 1023
- embed_table: float32 [32000, 1152], P('col', 'row'), may hold values from -0.375 to 0.375
- norm_gains: float32 [3, 1152], replicated, may hold values from 0.5 to 1.5
- qkv_weight: float32 [1152, 1920], P('row', 'col'), may hold values from -0.1875 to 0.1875
- output_weight: float32 [1152, 1152], P('row', 'col'), may hold values from -3 to 3
- mlp_weight: float32 [3, 1152, 3072], P(None, 'row', 'col'), may hold values from -0.1875 to 0.1875
- embed_mean: float32 [32000, 1152], P('col', 'row'), may hold values from -0.05 to 0.05
- embed_square: float32 [32000, 1152], P('col', 'row'), may hold values from 2e-05 to 0.0002
- gain_mean: float32 [3, 1152], replicated, may hold values from -0.05 to 0.05
- gain_square: float32 [3, 1152], replicated, may hold values from 2e-05 to 0.0002
- qkv_mean: float32 [1152, 1920], P('row', 'col'), may hold values from -0.05 to 0.05
- qkv_square: float32 [1152, 1920], P('row', 'col'), may hold values from 2e-05 to 0.0002
- out_mean: float32 [1152, 1152], P('row', 'col'), may hold values from -0.00390625 to 0.00390625
- out_square: float32 [1152, 1152], P('row', 'col'), may hold values from 9.765625e-08 to 9.765625e-07
- mlp_mean: float32 [3, 1152, 3072], P(None, 'row', 'col'), may hold values from -0.01953125 to 0.01953125
- mlp_square: float32 [3, 1152, 3072], P(None, 'row', 'col'), may hold values from 1.953125e-06 to 1.953125e-05
- left_bases: float32 [5, 1152, 1152], P(None, 'row'), may hold values from -0.1875 to 0.1875
- qkv_bases: float32 [1920, 1920], P('col'), may hold values from -0.125 to 0.125
- out_bases: float32 [1152, 1152], P('col'), may hold values from -0.1875 to 0.1875
- feedforward_bases: float32 [3, 3072, 3072], P(None, 'col'), may hold values from -0.109375 to 0.109375
Outputs:
- loss_value: float32 [], replicated
- embed_next: float32 [32000, 1152], P('col', 'row')
- embed_moment: float32 [32000, 1152], P('col', 'row')
- embed_scale: float32 [32000, 1152], P('col', 'row')
- gain_update: float32 [3, 1152], replicated
- gain_moment: float32 [3, 1152], replicated
- gain_scale: float32 [3, 1152], replicated
- qkv_next: float32 [1152, 1920], P('row', 'col')
- qkv_moment: float32 [1152, 1920], P('row', 'col')
- qkv_scale: float32 [1152, 1920], P('row', 'col')
- out_update: float32 [1152, 1152], P('row', 'col')
- out_moment: float32 [1152, 1152], P('row', 'col')
- out_scale: float32 [1152, 1152], P('row', 'col')
- mlp_next: float32 [3, 1152, 3072], P(None, 'row', 'col')
- mlp_moment: float32 [3, 1152, 3072], P(None, 'row', 'col')
- mlp_scale: float32 [3, 1152, 3072], P(None, 'row', 'col')
All inputs are finite; a program needn't handle non-finite values.
Results may differ from a plain program's by a relative error of at most 0.018.
Values may be sent and summed in bfloat16 or wider, within the bound.
A program may use at most 320 MiB of HBM per device.

v0:
```python
import jax
import jax.numpy as jnp
from jax import lax
from jax.sharding import PartitionSpec as P

Q_HEADS = 18
KV_HEADS = 6
HEAD = 64
LEN = 1024
PICK = 128


NORM_EPSILON = 1e-05
ADAM_EPSILON = 1e-08
MOMENT_BETA = 0.5
SOAP_RATE = 0.05
ADAM_RATE = 0.01
WEIGHT_DECAY = 0.1
MASK_VALUE = -1e30
FULL_PRECISION = lax.Precision.HIGHEST


def merged(value, axis, combine):
    everything = jax.tree.map(lambda part: lax.all_gather(part, axis), value)
    leading = jax.tree.map(lambda part: part[0], everything)

    def lap(k, so_far):
        return combine(so_far, jax.tree.map(lambda part: part[k], everything))

    return lax.fori_loop(1, lax.axis_size(axis), lap, leading)


def rms_norm(values, gain_vec):
    return (
        values
        * lax.rsqrt(jnp.mean(values * values, axis=-1, keepdims=True) + NORM_EPSILON)
        * gain_vec
    )


def rotary(values, positions):
    half_width = values.shape[-1] // 2
    frequency = jnp.power(10000.0, -jnp.arange(half_width, dtype=jnp.float32) / half_width)
    angles = positions[:, None].astype(jnp.float32) * frequency[None, :]
    cosine = jnp.cos(angles)[:, None, :]
    sine_part = jnp.sin(angles)[:, None, :]
    first_half = values[..., :half_width]
    second_half = values[..., half_width:]
    return jnp.concatenate(
        [
            first_half * cosine - second_half * sine_part,
            second_half * cosine + first_half * sine_part,
        ],
        axis=-1,
    )


def swiglu(gate_part, upward):
    return jax.nn.silu(gate_part) * upward


def matmul(left_op, right_op):
    return jnp.dot(left_op, right_op, preferred_element_type=jnp.float32)


def matmul_last(left_op, right_op):
    return lax.dot_general(
        left_op, right_op, (((1,), (1,)), ((), ())), preferred_element_type=jnp.float32
    )


def matmul_first(left_op, right_op):
    return lax.dot_general(
        left_op, right_op, (((0,), (0,)), ((), ())), preferred_element_type=jnp.float32
    )


def exact_dot(left_op, right_op):
    return jnp.dot(left_op, right_op, precision=FULL_PRECISION, preferred_element_type=jnp.float32)


def exact_last(left_op, right_op):
    return lax.dot_general(
        left_op,
        right_op,
        (((1,), (1,)), ((), ())),
        precision=FULL_PRECISION,
        preferred_element_type=jnp.float32,
    )


def exact_first(left_op, right_op):
    return lax.dot_general(
        left_op,
        right_op,
        (((0,), (0,)), ((), ())),
        precision=FULL_PRECISION,
        preferred_element_type=jnp.float32,
    )


def token_rows(values):
    return lax.all_gather(values, "col", axis=0, tiled=True)


def token_sums(term):
    return lax.psum_scatter(
        term.astype(jnp.bfloat16), "col", scatter_dimension=0, tiled=True
    ).astype(jnp.float32)


def to_heads(values):
    return lax.all_to_all(values, "col", split_axis=0, concat_axis=1, tiled=True)


def from_heads(values):
    return lax.all_to_all(values, "col", split_axis=1, concat_axis=0, tiled=True)


def combine_totals(earlier, latter):
    largest = jnp.maximum(earlier[0], latter[0])
    exponent_total = earlier[1] * jnp.exp(earlier[0] - largest) + latter[1] * jnp.exp(
        latter[0] - largest
    )
    return (largest, exponent_total, earlier[2] + latter[2])


def norm_back(values, gain_vec, grad_output):
    unused, pull_back = jax.vjp(rms_norm, values, gain_vec)
    return pull_back(grad_output)


def moments(rotated, moment, square_avg):
    moment_new = MOMENT_BETA * moment + (1.0 - MOMENT_BETA) * rotated
    square_new = MOMENT_BETA * square_avg + (1.0 - MOMENT_BETA) * rotated * rotated
    return (moment_new, square_new, moment_new / (jnp.sqrt(square_new) + ADAM_EPSILON))


def adam_update(weight, gradient_value, moment, square_avg, decay_rate):
    moment_new = MOMENT_BETA * moment + (1.0 - MOMENT_BETA) * gradient_value
    square_new = MOMENT_BETA * square_avg + (1.0 - MOMENT_BETA) * gradient_value * gradient_value
    change = -(
        ADAM_RATE * (moment_new / (jnp.sqrt(square_new) + ADAM_EPSILON) + decay_rate * weight)
    )
    return (change, moment_new, square_new)


def per_device(
    token_ids,
    target_ids,
    loss_slots,
    valid_mask,
    prefix_lens,
    embed_table,
    norm_gains,
    qkv_weight,
    output_weight,
    mlp_weight,
    embed_mean,
    embed_square,
    gain_mean,
    gain_square,
    qkv_mean,
    qkv_square,
    out_mean,
    out_square,
    mlp_mean,
    mlp_square,
    left_bases,
    qkv_bases,
    out_bases,
    feedforward_bases,
):
    row_index = lax.axis_index("row")
    col_index = lax.axis_index("col")
    col_count = lax.axis_size("col")
    group_tokens = token_ids.shape[0]
    pick_count = loss_slots.shape[0]
    device_tokens = group_tokens // col_count
    vocab_shard = embed_table.shape[0]
    query_width = Q_HEADS * HEAD
    kv_width = KV_HEADS * HEAD
    group_size = Q_HEADS // KV_HEADS
    scaling = HEAD ** (-0.5)
    table_full, qkv_full, out_full, mlp_full = (
        lax.all_gather(embed_table.astype(jnp.bfloat16), "row", axis=1, tiled=True),
        lax.all_gather(qkv_weight.astype(jnp.bfloat16), "row", axis=0, tiled=True),
        lax.all_gather(output_weight.astype(jnp.bfloat16), "row", axis=0, tiled=True),
        lax.all_gather(mlp_weight.astype(jnp.bfloat16), "row", axis=1, tiled=True),
    )
    local_ids = token_ids - col_index * vocab_shard
    inside = (local_ids >= 0) & (local_ids < vocab_shard)
    safe_ids = jnp.clip(local_ids, 0, vocab_shard - 1)
    looked = jnp.take(table_full, safe_ids, axis=0)
    embedded = token_sums(jnp.where(inside[:, None], looked.astype(jnp.float32), 0.0))
    normed_all = token_rows(rms_norm(embedded, norm_gains[0]).astype(jnp.bfloat16))
    project = to_heads(matmul(normed_all, qkv_full).astype(jnp.bfloat16))
    first_token = col_index * device_tokens
    positions = (first_token + jnp.arange(device_tokens, dtype=jnp.int32)) % LEN
    seq_global = row_index * (group_tokens // LEN) + first_token // LEN
    seq_prefix = jnp.sum(
        jnp.where(jnp.arange(prefix_lens.shape[0], dtype=jnp.int32) == seq_global, prefix_lens, 0)
    )

    def rotate_here(values):
        return rotary(values, positions)

    queries_raw = project[:, :query_width].astype(jnp.float32).reshape(device_tokens, Q_HEADS, HEAD)
    keys_raw = (
        project[:, query_width : query_width + kv_width]
        .astype(jnp.float32)
        .reshape(device_tokens, KV_HEADS, HEAD)
    )
    queries = (
        rotate_here(queries_raw)
        .astype(jnp.bfloat16)
        .reshape(device_tokens, KV_HEADS, group_size, HEAD)
    )
    keys_local = rotate_here(keys_raw).astype(jnp.bfloat16).reshape(device_tokens, kv_width)
    keys_values = token_rows(
        jnp.concatenate([keys_local, project[:, query_width + kv_width :]], axis=1)
    )
    attn_keys = keys_values[:, :kv_width].reshape(LEN, KV_HEADS, HEAD)
    attn_values = keys_values[:, kv_width:].reshape(LEN, KV_HEADS, HEAD)
    key_positions = jnp.arange(LEN, dtype=jnp.int32)
    allowed = (key_positions[None, :] <= positions[:, None]) | (key_positions[None, :] < seq_prefix)

    def attention_probs():
        raw_scores = (
            jnp.einsum("qhgd,khd->hgqk", queries, attn_keys, preferred_element_type=jnp.float32)
            * scaling
        )
        scores = jnp.where(allowed, raw_scores, MASK_VALUE)
        largest = jnp.max(scores, axis=-1, keepdims=True)
        weights = jnp.exp(scores - largest)
        return weights / jnp.sum(weights, axis=-1, keepdims=True)

    attn_probs = attention_probs()
    attended = jnp.einsum(
        "hgqk,khd->qhgd",
        attn_probs.astype(jnp.bfloat16),
        attn_values,
        preferred_element_type=jnp.float32,
    )
    attended_all = from_heads(attended.reshape(device_tokens, query_width).astype(jnp.bfloat16))
    hidden_one = embedded + token_sums(matmul_last(attended_all, out_full))
    middle_all = token_rows(rms_norm(hidden_one, norm_gains[1]).astype(jnp.bfloat16))
    gate_part = matmul(middle_all, mlp_full[0])
    upward = matmul(middle_all, mlp_full[1])
    inner_act = swiglu(gate_part, upward).astype(jnp.bfloat16)
    hidden_two = hidden_one + token_sums(matmul_last(inner_act, mlp_full[2]))
    final_all = token_rows(rms_norm(hidden_two, norm_gains[2]).astype(jnp.bfloat16))
    pick_rows = jnp.arange(pick_count, dtype=jnp.int32) // PICK * LEN + loss_slots
    final_pick = jnp.take(final_all, pick_rows, axis=0)
    logits = matmul_last(final_pick, table_full)
    local_max = jnp.max(logits, axis=-1)
    local_sum = jnp.sum(jnp.exp(logits - local_max[:, None]), axis=-1)
    target_hit = (
        jnp.arange(vocab_shard, dtype=jnp.int32)[None, :]
        == (target_ids - col_index * vocab_shard)[:, None]
    )
    local_target = jnp.sum(jnp.where(target_hit, logits, 0.0), axis=-1)
    largest, exponent_total, target_logit = merged(
        (local_max, local_sum, local_target), "col", combine_totals
    )
    log_total = largest + jnp.log(exponent_total)
    valid_count = jnp.maximum(jnp.sum(valid_mask).astype(jnp.float32), 1.0)
    row_weights = (
        lax.dynamic_slice_in_dim(valid_mask, row_index * pick_count, pick_count).astype(jnp.float32)
        / valid_count
    )
    loss_part = jnp.where(col_index == 0, jnp.sum(row_weights * (log_total - target_logit)), 0.0)
    grad_logits = (
        (jnp.exp(logits - log_total[:, None]) - target_hit.astype(jnp.float32))
        * row_weights[:, None]
    ).astype(jnp.bfloat16)
    grad_table = matmul_first(grad_logits, final_pick)
    grad_pick = matmul(grad_logits, table_full)
    grad_final = token_sums(
        jnp.zeros((group_tokens, grad_pick.shape[1]), jnp.float32).at[pick_rows].add(grad_pick)
    )
    grad_two, gain_two = norm_back(hidden_two, norm_gains[2], grad_final)
    grad_two_all = token_rows(grad_two.astype(jnp.bfloat16))
    grad_down = matmul_first(grad_two_all, inner_act)
    grad_inner = matmul(grad_two_all, mlp_full[2])
    unused, pull_swiglu = jax.vjp(swiglu, gate_part, upward)
    grad_gate, grad_up = pull_swiglu(grad_inner)
    grad_gate = grad_gate.astype(jnp.bfloat16)
    grad_up = grad_up.astype(jnp.bfloat16)
    gate_weight_gradient = matmul_first(middle_all, grad_gate)
    grad_up_w = matmul_first(middle_all, grad_up)
    grad_middle = token_sums(
        matmul_last(grad_gate, mlp_full[0]) + matmul_last(grad_up, mlp_full[1])
    )
    grad_middle_in, gain_one = norm_back(hidden_one, norm_gains[1], grad_middle)
    grad_one = grad_two + grad_middle_in
    grad_one_all = token_rows(grad_one.astype(jnp.bfloat16))
    grad_out = matmul_first(grad_one_all, attended_all)
    mlp_grads = jnp.stack([gate_weight_gradient, grad_up_w, grad_down])
    grad_attended = to_heads(matmul(grad_one_all, out_full).astype(jnp.bfloat16)).reshape(
        device_tokens, KV_HEADS, group_size, HEAD
    )
    probs_back = attention_probs()
    grad_probs = jnp.einsum(
        "qhgd,khd->hgqk", grad_attended, attn_values, preferred_element_type=jnp.float32
    )
    inner_sum = jnp.sum(probs_back * grad_probs, axis=-1, keepdims=True)
    grad_scores = (probs_back * (grad_probs - inner_sum)).astype(jnp.bfloat16)
    grad_queries = (
        jnp.einsum("hgqk,khd->qhgd", grad_scores, attn_keys, preferred_element_type=jnp.float32)
        * scaling
    )
    grad_keys = (
        jnp.einsum("hgqk,qhgd->khd", grad_scores, queries, preferred_element_type=jnp.float32)
        * scaling
    )
    grad_values = jnp.einsum(
        "hgqk,qhgd->khd",
        probs_back.astype(jnp.bfloat16),
        grad_attended,
        preferred_element_type=jnp.float32,
    )
    grad_pairs = jnp.concatenate(
        [grad_keys.reshape(LEN, kv_width), grad_values.reshape(LEN, kv_width)], axis=1
    )
    grad_pairs = token_sums(grad_pairs)
    unused, pull_query = jax.vjp(rotate_here, queries_raw)
    grad_query_raw = pull_query(grad_queries.reshape(device_tokens, Q_HEADS, HEAD))[0]
    unused, pull_key = jax.vjp(rotate_here, keys_raw)
    grad_key_raw = pull_key(grad_pairs[:, :kv_width].reshape(device_tokens, KV_HEADS, HEAD))[0]
    grad_project = jnp.concatenate(
        [
            grad_query_raw.reshape(device_tokens, query_width),
            grad_key_raw.reshape(device_tokens, kv_width),
            grad_pairs[:, kv_width:],
        ],
        axis=1,
    ).astype(jnp.bfloat16)
    grad_project_all = from_heads(grad_project)
    grad_qkv = matmul_first(normed_all, grad_project_all)
    grad_normed = token_sums(matmul_last(grad_project_all, qkv_full))
    grad_embed_in, gain_zero = norm_back(embedded, norm_gains[0], grad_normed)
    grad_embedded_all = token_rows((grad_one + grad_embed_in).astype(jnp.bfloat16))
    grad_table = grad_table + jax.ops.segment_sum(
        jnp.where(inside[:, None], grad_embedded_all.astype(jnp.float32), 0.0),
        safe_ids,
        num_segments=vocab_shard,
    )
    gain_grads, loss_value = lax.psum(
        (jnp.stack([gain_zero, gain_one, gain_two]), loss_part), ("row", "col")
    )
    table_summed, qkv_summed, out_summed, mlp_summed = (
        lax.psum_scatter(
            grad_table.astype(jnp.bfloat16), "row", scatter_dimension=1, tiled=True
        ).astype(jnp.float32),
        lax.psum_scatter(
            grad_qkv.astype(jnp.bfloat16), "row", scatter_dimension=0, tiled=True
        ).astype(jnp.float32),
        lax.psum_scatter(
            grad_out.astype(jnp.bfloat16), "row", scatter_dimension=0, tiled=True
        ).astype(jnp.float32),
        lax.psum_scatter(
            mlp_grads.astype(jnp.bfloat16), "row", scatter_dimension=1, tiled=True
        ).astype(jnp.float32),
    )
    left_qkv = exact_first(left_bases[0], qkv_summed)
    left_out = exact_first(left_bases[1], out_summed)
    left_feedforward = jnp.einsum(
        "jcg,jck->jgk",
        left_bases[2:],
        mlp_summed,
        precision=FULL_PRECISION,
        preferred_element_type=jnp.float32,
    )
    left_qkv, left_out, left_feedforward = (
        lax.psum_scatter(
            left_qkv.astype(jnp.bfloat16), "row", scatter_dimension=0, tiled=True
        ).astype(jnp.float32),
        lax.psum_scatter(
            left_out.astype(jnp.bfloat16), "row", scatter_dimension=0, tiled=True
        ).astype(jnp.float32),
        lax.psum_scatter(
            left_feedforward.astype(jnp.bfloat16), "row", scatter_dimension=1, tiled=True
        ).astype(jnp.float32),
    )
    right_qkv = exact_dot(left_qkv, qkv_bases)
    right_out = exact_dot(left_out, out_bases)
    right_mlp = jnp.einsum(
        "evd,edo->evo",
        left_feedforward,
        feedforward_bases,
        precision=FULL_PRECISION,
        preferred_element_type=jnp.float32,
    )
    rotated_qkv, rotated_out, rotated_mlp = (
        lax.psum_scatter(
            right_qkv.astype(jnp.bfloat16), "col", scatter_dimension=1, tiled=True
        ).astype(jnp.float32),
        lax.psum_scatter(
            right_out.astype(jnp.bfloat16), "col", scatter_dimension=1, tiled=True
        ).astype(jnp.float32),
        lax.psum_scatter(
            right_mlp.astype(jnp.bfloat16), "col", scatter_dimension=2, tiled=True
        ).astype(jnp.float32),
    )
    qkv_moment, qkv_scale, qkv_step = moments(rotated_qkv, qkv_mean, qkv_square)
    out_moment, out_scale, out_step = moments(rotated_out, out_mean, out_square)
    mlp_moment, mlp_scale, mlp_step = moments(rotated_mlp, mlp_mean, mlp_square)
    whole_qkv, whole_out, complete_feedforward = (
        lax.all_gather(qkv_step.astype(jnp.bfloat16), "col", axis=1, tiled=True).astype(
            qkv_step.dtype
        ),
        lax.all_gather(out_step.astype(jnp.bfloat16), "col", axis=1, tiled=True).astype(
            out_step.dtype
        ),
        lax.all_gather(mlp_step.astype(jnp.bfloat16), "col", axis=2, tiled=True).astype(
            mlp_step.dtype
        ),
    )
    back_qkv = exact_last(whole_qkv, qkv_bases)
    back_out = exact_last(whole_out, out_bases)
    back_mlp = jnp.einsum(
        "hlb,hab->hla",
        complete_feedforward,
        feedforward_bases,
        precision=FULL_PRECISION,
        preferred_element_type=jnp.float32,
    )
    back_qkv, back_out, back_mlp = (
        lax.all_gather(back_qkv.astype(jnp.bfloat16), "row", axis=0, tiled=True).astype(
            back_qkv.dtype
        ),
        lax.all_gather(back_out.astype(jnp.bfloat16), "row", axis=0, tiled=True).astype(
            back_out.dtype
        ),
        lax.all_gather(back_mlp.astype(jnp.bfloat16), "row", axis=1, tiled=True).astype(
            back_mlp.dtype
        ),
    )
    update_qkv = exact_dot(left_bases[0], back_qkv)
    update_out = exact_dot(left_bases[1], back_out)
    update_mlp = jnp.einsum(
        "avk,akn->avn",
        left_bases[2:],
        back_mlp,
        precision=FULL_PRECISION,
        preferred_element_type=jnp.float32,
    )
    qkv_next = qkv_weight + -(SOAP_RATE * (update_qkv + WEIGHT_DECAY * qkv_weight))
    out_update = -(SOAP_RATE * (update_out + WEIGHT_DECAY * output_weight))
    mlp_next = mlp_weight + -(SOAP_RATE * (update_mlp + WEIGHT_DECAY * mlp_weight))
    embed_change, embed_moment, embed_scale = adam_update(
        embed_table, table_summed, embed_mean, embed_square, WEIGHT_DECAY
    )
    embed_next = embed_table + embed_change
    gain_update, gain_moment, gain_scale = adam_update(
        norm_gains, gain_grads, gain_mean, gain_square, 0.0
    )
    return (
        loss_value,
        embed_next,
        embed_moment,
        embed_scale,
        gain_update,
        gain_moment,
        gain_scale,
        qkv_next,
        qkv_moment,
        qkv_scale,
        out_update,
        out_moment,
        out_scale,
        mlp_next,
        mlp_moment,
        mlp_scale,
    )


def solution(mesh):
    placed = (
        P("row"),
        P("row"),
        P("row"),
        P(),
        P(),
        P("col", "row"),
        P(),
        P("row", "col"),
        P("row", "col"),
        P(None, "row", "col"),
        P("col", "row"),
        P("col", "row"),
        P(),
        P(),
        P("row", "col"),
        P("row", "col"),
        P("row", "col"),
        P("row", "col"),
        P(None, "row", "col"),
        P(None, "row", "col"),
        P(None, "row", None),
        P("col", None),
        P("col", None),
        P(None, "col", None),
    )
    return jax.shard_map(
        per_device,
        mesh=mesh,
        in_specs=placed,
        out_specs=(
            P(),
            P("col", "row"),
            P("col", "row"),
            P("col", "row"),
            P(),
            P(),
            P(),
            P("row", "col"),
            P("row", "col"),
            P("row", "col"),
            P("row", "col"),
            P("row", "col"),
            P("row", "col"),
            P(None, "row", "col"),
            P(None, "row", "col"),
            P(None, "row", "col"),
        ),
        check_vma=False,
    )
```

profile of v0, /device:TPU:0, one launch (start us, length us, event | category | flops | bytes accessed | tf_op | source)
XLA Modules:
  0.0 1854.6 jit_solution(6588651793408107650)
XLA Ops:
  12.0 99.6 %all-gather.22.cloned.1.call-done = bf16[8000,1152]{0,1:T(8,128)(2,1)} async-done(((bf16[8000,144]{0,1:T(8,128)(2,1)}), bf16[8000,1152]{0,1:T(8,128)(2,1)}) %all-gather.22.cloned.1.call-update) | async-done | bytes 18432016 | tf_op jit(solution)/shard_map/all_gather | solution.py:186
  111.7 23.5 %copy.109 = bf16[8000,1152]{1,0:T(8,128)(2,1)} copy(bf16[8000,1152]{0,1:T(8,128)(2,1)} %all-gather.22.cloned.1.call-done) | data formatting | bytes 36864000 | tf_op jit(solution)/shard_map/all_gather | solution.py:186
  135.2 14.9 gather_fusion
  155.2 46.4 %reduce-scatter.27.cloned.1.call-done = bf16[256,1152]{1,0:T(8,128)(2,1)} async-done(((bf16[1024,1152]{1,0:T(8,128)(2,1)}), bf16[256,1152]{1,0:T(8,128)(2,1)}) %reduce-scatter.27.cloned.1.call-update) | async-done | bytes 589840 | tf_op jit(solution)/shard_map/reduce_scatter | solution.py:107
  205.0 22.7 %all-gather.26.cloned.1.call-done = bf16[1152,480]{1,0:T(8,128)(2,1)} async-done(((bf16[144,480]{1,0:T(8,128)(2,1)}), bf16[1152,480]{1,0:T(8,128)(2,1)}) %all-gather.26.cloned.1.call-update) | async-done | bytes 1105936 | tf_op jit(solution)/shard_map/all_gather | solution.py:187
  227.7 52.5 %all-gather.24.cloned.1.call-done = bf16[1024,1152]{1,0:T(8,128)(2,1)} async-done(((bf16[256,1152]{1,0:T(8,128)(2,1)}), bf16[1024,1152]{1,0:T(8,128)(2,1)}) %all-gather.24.cloned.1.call-update) | async-done | bytes 2359312 | tf_op jit(solution)/shard_map/all_gather | solution.py:103
  289.0 23.7 %all-to-all-done = bf16[4,256,480]{1,2,0:T(8,128)(2,1)S(1)} async-done(((bf16[4,256,480]{1,2,0:T(8,128)(2,1)}), bf16[4,256,480]{1,2,0:T(8,128)(2,1)S(1)}, u32[]{:S(2)}, u32[]{:S(2)}) %all-to-all-start) | async-done | bytes 983072 | tf_op jit(solution)/shard_map/all_to_all | solution.py:113
  316.3 34.2 %all-gather.28.cloned.1.call-done = bf16[1024,768]{0,1:T(8,128)(2,1)} async-done(((bf16[256,768]{0,1:T(8,128)(2,1)}), bf16[1024,768]{0,1:T(8,128)(2,1)}) %all-gather.28.cloned.1.call-update) | async-done | bytes 1572880 | tf_op jit(solution)/shard_map/all_gather | solution.py:103
  352.1 11.0 fusion.141
  363.1 9.0 fusion.71
  375.7 11.7 all_gather.73
  397.0 47.3 %reduce-scatter.29.cloned.1.call-done = bf16[256,1152]{1,0:T(8,128)(2,1)} async-done(((bf16[1024,1152]{1,0:T(8,128)(2,1)}), bf16[256,1152]{1,0:T(8,128)(2,1)}) %reduce-scatter.29.cloned.1.call-update) | async-done | bytes 589840 | tf_op jit(solution)/shard_map/reduce_scatter | solution.py:107
  448.0 39.7 %all-gather.32.cloned.1.call-done = bf16[3,1152,768]{2,1,0:T(8,128)(2,1)} async-done(((bf16[3,144,768]{2,1,0:T(8,128)(2,1)}), bf16[3,1152,768]{2,1,0:T(8,128)(2,1)}) %all-gather.32.cloned.1.call-update) | async-done | bytes 5308432 | tf_op jit(solution)/shard_map/all_gather | solution.py:189
  487.8 52.7 %all-gather.30.cloned.1.call-done = bf16[1024,1152]{1,0:T(8,128)(2,1)} async-done(((bf16[256,1152]{1,0:T(8,128)(2,1)}), bf16[1024,1152]{1,0:T(8,128)(2,1)}) %all-gather.30.cloned.1.call-update) | async-done | bytes 2359312 | tf_op jit(solution)/shard_map/all_gather | solution.py:103
  540.4 4.5 fusion.44
  554.0 46.9 %reduce-scatter.31.cloned.1.call-done = bf16[256,1152]{1,0:T(8,128)(2,1)} async-done(((bf16[1024,1152]{1,0:T(8,128)(2,1)}), bf16[256,1152]{1,0:T(8,128)(2,1)}) %reduce-scatter.31.cloned.1.call-update) | async-done | bytes 589840 | tf_op jit(solution)/shard_map/reduce_scatter | solution.py:107
  605.9 48.7 %all-gather.34.cloned.1.call-done = bf16[1024,1152]{1,0:T(8,128)(2,1)} async-done(((bf16[256,1152]{1,0:T(8,128)(2,1)}), bf16[1024,1152]{1,0:T(8,128)(2,1)}) %all-gather.34.cloned.1.call-update) | async-done | bytes 2359312 | tf_op jit(solution)/shard_map/all_gather | solution.py:103
  657.7 11.2 fusion.142
  672.0 8.4 all-gather.4
  680.4 8.6 all-gather.5
  689.1 8.6 all-gather.3
  698.4 12.9 fusion.129
  719.6 46.9 %reduce-scatter.33.cloned.1.call-done = bf16[256,1152]{1,0:T(8,128)(2,1)} async-done(((bf16[1024,1152]{1,0:T(8,128)(2,1)}), bf16[256,1152]{1,0:T(8,128)(2,1)}) %reduce-scatter.33.cloned.1.call-update) | async-done | bytes 589840 | tf_op jit(solution)/shard_map/reduce_scatter | solution.py:107
  770.4 49.8 %all-gather.36.cloned.1.call-done = bf16[1024,1152]{1,0:T(8,128)(2,1)} async-done(((bf16[256,1152]{1,0:T(8,128)(2,1)}), bf16[1024,1152]{1,0:T(8,128)(2,1)}) %all-gather.36.cloned.1.call-update) | async-done | bytes 2359312 | tf_op jit(solution)/shard_map/all_gather | solution.py:103
  820.2 6.9 multiply_convert_fusion.1
  827.2 4.8 fusion.43
  832.1 5.2 add_convert_fusion
  837.3 47.0 %reduce-scatter.35.cloned.1.call-done = bf16[256,1152]{1,0:T(8,128)(2,1)} async-done(((bf16[1024,1152]{1,0:T(8,128)(2,1)}), bf16[256,1152]{1,0:T(8,128)(2,1)}) %reduce-scatter.35.cloned.1.call-update) | async-done | bytes 589840 | tf_op jit(solution)/shard_map/reduce_scatter | solution.py:107
  889.7 50.1 %all-gather.38.cloned.1.call-done = bf16[1024,1152]{1,0:T(8,128)(2,1)} async-done(((bf16[256,1152]{1,0:T(8,128)(2,1)}), bf16[1024,1152]{1,0:T(8,128)(2,1)}) %all-gather.38.cloned.1.call-update) | async-done | bytes 2359312 | tf_op jit(solution)/shard_map/all_gather | solution.py:103
  942.7 19.0 %all_to_all.67 = bf16[4,256,288]{1,2,0:T(8,128)(2,1)S(1)} all-to-all(bf16[4,256,288]{1,2,0:T(8,128)(2,1)S(1)} %bitcast.270), channel_id=1, replica_groups=mesh['row'=8,'col'=4] {'col'}, dimensions={0} | all-to-all | bytes 1179648 | tf_op jit(solution)/shard_map/all_to_all | solution.py:113
  961.7 9.4 bitcast_convert_fusion
  971.1 12.0 fusion.8
  983.1 13.1 fusion.10
  1001.4 4.3 fusion.30
  1013.9 5.4 convolution_multiply_fusion
  1019.6 16.0 reduce-scatter.37.cloned.1.call-done
  1036.9 27.0 %all_to_all.68 = bf16[256,4,480]{0,2,1:T(8,128)(2,1)S(1)} all-to-all(bf16[256,4,480]{0,2,1:T(8,128)(2,1)S(1)} %bitcast.262), channel_id=1, replica_groups=mesh['row'=8,'col'=4] {'col'}, dimensions={1} | all-to-all | bytes 1966080 | tf_op jit(solution)/shard_map/all_to_all | solution.py:117
  1067.7 27.1 %reduce-scatter.45.cloned.1.call-done = bf16[3,144,768]{2,1,0:T(8,128)(2,1)} async-done(((bf16[3,1152,768]{2,1,0:T(8,128)(2,1)}), bf16[3,144,768]{2,1,0:T(8,128)(2,1)}) %reduce-scatter.45.cloned.1.call-update) | async-done | bytes 663568 | tf_op jit(solution)/shard_map/reduce_scatter | solution.py:362
  1094.8 9.0 fusion.23
  1103.9 12.5 copy.121
  1122.8 12.8 reduce-scatter.41.cloned.1.call-done
  1140.1 111.6 %all-reduce.8.cloned.1.call-done = bf16[3,1152,768]{2,0,1:T(4,128)(2,1)} async-done(((bf16[3,1152,768]{2,0,1:T(4,128)(2,1)}), bf16[3,1152,768]{2,0,1:T(4,128)(2,1)}) %all-reduce.8.cloned.1.call-update) | async-done | bytes 5308432
  1253.2 16.9 convolution_convert_fusion.1
  1275.7 14.5 reduce-scatter.43.cloned.1.call-done
  1293.4 37.5 %reduce-scatter.51.cloned.1.call-done = bf16[144,480]{1,0:T(8,128)(2,1)} async-done(((bf16[1152,480]{1,0:T(8,128)(2,1)}), bf16[144,480]{1,0:T(8,128)(2,1)}) %reduce-scatter.51.cloned.1.call-update) | async-done | bytes 138256
  1336.1 50.4 %reduce-scatter.47.cloned.1.call-done = bf16[3,144,768]{2,1,0:T(8,128)(2,1)} async-done(((bf16[3,144,3072]{2,1,0:T(8,128)(2,1)}), bf16[3,144,768]{2,1,0:T(8,128)(2,1)}) %reduce-scatter.47.cloned.1.call-update) | async-done | bytes 663568 | tf_op jit(solution)/shard_map/reduce_scatter | solution.py:402
  1390.7 46.4 %reduce-scatter.39.cloned.1.call-done = bf16[256,1152]{1,0:T(8,128)(2,1)} async-done(((bf16[1024,1152]{1,0:T(8,128)(2,1)}), bf16[256,1152]{1,0:T(8,128)(2,1)}) %reduce-scatter.39.cloned.1.call-update) | async-done | bytes 589840 | tf_op jit(solution)/shard_map/reduce_scatter | solution.py:107
  1441.1 33.9 %reduce-scatter.55.cloned.1.call-done = bf16[144,288]{1,0:T(8,128)(2,1)} async-done(((bf16[1152,288]{1,0:T(8,128)(2,1)}), bf16[144,288]{1,0:T(8,128)(2,1)}) %reduce-scatter.55.cloned.1.call-update) | async-done | bytes 82960
  1477.9 25.6 %reduce-scatter.53.cloned.1.call-done = bf16[480,144]{1,0:T(8,128)(2,1)} async-done(((bf16[1920,144]{1,0:T(8,128)(2,1)}), bf16[480,144]{1,0:T(8,128)(2,1)}) %reduce-scatter.53.cloned.1.call-update) | async-done | bytes 138256
  1505.5 19.9 %all-gather.6 = bf16[4,480,144]{1,2,0:T(8,128)(2,1)S(1)} all-gather(bf16[1,480,144]{1,2,0:T(8,128)(2,1)S(1)} %get-tuple-element.296), channel_id=1, replica_groups=mesh['row'=8,'col'=4] {'col'}, dimensions={0}, use_global_device_ids=true | all-gather | bytes 691200 | tf_op jit(solution)/shard_map/all_gather | solution.py:410
  1526.6 4.8 convolution_convert_fusion.17
  1531.4 31.3 %all-gather.44.cloned.1.call-done = bf16[3,144,3072]{2,1,0:T(8,128)(2,1)} async-done(((bf16[3,144,768]{2,1,0:T(8,128)(2,1)}), bf16[3,144,3072]{2,1,0:T(8,128)(2,1)}) %all-gather.44.cloned.1.call-update) | async-done | bytes 2654224 | tf_op jit(solution)/shard_map/all_gather | solution.py:416
  1562.7 19.9 %convolution_convert_fusion.15 = bf16[3,144,768]{2,1,0:T(8,128)(2,1)} fusion(bf16[3,144,3072]{2,1,0:T(8,128)(2,1)} %all-gather.44.cloned.1.call-done, f32[3,768,3072]{2,1,0:T(8,128)} %param.49), kind=kOutput, calls=%fused_computation.121 | convolution fusion | flops 12230922240 | bytes 31629312 | tf_op jit(solution)/shard_map/hlb,hab->hla/dot_general | solution.py:422
  1582.9 16.1 fusion.107
  1599.0 15.2 all-gather.40.cloned.1.call-done
  1614.2 35.1 %scatter_custom_fusion.1 = f32[8000,1152]{1,0:T(8,128)} fusion(f32[8000,1152]{1,0:T(8,128)} %fusion.107, s32[1024]{0:T(1024)} %copy-done.46, bf16[1024,1152]{1,0:T(8,128)(2,1)} %all-gather.40.cloned.1.call-done, f32[]{:T(128)} %constant.169.clone.1, pred[1024]{0:T(1024)(128)(4,1)S(1)} %copy-done.56), kind=kCustom, calls=%fused_computation.32 | custom fusion | flops 3538944 | bytes 39224832 | tf_op jit(solution)/shard_map/scatter-add | solution.py:344
  1649.3 20.1 %convert_element_type.263 = bf16[8000,1152]{1,0:T(8,128)(2,1)} convert(f32[8000,1152]{1,0:T(8,128)} %scatter_custom_fusion.1) | non-fusion elementwise | flops 9216000 | bytes 55296000 | tf_op jit(solution)/shard_map/convert_element_type | solution.py:354
  1669.4 24.0 %copy.131 = bf16[8000,1152]{0,1:T(8,128)(2,1)} copy(bf16[8000,1152]{1,0:T(8,128)(2,1)} %convert_element_type.263) | data formatting | bytes 36864000
  1696.2 14.7 all-gather.7
  1712.4 12.1 all_gather.89
  1727.4 38.3 %all-reduce.5 = (f32[]{:T(128)}, f32[3,1152]{1,0:T(4,128)S(1)}) all-reduce(f32[]{:T(128)S(6)} %select_n.92, f32[3,1152]{1,0:T(4,128)S(1)} %pad_maximum_fusion.13), channel_id=1, replica_groups=mesh['row'=8,'col'=4] {'row','col'}, use_global_device_ids=true, to_apply=%region_16.17 | all-reduce | flops 3457 | bytes 27656 | tf_op jit(solution)/shard_map/psum | solution.py:349
  1769.2 7.0 fusion.67
  1776.3 59.7 %reduce-scatter.49.cloned.1.call-done = bf16[144,8000]{1,0:T(8,128)(2,1)} async-done(((bf16[1152,8000]{1,0:T(8,128)(2,1)}), bf16[144,8000]{1,0:T(8,128)(2,1)}) %reduce-scatter.49.cloned.1.call-update) | async-done | bytes 2304016
  1836.0 11.6 negate_add_fusion
  (325 shorter events, 153.0 us)
Async XLA Ops:
  7.2 1467.8 %copy-start = (f32[288,1152]{1,0:T(8,128)S(1)}, f32[288,1152]{1,0:T(8,128)}, u32[]{:S(2)}) copy-start(f32[288,1152]{1,0:T(8,128)} %param.48) | copy-start | bytes 3981316
  7.2 104.5 %all-gather.22.cloned.1.call-start = ((), (), s32[]{:S(2)}) async-start(), calls=%async_computation.20 | async-start | bytes 20901888 | tf_op jit(solution)/shard_map/all_gather | solution.py:186
  11.3 190.3 %reduce-scatter.27.cloned.1.call-start = ((), (), s32[]{:S(2)}) async-start(), calls=%async_computation.21 | async-start | bytes 2949120 | tf_op jit(solution)/shard_map/reduce_scatter | solution.py:107
  11.4 138.7 %copy-start.55 = (pred[1024]{0:T(1024)(128)(4,1)}, pred[1024]{0:T(1024)(128)(4,1)S(1)}, u32[]{:S(2)}) copy-start(pred[1024]{0:T(1024)(128)(4,1)S(1)} %get-tuple-element.331) | copy-start | bytes 3076
  153.4 74.3 %all-gather.26.cloned.1.call-start = ((), (), s32[]{:S(2)}) async-start(), calls=%async_computation.23 | async-start | bytes 1327104 | tf_op jit(solution)/shard_map/all_gather | solution.py:187
  155.0 125.1 %all-gather.24.cloned.1.call-start = ((), (), s32[]{:S(2)}) async-start(), calls=%async_computation.22 | async-start | bytes 2949120 | tf_op jit(solution)/shard_map/all_gather | solution.py:103
  155.1 128.5 %copy-start.36 = (f32[1152]{0:T(1024)}, f32[1152]{0:T(1024)S(1)}, u32[]{:S(2)}) copy-start(f32[1152]{0:T(1024)S(1)} %get-tuple-element.270) | copy-start | bytes 13828
  202.8 80.8 %copy-start.53 = (f32[256]{0:T(256)}, f32[256]{0:T(256)S(1)}, u32[]{:S(2)}) copy-start(f32[256]{0:T(256)S(1)} %fusion.83) | copy-start | bytes 3076
  202.9 80.8 %copy-start.44 = (f32[256]{0:T(256)}, f32[256]{0:T(256)S(1)}, u32[]{:S(2)}) copy-start(f32[256]{0:T(256)S(1)} %fusion.113) | copy-start | bytes 3076
  284.7 28.0 %all-to-all-start = ((bf16[4,256,480]{1,2,0:T(8,128)(2,1)}), bf16[4,256,480]{1,2,0:T(8,128)(2,1)S(1)}, u32[]{:S(2)}, u32[]{:S(2)}) async-start(bf16[4,256,480]{1,2,0:T(8,128)(2,1)} %bitcast.252), calls=%async_computation.1 | async-start | bytes 1966080 | tf_op jit(solution)/shard_map/all_to_all | solution.py:113
  288.2 62.4 %all-gather.28.cloned.1.call-start = ((), (), s32[]{:S(2)}) async-start(), calls=%async_computation.24 | async-start | bytes 1966080 | tf_op jit(solution)/shard_map/all_gather | solution.py:103
  316.3 46.8 %copy-start.14 = (bf16[256,18,32]{0,2,1:T(8,128)(2,1)}, bf16[256,18,32]{0,2,1:T(8,128)(2,1)S(1)}, u32[]{:S(2)}) copy-start(bf16[256,18,32]{0,2,1:T(8,128)(2,1)S(1)} %get-tuple-element.321) | copy-start | bytes 884740
  316.3 46.8 %copy-start.16 = (bf16[256,18,32]{0,2,1:T(8,128)(2,1)}, bf16[256,18,32]{0,2,1:T(8,128)(2,1)S(1)}, u32[]{:S(2)}) copy-start(bf16[256,18,32]{0,2,1:T(8,128)(2,1)S(1)} %get-tuple-element.322) | copy-start | bytes 884740
  372.1 18.7 %all-to-all-start.1 = ((bf16[256,4,288]{0,2,1:T(8,128)(2,1)}), bf16[256,4,288]{0,2,1:T(8,128)(2,1)S(1)}, u32[]{:S(2)}, u32[]{:S(2)}) async-start(bf16[256,4,288]{0,2,1:T(8,128)(2,1)} %bitcast.287), calls=%async_computation.2 | async-start | bytes 1179648 | tf_op jit(solution)/shard_map/all_to_all | solution.py:117
  375.6 68.7 %reduce-scatter.29.cloned.1.call-start = ((), (), s32[]{:S(2)}) async-start(), calls=%async_computation.25 | async-start | bytes 2949120 | tf_op jit(solution)/shard_map/reduce_scatter | solution.py:107
  396.0 48.4 %copy-start.2 = (bf16[256,1152]{1,0:T(8,128)(2,1)S(1)}, bf16[256,1152]{1,0:T(8,128)(2,1)}, u32[]{:S(2)}) copy-start(bf16[256,1152]{1,0:T(8,128)(2,1)} %reduce-scatter.27.cloned.1.call-done) | copy-start | bytes 1769476
  396.0 91.8 %all-gather.32.cloned.1.call-start = ((), (), s32[]{:S(2)}) async-start(), calls=%async_computation.27 | async-start | bytes 5971968 | tf_op jit(solution)/shard_map/all_gather | solution.py:189
  397.0 143.5 %all-gather.30.cloned.1.call-start = ((), (), s32[]{:S(2)}) async-start(), calls=%async_computation.26 | async-start | bytes 2949120 | tf_op jit(solution)/shard_map/all_gather | solution.py:103
  447.8 153.1 %reduce-scatter.31.cloned.1.call-start = ((), (), s32[]{:S(2)}) async-start(), calls=%async_computation.28 | async-start | bytes 2949120 | tf_op jit(solution)/shard_map/reduce_scatter | solution.py:107
  553.8 47.0 %copy-start.4 = (bf16[256,1152]{1,0:T(8,128)(2,1)S(1)}, bf16[256,1152]{1,0:T(8,128)(2,1)}, u32[]{:S(2)}) copy-start(bf16[256,1152]{1,0:T(8,128)(2,1)} %reduce-scatter.29.cloned.1.call-done) | copy-start | bytes 1769476
  553.9 50.7 %copy-start.57 = (s32[1024]{0:T(1024)S(1)}, s32[1024]{0:T(1024)}, u32[]{:S(2)}) copy-start(s32[1024]{0:T(1024)} %param.29) | copy-start | bytes 12292
  553.9 52.0 %copy-start.66 = (s32[128]{0:T(128)S(1)}, s32[128]{0:T(128)}, u32[]{:S(2)}) copy-start(s32[128]{0:T(128)} %param.28) | copy-start | bytes 1540
  553.9 52.0 %copy-start.67 = (s32[128]{0:T(128)S(1)}, s32[128]{0:T(128)}, u32[]{:S(2)}) copy-start(s32[128]{0:T(128)} %param.27) | copy-start | bytes 1540
  553.9 100.7 %all-gather.34.cloned.1.call-start = ((), (), s32[]{:S(2)}) async-start(), calls=%async_computation.29 | async-start | bytes 2949120 | tf_op jit(solution)/shard_map/all_gather | solution.py:103
  604.5 162.0 %reduce-scatter.33.cloned.1.call-start = ((), (), s32[]{:S(2)}) async-start(), calls=%async_computation.30 | async-start | bytes 2949120 | tf_op jit(solution)/shard_map/reduce_scatter | solution.py:107
  605.9 63.1 %copy-start.58 = (pred[128]{0:T(512)(128)(4,1)}, pred[128]{0:T(512)(128)(4,1)S(1)}, u32[]{:S(2)}) copy-start(pred[128]{0:T(512)(128)(4,1)S(1)} %get-tuple-element.310) | copy-start | bytes 388
  605.9 92.5 %copy-start.47 = (s32[128]{0:T(128)}, s32[128]{0:T(128)S(1)}, u32[]{:S(2)}) copy-start(s32[128]{0:T(128)S(1)} %broadcast_subtract_fusion) | copy-start | bytes 1540
  719.6 47.0 %copy-start.5 = (bf16[256,1152]{1,0:T(8,128)(2,1)S(1)}, bf16[256,1152]{1,0:T(8,128)(2,1)}, u32[]{:S(2)}) copy-start(bf16[256,1152]{1,0:T(8,128)(2,1)} %reduce-scatter.31.cloned.1.call-done) | copy-start | bytes 1769476
  719.6 100.7 %all-gather.36.cloned.1.call-start = ((), (), s32[]{:S(2)}) async-start(), calls=%async_computation.31 | async-start | bytes 2949120 | tf_op jit(solution)/shard_map/all_gather | solution.py:103
  770.1 114.2 %reduce-scatter.35.cloned.1.call-start = ((), (), s32[]{:S(2)}) async-start(), calls=%async_computation.32 | async-start | bytes 2949120 | tf_op jit(solution)/shard_map/reduce_scatter | solution.py:107
  837.3 102.5 %all-gather.38.cloned.1.call-start = ((), (), s32[]{:S(2)}) async-start(), calls=%async_computation.33 | async-start | bytes 2949120 | tf_op jit(solution)/shard_map/all_gather | solution.py:103
  889.7 146.0 %reduce-scatter.37.cloned.1.call-start = ((), (), s32[]{:S(2)}) async-start(), calls=%async_computation.34 | async-start | bytes 1966080 | tf_op jit(solution)/shard_map/reduce_scatter | solution.py:107
  1001.2 93.7 %reduce-scatter.45.cloned.1.call-start = ((), (), s32[]{:S(2)}) async-start(), calls=%async_computation.40 | async-start | bytes 5971968 | tf_op jit(solution)/shard_map/reduce_scatter | solution.py:362
  1012.8 122.8 %reduce-scatter.41.cloned.1.call-start = ((), (), s32[]{:S(2)}) async-start(), calls=%async_computation.37 | async-start | bytes 1327104 | tf_op jit(solution)/shard_map/reduce_scatter | solution.py:356
  1067.4 184.3 %all-reduce.8.cloned.1.call-start = ((), (), s32[]{:S(2)}) async-start(), calls=%async_computation.49 | async-start | bytes 14155776
  1116.4 173.8 %reduce-scatter.43.cloned.1.call-start = ((), (), s32[]{:S(2)}) async-start(), calls=%async_computation.39 | async-start | bytes 995328 | tf_op jit(solution)/shard_map/reduce_scatter | solution.py:359
  1121.5 209.5 %reduce-scatter.51.cloned.1.call-start = ((), (), s32[]{:S(2)}) async-start(), calls=%async_computation.45 | async-start | bytes 1327104
  1139.6 246.9 %reduce-scatter.47.cloned.1.call-start = ((), (), s32[]{:S(2)}) async-start(), calls=%async_computation.41 | async-start | bytes 3317760 | tf_op jit(solution)/shard_map/reduce_scatter | solution.py:402
  1270.1 167.0 %reduce-scatter.39.cloned.1.call-start = ((), (), s32[]{:S(2)}) async-start(), calls=%async_computation.35 | async-start | bytes 2949120 | tf_op jit(solution)/shard_map/reduce_scatter | solution.py:107
  1275.6 199.4 %reduce-scatter.55.cloned.1.call-start = ((), (), s32[]{:S(2)}) async-start(), calls=%async_computation.47 | async-start | bytes 995328
  1293.4 210.0 %reduce-scatter.53.cloned.1.call-start = ((), (), s32[]{:S(2)}) async-start(), calls=%async_computation.46 | async-start | bytes 1228800
  1336.0 101.1 %copy-start.37 = (f32[1152]{0:T(1024)S(1)}, f32[1152]{0:T(1024)}, u32[]{:S(2)}) copy-start(f32[1152]{0:T(1024)} %copy-done.36) | copy-start | bytes 13828
  1336.0 101.1 %copy-start.45 = (f32[256]{0:T(256)S(1)}, f32[256]{0:T(256)}, u32[]{:S(2)}) copy-start(f32[256]{0:T(256)} %copy-done.44) | copy-start | bytes 3076
  1336.0 102.7 %copy-start.54 = (f32[256]{0:T(256)S(1)}, f32[256]{0:T(256)}, u32[]{:S(2)}) copy-start(f32[256]{0:T(256)} %copy-done.53) | copy-start | bytes 3076
  1336.0 226.7 %all-gather.44.cloned.1.call-start = ((), (), s32[]{:S(2)}) async-start(), calls=%async_computation.42 | async-start | bytes 3317760 | tf_op jit(solution)/shard_map/all_gather | solution.py:416
  1390.5 48.3 %copy-start.9 = (f32[256,1152]{1,0:T(8,128)S(1)}, f32[256,1152]{1,0:T(8,128)}, u32[]{:S(2)}) copy-start(f32[256,1152]{1,0:T(8,128)} %get-tuple-element.306) | copy-start | bytes 3538948
  1390.5 223.8 %all-gather.40.cloned.1.call-start = ((), (), s32[]{:S(2)}) async-start(), calls=%async_computation.36 | async-start | bytes 2949120 | tf_op jit(solution)/shard_map/all_gather | solution.py:103
  1441.0 63.5 %copy-start.32 = (f32[144,480]{1,0:T(8,128)S(1)}, f32[144,480]{1,0:T(8,128)}, u32[]{:S(2)}) copy-start(f32[144,480]{1,0:T(8,128)} %param.41) | copy-start | bytes 829444
  1441.0 63.5 %copy-start.33 = (f32[144,480]{1,0:T(8,128)S(1)}, f32[144,480]{1,0:T(8,128)}, u32[]{:S(2)}) copy-start(f32[144,480]{1,0:T(8,128)} %param.40) | copy-start | bytes 829444
  1441.0 253.2 %reduce-scatter.57.cloned.1.call-start = ((), (), s32[]{:S(2)}) async-start(), calls=%async_computation.48 | async-start | bytes 737280
  1477.8 288.5 %all-gather.42.cloned.1.call-start = ((), (), s32[]{:S(2)}) async-start(), calls=%async_computation.38 | async-start | bytes 1327104 | tf_op jit(solution)/shard_map/all_gather | solution.py:430
  1531.3 51.5 %copy-start.11 = (bf16[128,1152]{1,0:T(8,128)(2,1)S(1)}, bf16[128,1152]{1,0:T(8,128)(2,1)}, u32[]{:S(2)}) copy-start(bf16[128,1152]{1,0:T(8,128)(2,1)} %copy-done.10) | copy-start | bytes 884740
  1531.4 51.5 %copy-start.48 = (s32[128]{0:T(128)S(1)}, s32[128]{0:T(128)}, u32[]{:S(2)}) copy-start(s32[128]{0:T(128)} %copy-done.47) | copy-start | bytes 1540
  1531.4 51.5 %copy-start.50 = (f32[128]{0:T(128)S(1)}, f32[128]{0:T(128)}, u32[]{:S(2)}) copy-start(f32[128]{0:T(128)} %copy-done.49) | copy-start | bytes 1540
  1531.4 51.5 %copy-start.52 = (f32[128]{0:T(128)S(1)}, f32[128]{0:T(128)}, u32[]{:S(2)}) copy-start(f32[128]{0:T(128)} %copy-done.51) | copy-start | bytes 1540
  1531.4 51.5 %copy-start.59 = (pred[128]{0:T(512)(128)(4,1)S(1)}, pred[128]{0:T(512)(128)(4,1)}, u32[]{:S(2)}) copy-start(pred[128]{0:T(512)(128)(4,1)} %copy-done.58) | copy-start | bytes 388
  1531.4 237.8 %all-gather.46.cloned.1.call-start = ((), (), s32[]{:S(2)}) async-start(), calls=%async_computation.43 | async-start | bytes 5971968 | tf_op jit(solution)/shard_map/all_gather | solution.py:436
  1582.6 31.6 %copy-start.56 = (pred[1024]{0:T(1024)(128)(4,1)S(1)}, pred[1024]{0:T(1024)(128)(4,1)}, u32[]{:S(2)}) copy-start(pred[1024]{0:T(1024)(128)(4,1)} %copy-done.55) | copy-start | bytes 3076
  1582.6 253.3 %reduce-scatter.49.cloned.1.call-start = ((), (), s32[]{:S(2)}) async-start(), calls=%async_computation.44 | async-start | bytes 20901888
  1711.4 54.3 %copy-start.39 = (f32[3,1152]{1,0:T(4,128)S(1)}, f32[3,1152]{1,0:T(4,128)}, u32[]{:S(2)}) copy-start(f32[3,1152]{1,0:T(4,128)} %param.32) | copy-start | bytes 41476
  1711.4 54.3 %copy-start.42 = (f32[3,1152]{1,0:T(4,128)S(1)}, f32[3,1152]{1,0:T(4,128)}, u32[]{:S(2)}) copy-start(f32[3,1152]{1,0:T(4,128)} %param.39) | copy-start | bytes 41476
  1711.4 54.2 %copy-start.43 = (f32[3,1152]{1,0:T(4,128)S(1)}, f32[3,1152]{1,0:T(4,128)}, u32[]{:S(2)}) copy-start(f32[3,1152]{1,0:T(4,128)} %param.38) | copy-start | bytes 41476
  1711.4 54.9 %copy-start.19 = (f32[144,480]{1,0:T(8,128)S(1)}, f32[144,480]{1,0:T(8,128)}, u32[]{:S(2)}) copy-start(f32[144,480]{1,0:T(8,128)} %param.33) | copy-start | bytes 829444
  1724.5 44.7 %copy-start.8 = (f32[3,144,768]{2,1,0:T(8,128)S(1)}, f32[3,144,768]{2,1,0:T(8,128)}, u32[]{:S(2)}) copy-start(f32[3,144,768]{2,1,0:T(8,128)} %param.35) | copy-start | bytes 3981316
  (43 other events, 312.3 us)
Sparse Core Ops, SparseCore 0:
  11.4 100.1 all-gather.21
  153.5 48.0 reduce-scatter.26
  204.1 23.5 all-gather.25
  229.7 50.4 all-gather.23
  313.8 36.7 all-gather.27
  396.1 48.1 reduce-scatter.28
  446.8 40.8 all-gather.31
  489.9 50.4 all-gather.29
  554.0 46.8 reduce-scatter.30
  604.6 49.9 all-gather.33
  719.7 46.7 reduce-scatter.32
  770.2 49.9 all-gather.35
  837.4 46.8 reduce-scatter.34
  889.8 49.9 all-gather.37
  1001.3 34.3 reduce-scatter.36
  1038.9 55.8 reduce-scatter.44
  1098.8 36.7 reduce-scatter.40
  1138.8 112.8 all-reduce.7
  1254.9 35.1 reduce-scatter.42
  1294.1 36.7 reduce-scatter.50
  1333.8 52.5 reduce-scatter.46
  1389.4 47.7 reduce-scatter.38
  1440.4 34.5 reduce-scatter.54
  1477.3 26.1 reduce-scatter.52
  1505.6 57.0 all-gather.43
  1564.7 49.4 all-gather.39
  1616.4 20.7 reduce-scatter.56
  1639.6 22.4 all-gather.41
  1664.5 41.3 all-gather.45
  1709.6 126.3 reduce-scatter.48
where the time goes:
time: 1860 us; the launch traced here: 1850 us
  waiting for transfers between devices  1190 us (64%)
  matrix products  223 us (12%)
  blocking collectives  168 us (9%)
  other arithmetic  137 us (7%)
  local copies, waits for them, and re-layouts  103 us (6%)
    all_gather x7, waiting for transfers between devices, token_rows(): return lax.all_gather(values, 'col', axis=0, tiled=True)  303 us
    reduce_scatter x7, waiting for transfers between devices, token_sums(): lax.psum_scatter(term.astype(jnp.bfloat16), 'col', scatter_dimension=0, t...  297 us
    unnamed x36, waiting for transfers between devices  269 us
    all_gather x1, waiting for transfers between devices, per_device(): lax.all_gather(embed_table.astype(jnp.bfloat16), 'row', axis=1, tiled=True)  99.6 us
    reduce_scatter x1, waiting for transfers between devices, per_device(): lax.psum_scatter(right_mlp.astype(jnp.bfloat16), 'col', scatter_dimension...  50.4 us
    unnamed x161, local copies, waits for them, and re-layouts  44.9 us
    all_gather x1, waiting for transfers between devices, per_device(): lax.all_gather(mlp_weight.astype(jnp.bfloat16), 'row', axis=1, tiled=True)  39.7 us
    psum x1, blocking collectives, per_device(): lax.psum((jnp.stack([gain_zero, gain_one, gain_two]), loss_part), ('row',...  38.3 us
  transfers between devices with their start and end apart: 32, of which 29 were waited for; matrix products, arithmetic and copies ran while one was open for 13% of the time, Pallas kernels for 0%

commit v1 on v0

v1 whole, which is shorter than its diff:
```python
import jax
import jax.numpy as jnp
from jax import lax
from jax.sharding import PartitionSpec as P

Q_HEADS = 18
KV_HEADS = 6
HEAD = 64
LEN = 1024
PICK = 128


NORM_EPSILON = 1e-05
ADAM_EPSILON = 1e-08
MOMENT_BETA = 0.5
SOAP_RATE = 0.05
ADAM_RATE = 0.01
WEIGHT_DECAY = 0.1
MASK_VALUE = -1e30


def send(value, axis, shift):
    count = lax.axis_size(axis)
    return lax.ppermute(value, axis, [(k, (k + shift) % count) for k in range(count)])


def collect(value, axis):
    return [value] + [send(value, axis, k) for k in range(1, lax.axis_size(axis))]


def deliver(pieces, axis, sign):
    return [pieces[0]] + [send(pieces[k], axis, sign * k) for k in range(1, len(pieces))]


def summed(pieces):
    total = pieces[0].astype(jnp.float32)
    for piece in pieces[1:]:
        total = total + piece.astype(jnp.float32)
    return total


def to_absolute(pieces, index):
    count = len(pieces)
    order = [pieces[0]] + [pieces[count - k] for k in range(1, count)]
    return jnp.roll(jnp.stack(order), index, axis=0)


def pick_block(values, index, axis):
    return lax.dynamic_index_in_dim(values, index, axis, keepdims=False)


def rms_norm(values, gain_vec):
    return (
        values
        * lax.rsqrt(jnp.mean(values * values, axis=-1, keepdims=True) + NORM_EPSILON)
        * gain_vec
    )


def rotary(values, positions):
    half_width = values.shape[-1] // 2
    frequency = jnp.power(10000.0, -jnp.arange(half_width, dtype=jnp.float32) / half_width)
    angles = positions[:, None].astype(jnp.float32) * frequency[None, :]
    cosine = jnp.cos(angles)[:, None, :]
    sine_part = jnp.sin(angles)[:, None, :]
    first_half = values[..., :half_width]
    second_half = values[..., half_width:]
    return jnp.concatenate(
        [
            first_half * cosine - second_half * sine_part,
            second_half * cosine + first_half * sine_part,
        ],
        axis=-1,
    )


def swiglu(gate_part, upward):
    return jax.nn.silu(gate_part) * upward


def matmul(left_op, right_op):
    return jnp.dot(left_op, right_op, preferred_element_type=jnp.float32)


def matmul_last(left_op, right_op):
    return lax.dot_general(
        left_op, right_op, (((1,), (1,)), ((), ())), preferred_element_type=jnp.float32
    )


def matmul_first(left_op, right_op):
    return lax.dot_general(
        left_op, right_op, (((0,), (0,)), ((), ())), preferred_element_type=jnp.float32
    )


def norm_back(values, gain_vec, grad_output):
    unused, pull_back = jax.vjp(rms_norm, values, gain_vec)
    return pull_back(grad_output)


def moments(rotated, moment, square_avg):
    moment_new = MOMENT_BETA * moment + (1.0 - MOMENT_BETA) * rotated
    square_new = MOMENT_BETA * square_avg + (1.0 - MOMENT_BETA) * rotated * rotated
    return (moment_new, square_new, moment_new / (jnp.sqrt(square_new) + ADAM_EPSILON))


def adam_update(weight, gradient_value, moment, square_avg, decay_rate):
    moment_new = MOMENT_BETA * moment + (1.0 - MOMENT_BETA) * gradient_value
    square_new = MOMENT_BETA * square_avg + (1.0 - MOMENT_BETA) * gradient_value * gradient_value
    change = -(
        ADAM_RATE * (moment_new / (jnp.sqrt(square_new) + ADAM_EPSILON) + decay_rate * weight)
    )
    return (change, moment_new, square_new)


def per_device(
    token_ids,
    target_ids,
    loss_slots,
    valid_mask,
    prefix_lens,
    embed_table,
    norm_gains,
    qkv_weight,
    output_weight,
    mlp_weight,
    embed_mean,
    embed_square,
    gain_mean,
    gain_square,
    qkv_mean,
    qkv_square,
    out_mean,
    out_square,
    mlp_mean,
    mlp_square,
    left_bases,
    qkv_bases,
    out_bases,
    feedforward_bases,
):
    row_index = lax.axis_index("row")
    col_index = lax.axis_index("col")
    row_count = lax.axis_size("row")
    col_count = lax.axis_size("col")
    low = jnp.bfloat16
    group_tokens = token_ids.shape[0]
    pick_count = loss_slots.shape[0]
    device_tokens = group_tokens // col_count
    vocab_shard, features = embed_table.shape
    width = features * row_count
    query_width = Q_HEADS * HEAD
    kv_width = KV_HEADS * HEAD
    group_size = Q_HEADS // KV_HEADS
    scaling = HEAD ** (-0.5)
    qkv_cols, out_cols, ff_cols = qkv_weight.shape[1], output_weight.shape[1], mlp_weight.shape[2]
    vocab_part = vocab_shard // row_count

    ids_all = lax.all_gather(jnp.concatenate([token_ids, target_ids]), "row", axis=0)
    tokens_all = ids_all[:, :group_tokens].reshape(row_count, col_count, device_tokens)
    targets_all = ids_all[:, group_tokens:].reshape(row_count * pick_count)
    local_tokens = tokens_all - col_index * vocab_shard
    vocab_line = jnp.arange(vocab_shard, dtype=jnp.int32)

    table_low_t = embed_table.astype(low).T
    attn_block = jnp.concatenate(
        collect(qkv_weight.astype(low), "col") + collect(output_weight.astype(low), "col"), axis=1
    )
    attn_full = lax.all_gather(attn_block, "row", axis=0, tiled=True)
    mlp_low = mlp_weight.astype(low)
    mlp_block = jnp.concatenate(
        collect(mlp_low[0], "col") + collect(mlp_low[1], "col") + collect(mlp_low[2], "col"), axis=1
    )
    mlp_full = lax.all_gather(mlp_block, "row", axis=0, tiled=True)
    bases_low = left_bases.astype(low)
    left_full = lax.all_gather(
        jnp.concatenate([bases_low[k] for k in range(5)], axis=1), "row", axis=0, tiled=True
    )
    qkv_width, out_width, ff_width = (
        qkv_cols * col_count,
        out_cols * col_count,
        ff_cols * col_count,
    )
    qkv_full, out_full = attn_full[:, :qkv_width], attn_full[:, qkv_width:]
    gate_full, up_full, down_full = (
        mlp_full[:, k * ff_width : (k + 1) * ff_width] for k in range(3)
    )

    def rotate_left(values, k):
        return matmul(values, left_full[:, k * width : (k + 1) * width]).astype(low)

    def absolute_columns(values):
        count = values.shape[1] // col_count
        parts = [values[:, k * count : (k + 1) * count] for k in range(col_count)]
        stacked = to_absolute(parts, col_index)
        return jnp.moveaxis(stacked, 0, 1).reshape(values.shape)

    def relative_columns(values):
        count = values.shape[1] // col_count
        stacked = jnp.moveaxis(values.reshape(values.shape[0], col_count, count), 1, 0)
        turned = jnp.roll(stacked, -col_index, axis=0)
        order = [turned[0]] + [turned[col_count - k] for k in range(1, col_count)]
        return jnp.concatenate(order, axis=1)

    table_parts = jnp.moveaxis(table_low_t.reshape(features, row_count, vocab_part), 1, 0)
    part_pieces = [
        pick_block(table_parts, (row_index + k) % row_count, 0) for k in range(row_count)
    ]
    table_part = to_absolute(deliver(part_pieces, "row", 1), row_index).reshape(width, vocab_part)

    def chosen(k):
        return pick_block(local_tokens, (col_index + k) % col_count, 1).reshape(-1)

    def one_hot(ids):
        return (ids[:, None] == vocab_line[None, :]).astype(low)

    looked = [
        matmul_last(one_hot(chosen(k)), table_low_t).astype(low) for k in range(col_count)
    ]
    found = summed(deliver(looked, "col", 1)).astype(low)
    embedded = lax.all_to_all(found, "row", split_axis=0, concat_axis=1, tiled=True).astype(
        jnp.float32
    )

    normed = rms_norm(embedded, norm_gains[0]).astype(low)
    project = absolute_columns(matmul(normed, qkv_full).astype(low))
    first_token = col_index * device_tokens
    positions = first_token + jnp.arange(device_tokens, dtype=jnp.int32)
    seq_prefix = jnp.sum(
        jnp.where(jnp.arange(prefix_lens.shape[0], dtype=jnp.int32) == row_index, prefix_lens, 0)
    )

    def rotate_here(values):
        return rotary(values, positions)

    queries_raw = project[:, :query_width].astype(jnp.float32).reshape(device_tokens, Q_HEADS, HEAD)
    keys_raw = (
        project[:, query_width : query_width + kv_width]
        .astype(jnp.float32)
        .reshape(device_tokens, KV_HEADS, HEAD)
    )
    queries = rotate_here(queries_raw).astype(low).reshape(device_tokens, KV_HEADS, group_size, HEAD)
    keys_local = rotate_here(keys_raw).astype(low).reshape(device_tokens, kv_width)
    keys_values = jnp.concatenate(
        collect(
            jnp.concatenate([keys_local, project[:, query_width + kv_width :]], axis=1), "col"
        ),
        axis=0,
    )
    attn_keys = keys_values[:, :kv_width].reshape(LEN, KV_HEADS, HEAD)
    attn_values = keys_values[:, kv_width:].reshape(LEN, KV_HEADS, HEAD)
    key_blocks = (col_index - jnp.arange(col_count, dtype=jnp.int32)) % col_count
    key_positions = (
        key_blocks[:, None] * device_tokens + jnp.arange(device_tokens, dtype=jnp.int32)[None, :]
    ).reshape(LEN)
    allowed = (key_positions[None, :] <= positions[:, None]) | (key_positions[None, :] < seq_prefix)

    raw_scores = (
        jnp.einsum("qhgd,khd->hgqk", queries, attn_keys, preferred_element_type=jnp.float32)
        * scaling
    )
    scores = jnp.where(allowed, raw_scores, MASK_VALUE)
    largest = jnp.max(scores, axis=-1, keepdims=True)
    weights = jnp.exp(scores - largest)
    attn_probs = weights / jnp.sum(weights, axis=-1, keepdims=True)
    attended = (
        jnp.einsum(
            "hgqk,khd->qhgd",
            attn_probs.astype(low),
            attn_values,
            preferred_element_type=jnp.float32,
        )
        .astype(low)
        .reshape(device_tokens, query_width)
    )
    attended = relative_columns(attended)
    hidden_one = embedded + matmul_last(attended, out_full)
    middle = rms_norm(hidden_one, norm_gains[1]).astype(low)
    gate_part = matmul(middle, gate_full)
    upward = matmul(middle, up_full)
    inner_act = swiglu(gate_part, upward).astype(low)
    hidden_two = hidden_one + matmul_last(inner_act, down_full)
    final = rms_norm(hidden_two, norm_gains[2]).astype(low)

    pick_hit = (loss_slots[:, None] == positions[None, :]).astype(low)
    final_here = matmul(pick_hit, final).astype(low)
    final_seq = lax.psum(final_here, "col")
    final_pick = lax.all_gather(final_seq, "row", axis=0, tiled=True)
    logits = matmul(final_pick, table_part)
    local_max = jnp.max(logits, axis=-1)
    local_sum = jnp.sum(jnp.exp(logits - local_max[:, None]), axis=-1)
    part_first = col_index * vocab_shard + row_index * vocab_part
    target_hit = (
        jnp.arange(vocab_part, dtype=jnp.int32)[None, :] == (targets_all - part_first)[:, None]
    )
    local_target = jnp.sum(jnp.where(target_hit, logits, 0.0), axis=-1)
    everyone = lax.all_gather(
        jnp.stack([local_max, local_sum, local_target]), ("row", "col"), axis=0
    )
    top = jnp.max(everyone[:, 0], axis=0)
    log_total = top + jnp.log(jnp.sum(everyone[:, 1] * jnp.exp(everyone[:, 0] - top), axis=0))
    target_logit = jnp.sum(everyone[:, 2], axis=0)
    valid_count = jnp.maximum(jnp.sum(valid_mask).astype(jnp.float32), 1.0)
    row_weights = valid_mask.astype(jnp.float32) / valid_count
    loss_value = jnp.sum(row_weights * (log_total - target_logit))
    grad_logits = (
        (jnp.exp(logits - log_total[:, None]) - target_hit.astype(jnp.float32))
        * row_weights[:, None]
    ).astype(low)
    grad_pick = matmul_last(grad_logits, table_part).astype(low)
    grad_seq = lax.psum_scatter(grad_pick, "row", scatter_dimension=0, tiled=True)
    grad_seq = lax.psum(grad_seq, "col")
    grad_final = matmul_first(pick_hit, grad_seq)

    table_grad_part = matmul_first(final_pick, grad_logits).astype(low)
    grad_parts = table_grad_part.reshape(row_count, features, vocab_part)
    grad_pieces = [pick_block(grad_parts, (row_index + k) % row_count, 0) for k in range(row_count)]
    table_grad = to_absolute(deliver(grad_pieces, "row", 1), row_index)
    table_grad = jnp.moveaxis(table_grad, 0, 1).reshape(features, vocab_shard).astype(jnp.float32)

    grad_two, gain_two = norm_back(hidden_two, norm_gains[2], grad_final)
    grad_two_low = grad_two.astype(low)
    down_grad = matmul_first(rotate_left(grad_two_low, 4), inner_act).astype(low)
    grad_inner = matmul(grad_two_low, down_full)
    unused, pull_swiglu = jax.vjp(swiglu, gate_part, upward)
    grad_gate, grad_up = pull_swiglu(grad_inner)
    grad_gate = grad_gate.astype(low)
    grad_up = grad_up.astype(low)
    gate_grad = matmul_first(rotate_left(middle, 2), grad_gate).astype(low)
    up_grad = matmul_first(rotate_left(middle, 3), grad_up).astype(low)
    grad_middle = matmul_last(grad_gate, gate_full) + matmul_last(grad_up, up_full)
    grad_middle_in, gain_one = norm_back(hidden_one, norm_gains[1], grad_middle)
    grad_one = grad_two + grad_middle_in
    grad_one_low = grad_one.astype(low)
    out_grad = matmul_first(rotate_left(grad_one_low, 1), attended).astype(low)
    grad_attended = absolute_columns(matmul(grad_one_low, out_full).astype(low)).reshape(
        device_tokens, KV_HEADS, group_size, HEAD
    )
    grad_probs = jnp.einsum(
        "qhgd,khd->hgqk", grad_attended, attn_values, preferred_element_type=jnp.float32
    )
    inner_sum = jnp.sum(attn_probs * grad_probs, axis=-1, keepdims=True)
    grad_scores = (attn_probs * (grad_probs - inner_sum)).astype(low)
    grad_queries = (
        jnp.einsum("hgqk,khd->qhgd", grad_scores, attn_keys, preferred_element_type=jnp.float32)
        * scaling
    )
    grad_keys = (
        jnp.einsum("hgqk,qhgd->khd", grad_scores, queries, preferred_element_type=jnp.float32)
        * scaling
    )
    grad_values = jnp.einsum(
        "hgqk,qhgd->khd",
        attn_probs.astype(low),
        grad_attended,
        preferred_element_type=jnp.float32,
    )
    grad_pairs = (
        jnp.concatenate([grad_keys.reshape(LEN, kv_width), grad_values.reshape(LEN, kv_width)], axis=1)
        .astype(low)
        .reshape(col_count, device_tokens, 2 * kv_width)
    )
    grad_pairs = summed(deliver([grad_pairs[k] for k in range(col_count)], "col", -1))
    unused, pull_query = jax.vjp(rotate_here, queries_raw)
    grad_query_raw = pull_query(grad_queries.reshape(device_tokens, Q_HEADS, HEAD))[0]
    unused, pull_key = jax.vjp(rotate_here, keys_raw)
    grad_key_raw = pull_key(grad_pairs[:, :kv_width].reshape(device_tokens, KV_HEADS, HEAD))[0]
    grad_project = relative_columns(
        jnp.concatenate(
            [
                grad_query_raw.reshape(device_tokens, query_width),
                grad_key_raw.reshape(device_tokens, kv_width),
                grad_pairs[:, kv_width:],
            ],
            axis=1,
        ).astype(low)
    )
    qkv_grad = matmul_first(rotate_left(normed, 0), grad_project).astype(low)
    grad_normed = matmul_last(grad_project, qkv_full)
    grad_embed_in, gain_zero = norm_back(embedded, norm_gains[0], grad_normed)
    grad_embedded = (grad_one + grad_embed_in).astype(low)
    by_feature = lax.all_to_all(grad_embedded, "row", split_axis=1, concat_axis=0, tiled=True)
    for k, piece in enumerate(collect(by_feature, "col")):
        table_grad = table_grad + matmul_first(piece, one_hot(chosen(-k)))
    gain_grads = lax.psum(jnp.stack([gain_zero, gain_one, gain_two]), ("row", "col"))

    def reduce_rows(*parts):
        together = parts[0] if len(parts) == 1 else jnp.concatenate(parts, axis=1)
        return lax.psum_scatter(together, "row", scatter_dimension=0, tiled=True)

    def reduce_cols(values):
        count = values.shape[1] // col_count
        return summed(
            deliver([values[:, k * count : (k + 1) * count] for k in range(col_count)], "col", -1)
        )

    def soap(left_rows, right_basis, weight, moment, square_avg):
        count = weight.shape[1]
        right_low = right_basis.astype(low)
        right = matmul(reduce_cols(left_rows).astype(low), right_low).astype(low)
        pieces = [
            lax.dynamic_slice_in_dim(right, (col_index + k) % col_count * count, count, 1)
            for k in range(col_count)
        ]
        rotated = summed(deliver(pieces, "col", 1))
        moment_new, square_new, step = moments(rotated, moment, square_avg)
        whole = absolute_columns(jnp.concatenate(collect(step.astype(low), "col"), axis=1))
        back = matmul_last(whole, right_low).astype(low)
        return moment_new, square_new, back

    mlp_down_rows = reduce_rows(down_grad)
    mlp_gate_up_rows = reduce_rows(gate_grad, up_grad)
    attn_rows = reduce_rows(out_grad, qkv_grad)
    down_moment, down_scale, down_back = soap(
        mlp_down_rows, feedforward_bases[2], mlp_weight[2], mlp_mean[2], mlp_square[2]
    )
    gate_moment, gate_scale, gate_back = soap(
        mlp_gate_up_rows[:, :ff_width], feedforward_bases[0], mlp_weight[0], mlp_mean[0], mlp_square[0]
    )
    up_moment, up_scale, up_back = soap(
        mlp_gate_up_rows[:, ff_width:], feedforward_bases[1], mlp_weight[1], mlp_mean[1], mlp_square[1]
    )
    out_moment, out_scale, out_back = soap(
        attn_rows[:, :out_width], out_bases, output_weight, out_mean, out_square
    )
    qkv_moment, qkv_scale, qkv_back = soap(
        attn_rows[:, out_width:], qkv_bases, qkv_weight, qkv_mean, qkv_square
    )
    back_mlp = lax.all_gather(
        jnp.concatenate([down_back, gate_back, up_back], axis=1), "row", axis=0, tiled=True
    )
    back_attn = lax.all_gather(
        jnp.concatenate([out_back, qkv_back], axis=1), "row", axis=0, tiled=True
    )
    update_down = matmul(bases_low[4], back_mlp[:, :ff_cols])
    update_gate = matmul(bases_low[2], back_mlp[:, ff_cols : 2 * ff_cols])
    update_up = matmul(bases_low[3], back_mlp[:, 2 * ff_cols :])
    update_out = matmul(bases_low[1], back_attn[:, :out_cols])
    update_qkv = matmul(bases_low[0], back_attn[:, out_cols:])
    update_mlp = jnp.stack([update_gate, update_up, update_down])
    mlp_moment = jnp.stack([gate_moment, up_moment, down_moment])
    mlp_scale = jnp.stack([gate_scale, up_scale, down_scale])
    qkv_next = qkv_weight + -(SOAP_RATE * (update_qkv + WEIGHT_DECAY * qkv_weight))
    out_update = -(SOAP_RATE * (update_out + WEIGHT_DECAY * output_weight))
    mlp_next = mlp_weight + -(SOAP_RATE * (update_mlp + WEIGHT_DECAY * mlp_weight))
    embed_change, embed_moment, embed_scale = adam_update(
        embed_table, table_grad.T, embed_mean, embed_square, WEIGHT_DECAY
    )
    embed_next = embed_table + embed_change
    gain_update, gain_moment, gain_scale = adam_update(
        norm_gains, gain_grads, gain_mean, gain_square, 0.0
    )
    return (
        loss_value,
        embed_next,
        embed_moment,
        embed_scale,
        gain_update,
        gain_moment,
        gain_scale,
        qkv_next,
        qkv_moment,
        qkv_scale,
        out_update,
        out_moment,
        out_scale,
        mlp_next,
        mlp_moment,
        mlp_scale,
    )


def solution(mesh):
    placed = (
        P("row"),
        P("row"),
        P("row"),
        P(),
        P(),
        P("col", "row"),
        P(),
        P("row", "col"),
        P("row", "col"),
        P(None, "row", "col"),
        P("col", "row"),
        P("col", "row"),
        P(),
        P(),
        P("row", "col"),
        P("row", "col"),
        P("row", "col"),
        P("row", "col"),
        P(None, "row", "col"),
        P(None, "row", "col"),
        P(None, "row", None),
        P("col", None),
        P("col", None),
        P(None, "col", None),
    )
    return jax.shard_map(
        per_device,
        mesh=mesh,
        in_specs=placed,
        out_specs=(
            P(),
            P("col", "row"),
            P("col", "row"),
            P("col", "row"),
            P(),
            P(),
            P(),
            P("row", "col"),
            P("row", "col"),
            P("row", "col"),
            P("row", "col"),
            P("row", "col"),
            P("row", "col"),
            P(None, "row", "col"),
            P(None, "row", "col"),
            P(None, "row", "col"),
        ),
        check_vma=False,
    )
```

time: 1860 us -> 1310 us (0.70)
  waiting for transfers between devices: 1190 us -> 425 us
  starting transfers between devices: 10.4 us -> 200 us
  matrix products: 223 us -> 346 us
  other arithmetic: 137 us -> 81.1 us
  blocking collectives: 168 us -> 126 us
    all_gather x13 -> x6, waiting for transfers between devices: 497 us -> 46.9 us  [the longest x1 46.8 us: per_device(): lax.all_gather(jnp.concatenate([bases_low[k] for k in range(5)], axis=1),...]
    reduce_scatter x11 -> x4, waiting for transfers between devices: 402 us -> 33.7 us  [the longest x1 33.7 us: per_device(): lax.psum_scatter(grad_pick, 'row', scatter_dimension=0, tiled=True)]
    unnamed x36 -> x12, waiting for transfers between devices: 269 us -> 0.2 us
    ppermute x0 -> x86, waiting for transfers between devices: none -> 260 us  [send(): lax.ppermute(value, axis, [(k, (k + shift) % count) for k in range(count)])]
    ppermute x0 -> x86, starting transfers between devices: none -> 190 us  [send(): lax.ppermute(value, axis, [(k, (k + shift) % count) for k in range(count)])]
    dot_general x6 -> x11, matrix products: 31.2 us -> 117 us  [matmul_first(): lax.dot_general(left_op, right_op, (((0,), (0,)), ((), ())), preferred_el...]
    dot_general x6 -> x15, matrix products: 33.4 us -> 112 us  [matmul_last(): lax.dot_general(left_op, right_op, (((1,), (1,)), ((), ())), preferred_el...]
    dot_general x14 -> x2, matrix products: 92.4 us -> 17.7 us  [the longest x1 9.61 us: per_device(): jnp.einsum('hgqk,qhgd->khd', attn_probs.astype(low), grad_attended, prefe...]
  transfers between devices with their start and end apart: 32 -> 100, of which waited for: 29 -> 40; matrix products, arithmetic and copies ran while one was open for 13% -> 36% of each run, Pallas kernels for 0% -> 0%
where the time goes in v1:
time: 1310 us; the launch traced here: 1300 us
  waiting for transfers between devices  425 us (32%)
  matrix products  346 us (26%)
  starting transfers between devices  200 us (15%)
  blocking collectives  126 us (10%)
  local copies, waits for them, and re-layouts  99.6 us (8%)
  other arithmetic  81.1 us (6%)
  between operations  17.8 us (1%)
    ppermute x86, waiting for transfers between devices, send(): lax.ppermute(value, axis, [(k, (k + shift) % count) for k in range(count)])  260 us
    ppermute x86, starting transfers between devices, send(): lax.ppermute(value, axis, [(k, (k + shift) % count) for k in range(count)])  190 us
    dot_general x11, matrix products, matmul_first(): lax.dot_general(left_op, right_op, (((0,), (0,)), ((), ())), preferred_el...  117 us
    dot_general x15, matrix products, matmul_last(): lax.dot_general(left_op, right_op, (((1,), (1,)), ((), ())), preferred_el...  112 us
    all_gather x1, blocking collectives, per_device(): lax.all_gather(jnp.stack([local_max, local_sum, local_target]), ('row', '...  69.5 us
    dot_general x17, matrix products, matmul(): return jnp.dot(left_op, right_op, preferred_element_type=jnp.float32)  65 us
    psum x1, blocking collectives, per_device(): lax.psum(jnp.stack([gain_zero, gain_one, gain_two]), ('row', 'col'))  47.3 us
    all_gather x1, waiting for transfers between devices, per_device(): lax.all_gather(jnp.concatenate([bases_low[k] for k in range(5)], axis=1),...  46.8 us
  transfers between devices with their start and end apart: 100, of which 40 were waited for; matrix products, arithmetic and copies ran while one was open for 36% of the time, Pallas kernels for 0%

profile of v1, /device:TPU:0, one launch (start us, length us, event | category | flops | bytes accessed | tf_op | source)
XLA Modules:
  0.0 1295.9 jit_solution(15247871977294278234)
XLA Ops:
  19.5 14.5 %collective-permute-done.7 = bf16[144,288]{1,0:T(8,128)(2,1)S(1)} collective-permute-done((bf16[144,288]{1,0:T(8,128)(2,1)S(1)}, bf16[144,288]{1,0:T(8,128)(2,1)S(1)}, u32[]{:S(2)}, u32[]{:S(2)}) %collective-permute-start.7) | collective-permute-done | bytes 82976 | tf_op jit(solution)/shard_map/ppermute | solution.py:24
  46.9 8.6 collective-permute-done.13
  58.4 10.6 collective-permute-start.19
  72.8 10.0 collective-permute-done.16
  82.9 9.4 collective-permute-done.19
  96.6 9.1 all-gather.2
  106.4 15.7 %fusion.91 = bf16[2048,144]{0,1:T(8,128)(2,1)} fusion(bf16[8000,144]{0,1:T(8,128)(2,1)S(1)} %convert_element_type.417, s32[2048]{0:T(1024)S(1)} %bitcast.531), kind=kOutput, calls=%fused_computation.122 | convolution fusion | flops 4735270912 | bytes 2902016 | tf_op jit(solution)/shard_map/dot_general | solution.py:86
  122.1 6.5 collective-permute-start.2
  128.6 15.7 %fusion.92 = bf16[2048,144]{0,1:T(8,128)(2,1)} fusion(bf16[8000,144]{0,1:T(8,128)(2,1)S(1)} %convert_element_type.417, s32[2048]{0:T(1024)S(1)} %bitcast.532), kind=kOutput, calls=%fused_computation.123 | convolution fusion | flops 4735270912 | bytes 2902016 | tf_op jit(solution)/shard_map/dot_general | solution.py:86
  144.7 15.7 %fusion.93 = bf16[2048,144]{0,1:T(8,128)(2,1)} fusion(bf16[8000,144]{0,1:T(8,128)(2,1)S(1)} %convert_element_type.417, s32[2048]{0:T(1024)S(1)} %bitcast.533), kind=kOutput, calls=%fused_computation.124 | convolution fusion | flops 4735270912 | bytes 2902016 | tf_op jit(solution)/shard_map/dot_general | solution.py:86
  161.5 23.3 %collective-permute-done.1 = bf16[2048,144]{0,1:T(8,128)(2,1)} collective-permute-done((bf16[2048,144]{0,1:T(8,128)(2,1)}, bf16[2048,144]{0,1:T(8,128)(2,1)}, u32[]{:S(2)}, u32[]{:S(2)}) %collective-permute-start.1) | collective-permute-done | bytes 589856 | tf_op jit(solution)/shard_map/ppermute | solution.py:24
  184.8 16.1 %add_convert_fusion.1 = bf16[2048,144]{0,1:T(8,128)(2,1)S(1)} fusion(bf16[2048,144]{0,1:T(8,128)(2,1)S(1)} %collective-permute-done.2, bf16[2048,144]{0,1:T(8,128)(2,1)} %collective-permute-done.1, bf16[2048,144]{0,1:T(8,128)(2,1)} %collective-permute-done, bf16[8000,144]{0,1:T(8,128)(2,1)S(1)} %convert_element_type.417, s32[2048]{0:T(1024)S(1)} %bitcast.526), kind=kOutput, calls=%fused_computation.231 | convolution fusion | flops 4737630208 | bytes 4671488 | tf_op jit(solution)/shard_map/dot_general | solution.py:86
  206.5 9.2 all-to-all-done
  229.2 7.0 collective-permute-done.11
  236.1 21.3 %collective-permute-done.10 = bf16[256,768]{0,1:T(8,128)(2,1)S(1)} collective-permute-done((bf16[256,768]{0,1:T(8,128)(2,1)S(1)}, bf16[256,768]{0,1:T(8,128)(2,1)S(1)}, u32[]{:S(2)}, u32[]{:S(2)}) %collective-permute-start.10) | collective-permute-done | bytes 393248 | tf_op jit(solution)/shard_map/ppermute | solution.py:24
  257.8 11.4 fusion.306
  269.3 8.1 fusion.123
  287.6 8.5 multiply_convert_fusion.2
  303.9 37.6 %all-reduce.7.cloned.1.call-done = bf16[128,1152]{1,0:T(8,128)(2,1)} async-done(((bf16[128,1152]{1,0:T(8,128)(2,1)}), bf16[128,1152]{1,0:T(8,128)(2,1)}) %all-reduce.7.cloned.1.call-update) | async-done | bytes 294928 | tf_op jit(solution)/shard_map/psum | solution.py:288
  351.4 6.0 constant_dynamic-slice_fusion.18
  382.4 13.1 %collective-permute-done.24 = bf16[144,1000]{1,0:T(8,128)(2,1)} collective-permute-done((bf16[144,1000]{1,0:T(8,128)(2,1)}, bf16[144,1000]{1,0:T(8,128)(2,1)}, u32[]{:S(2)}, u32[]{:S(2)}) %collective-permute-start.24) | collective-permute-done | bytes 288032 | tf_op jit(solution)/shard_map/ppermute | solution.py:24
  406.3 69.5 %all-gather.3 = f32[32,3,1024]{2,1,0:T(4,128)S(1)} all-gather(f32[1,3,1024]{2,1,0:T(4,128)S(1)} %maximum_bitcast_fusion), channel_id=3, replica_groups=mesh['row'=8,'col'=4] {'row','col'}, dimensions={0}, use_global_device_ids=true | all-gather | bytes 405504 | tf_op jit(solution)/shard_map/all_gather | solution.py:298
  487.8 33.7 %reduce-scatter.5.cloned.1.call-done = bf16[128,1152]{1,0:T(8,128)(2,1)} async-done(((bf16[1024,1152]{1,0:T(8,128)(2,1)}), bf16[128,1152]{1,0:T(8,128)(2,1)}) %reduce-scatter.5.cloned.1.call-update) | async-done | bytes 294928 | tf_op jit(solution)/shard_map/reduce_scatter | solution.py:312
  522.6 37.0 %all-reduce.9.cloned.1.call-done = bf16[128,1152]{1,0:T(8,128)(2,1)} async-done(((bf16[128,1152]{1,0:T(8,128)(2,1)}), bf16[128,1152]{1,0:T(8,128)(2,1)}) %all-reduce.9.cloned.1.call-update) | async-done | bytes 294928 | tf_op jit(solution)/shard_map/psum | solution.py:313
  563.7 7.2 fusion.55
  570.9 6.4 fusion.33
  577.4 6.2 multiply_reduce_fusion.1
  589.6 46.8 %all-gather.17.cloned.1.call-done = bf16[1152,5760]{1,0:T(8,128)(2,1)} async-done(((bf16[144,5760]{1,0:T(8,128)(2,1)}), bf16[1152,5760]{1,0:T(8,128)(2,1)}) %all-gather.17.cloned.1.call-update) | async-done | bytes 13271056 | tf_op jit(solution)/shard_map/all_gather | solution.py:177
  636.4 8.3 convolution_convert_fusion.2
  646.1 15.0 %fusion.17 = (f32[6,3,256]{2,1,0:T(4,128)S(1)}, f32[6,1024,256,3]{2,1,3,0:T(8,128)}) fusion(f32[6,3,256,1024]{2,3,1,0:T(8,128)} %get-tuple-element.162, f32[6,3,256]{2,1,0:T(4,128)S(1)} %copy-done.76, bf16[1024,6,64,1]{0,2,3,1:T(8,128)(2,1)S(1)} %bitcast.496, bf16[256,6,3,64]{0,3,2,1:T(8,128)(2,1)S(1)} %bitcast.505), kind=kOutput, calls=%fused_computation.26 | convolution fusion | flops 618130944 | bytes 39161856 | tf_op jit(solution)/shard_map/qhgd,khd->hgqk/dot_general | solution.py:340
  661.0 14.2 %fusion.19 = bf16[6,3,256,1024]{2,3,1,0:T(8,128)(2,1)S(1)} fusion(f32[6,1024,256,3]{2,1,3,0:T(8,128)} %get-tuple-element.174, f32[6,3,256]{2,1,0:T(4,128)S(1)} %get-tuple-element.173, f32[6,3,256,1024]{2,3,1,0:T(8,128)} %get-tuple-element.162, f32[6,3,256]{2,1,0:T(4,128)S(1)} %copy-done.76), kind=kLoop, calls=%fused_computation.28 | loop fusion | flops 18874368 | bytes 47222784 | tf_op jit(solution)/shard_map/convert_element_type | solution.py:344
  681.8 9.6 bitcast_convert_fusion
  714.2 9.6 collective-permute-done.36
  726.6 6.7 convolution_convert_fusion.4
  740.3 8.0 convolution_convert_fusion
  748.3 7.5 convolution_convert_fusion.1
  755.8 13.5 %pad_maximum_fusion = bf16[1152,6144]{1,0:T(8,128)(2,1)} fusion(bf16[1152,3072]{1,0:T(8,128)(2,1)} %convolution_convert_fusion, bf16[1152,3072]{1,0:T(8,128)(2,1)} %convolution_convert_fusion.1), kind=kLoop, calls=%fused_computation.32 | loop fusion | flops 28311552 | bytes 28311552 | tf_op jit(solution)/shard_map/concatenate | solution.py:389
  771.7 6.5 convolution_convert_fusion.6
  797.7 5.9 collective-permute-done.29
  809.8 20.1 %collective-permute-start.61 = (bf16[144,768]{1,0:T(8,128)(2,1)S(1)}, bf16[144,768]{1,0:T(8,128)(2,1)S(1)}, u32[]{:S(2)}, u32[]{:S(2)}) collective-permute-start(bf16[144,768]{1,0:T(8,128)(2,1)S(1)} %get-tuple-element.113), channel_id=1, source_target_pairs={{0,1},{1,2},{2,3},{3,0},{4,5},{5,6},{6,7},{7,4},{8,9},{9,10},{10,1... | collective-permute-start | bytes 663560 | tf_op jit(solution)/shard_map/ppermute | solution.py:24
  835.8 6.7 collective-permute-done.60
  842.6 6.9 convolution_convert_fusion.9
  850.4 7.3 collective-permute-start.64
  871.3 6.3 collective-permute-start.52
  884.9 6.6 collective-permute-start.46
  894.8 6.0 collective-permute-start.44
  914.0 11.3 collective-permute-done.48
  925.9 5.9 collective-permute-done.49
  932.5 6.6 collective-permute-done.53
  978.0 11.6 collective-permute-start.77
  995.7 8.3 collective-permute-start.73
  1021.2 9.9 collective-permute-done.72
  1031.0 7.0 collective-permute-done.81
  1059.6 6.2 reshape.400
  1065.9 9.8 collective-permute-done.84
  1075.7 6.7 collective-permute-start.65
  1088.3 13.4 %collective-permute-done.66 = bf16[144,768]{1,0:T(8,128)(2,1)S(1)} collective-permute-done((bf16[144,768]{1,0:T(8,128)(2,1)S(1)}, bf16[144,768]{1,0:T(8,128)(2,1)S(1)}, u32[]{:S(2)}, u32[]{:S(2)}) %collective-permute-start.66) | collective-permute-done | bytes 221216 | tf_op jit(solution)/shard_map/ppermute | solution.py:24
  1126.1 5.9 all-to-all-start.1
  1132.0 47.3 %psum.23 = f32[3,1152]{1,0:T(4,128)S(1)} all-reduce(f32[3,1152]{1,0:T(4,128)S(1)} %pad_maximum_fusion.25), channel_id=1, replica_groups=mesh['row'=8,'col'=4] {'row','col'}, use_global_device_ids=true, to_apply=%region_24.28 | all-reduce | flops 3456 | bytes 27648 | tf_op jit(solution)/shard_map/psum | solution.py:386
  1183.7 17.0 %fusion.22 = f32[144,8000]{1,0:T(8,128)} fusion(f32[144,8000]{1,0:T(8,128)} %reshape.400, bf16[2048,144]{0,1:T(8,128)(2,1)S(1)} %bitcast.502, s32[2048]{0:T(1024)S(1)} %bitcast.527), kind=kOutput, calls=%fused_computation.37 | convolution fusion | flops 4736128000 | bytes 9814016 | tf_op jit(solution)/shard_map/dot_general | solution.py:92
  1200.7 15.4 %fusion.5 = f32[144,8000]{1,0:T(8,128)} fusion(bf16[2048,144]{0,1:T(8,128)(2,1)S(1)} %collective-permute-done.40, s32[2048]{0:T(1024)S(1)} %bitcast.530), kind=kOutput, calls=%fused_computation.12 | convolution fusion | flops 4734976000 | bytes 5206016 | tf_op jit(solution)/shard_map/dot_general | solution.py:92
  1216.1 17.0 %collective-permute-done.39 = bf16[2048,144]{0,1:T(8,128)(2,1)S(1)} collective-permute-done((bf16[2048,144]{0,1:T(8,128)(2,1)S(1)}, bf16[2048,144]{0,1:T(8,128)(2,1)S(1)}, u32[]{:S(2)}, u32[]{:S(2)}) %collective-permute-start.39) | collective-permute-done | bytes 589856 | tf_op jit(solution)/shard_map/ppermute | solution.py:24
  1233.0 15.6 %fusion.4 = f32[144,8000]{1,0:T(8,128)} fusion(bf16[2048,144]{0,1:T(8,128)(2,1)S(1)} %collective-permute-done.39, s32[2048]{0:T(1024)S(1)} %bitcast.529), kind=kOutput, calls=%fused_computation.11 | convolution fusion | flops 4734976000 | bytes 5206016 | tf_op jit(solution)/shard_map/dot_general | solution.py:92
  1249.5 24.3 %negate_add_fusion = (f32[8000,144]{0,1:T(8,128)}, f32[8000,144]{0,1:T(8,128)}, f32[8000,144]{0,1:T(8,128)}) fusion(f32[8000,144]{0,1:T(8,128)S(1)} %bitcast.464, f32[8000,144]{0,1:T(8,128)} %param.43, f32[8000,144]{0,1:T(8,128)} %param.42, f32[144,8000]{1,0:T(8,128)} %fusion.5, f32[144,8000]{1,0:T(8,128)} %fusion.4, f32[144,8000]{1,0:T(8,128)} %fusion.22, ...), kind=kOutput, calls=%fused_computation.79 | convolution fusion | flops 4753408000 | bytes 42070016 | tf_op jit(solution)/shard_map/dot_general | solution.py:92
  (612 shorter events, 390.1 us)
Async XLA Ops:
  7.2 209.2 %all-gather.11.cloned.1.call-start = ((), (), s32[]{:S(2)}) async-start(), calls=%async_computation.6 | async-start | bytes 7962624 | tf_op jit(solution)/shard_map/all_gather | solution.py:170
  12.3 21.6 %collective-permute-start.3 = (bf16[144,480]{1,0:T(8,128)(2,1)S(1)}, bf16[144,480]{1,0:T(8,128)(2,1)S(1)}, u32[]{:S(2)}, u32[]{:S(2)}) collective-permute-start(bf16[144,480]{1,0:T(8,128)(2,1)S(1)} %convert_element_type.432), channel_id=1, source_target_pairs={{0,1},{1,2},{2,3},{3,0},{4,5},{5,6},{6,7},{7,4},{8,9},{9,10},{10,1... | collective-permute-start | bytes 414728 | tf_op jit(solution)/shard_map/ppermute | solution.py:24
  14.0 20.0 %collective-permute-start.4 = (bf16[144,480]{1,0:T(8,128)(2,1)S(1)}, bf16[144,480]{1,0:T(8,128)(2,1)S(1)}, u32[]{:S(2)}, u32[]{:S(2)}) collective-permute-start(bf16[144,480]{1,0:T(8,128)(2,1)S(1)} %convert_element_type.432), channel_id=1, source_target_pairs={{0,2},{1,3},{2,0},{3,1},{4,6},{5,7},{6,4},{7,5},{8,10},{9,11},{10,... | collective-permute-start | bytes 414728 | tf_op jit(solution)/shard_map/ppermute | solution.py:24
  15.1 18.9 %collective-permute-start.5 = (bf16[144,480]{1,0:T(8,128)(2,1)S(1)}, bf16[144,480]{1,0:T(8,128)(2,1)S(1)}, u32[]{:S(2)}, u32[]{:S(2)}) collective-permute-start(bf16[144,480]{1,0:T(8,128)(2,1)S(1)} %convert_element_type.432), channel_id=1, source_target_pairs={{0,3},{1,0},{2,1},{3,2},{4,7},{5,4},{6,5},{7,6},{8,11},{9,8},{10,9... | collective-permute-start | bytes 414728 | tf_op jit(solution)/shard_map/ppermute | solution.py:24
  35.4 246.8 %all-gather.13.cloned.1.call-start = ((), (), s32[]{:S(2)}) async-start(), calls=%async_computation.7 | async-start | bytes 23887872 | tf_op jit(solution)/shard_map/all_gather | solution.py:175
  40.9 28.1 %collective-permute-start.15 = (bf16[144,768]{1,0:T(8,128)(2,1)S(1)}, bf16[144,768]{1,0:T(8,128)(2,1)S(1)}, u32[]{:S(2)}, u32[]{:S(2)}) collective-permute-start(bf16[144,768]{1,0:T(8,128)(2,1)S(1)} %get-tuple-element.128), channel_id=1, source_target_pairs={{0,1},{1,2},{2,3},{3,0},{4,5},{5,6},{6,7},{7,4},{8,9},{9,10},{10,1... | collective-permute-start | bytes 663560 | tf_op jit(solution)/shard_map/ppermute | solution.py:24
  42.1 40.7 %collective-permute-start.16 = (bf16[144,768]{1,0:T(8,128)(2,1)S(1)}, bf16[144,768]{1,0:T(8,128)(2,1)S(1)}, u32[]{:S(2)}, u32[]{:S(2)}) collective-permute-start(bf16[144,768]{1,0:T(8,128)(2,1)S(1)} %get-tuple-element.128), channel_id=1, source_target_pairs={{0,2},{1,3},{2,0},{3,1},{4,6},{5,7},{6,4},{7,5},{8,10},{9,11},{10,... | collective-permute-start | bytes 663560 | tf_op jit(solution)/shard_map/ppermute | solution.py:24
  46.0 36.8 %collective-permute-start.17 = (bf16[144,768]{1,0:T(8,128)(2,1)S(1)}, bf16[144,768]{1,0:T(8,128)(2,1)S(1)}, u32[]{:S(2)}, u32[]{:S(2)}) collective-permute-start(bf16[144,768]{1,0:T(8,128)(2,1)S(1)} %get-tuple-element.128), channel_id=1, source_target_pairs={{0,3},{1,0},{2,1},{3,2},{4,7},{5,4},{6,5},{7,6},{8,11},{9,8},{10,9... | collective-permute-start | bytes 663560 | tf_op jit(solution)/shard_map/ppermute | solution.py:24
  55.5 27.4 %collective-permute-start.18 = (bf16[144,768]{1,0:T(8,128)(2,1)S(1)}, bf16[144,768]{1,0:T(8,128)(2,1)S(1)}, u32[]{:S(2)}, u32[]{:S(2)}) collective-permute-start(bf16[144,768]{1,0:T(8,128)(2,1)S(1)} %get-tuple-element.127), channel_id=1, source_target_pairs={{0,1},{1,2},{2,3},{3,0},{4,5},{5,6},{6,7},{7,4},{8,9},{9,10},{10,1... | collective-permute-start | bytes 663560 | tf_op jit(solution)/shard_map/ppermute | solution.py:24
  58.4 33.9 %collective-permute-start.19 = (bf16[144,768]{1,0:T(8,128)(2,1)S(1)}, bf16[144,768]{1,0:T(8,128)(2,1)S(1)}, u32[]{:S(2)}, u32[]{:S(2)}) collective-permute-start(bf16[144,768]{1,0:T(8,128)(2,1)S(1)} %get-tuple-element.127), channel_id=1, source_target_pairs={{0,2},{1,3},{2,0},{3,1},{4,6},{5,7},{6,4},{7,5},{8,10},{9,11},{10,... | collective-permute-start | bytes 663560 | tf_op jit(solution)/shard_map/ppermute | solution.py:24
  69.0 23.3 %collective-permute-start.20 = (bf16[144,768]{1,0:T(8,128)(2,1)S(1)}, bf16[144,768]{1,0:T(8,128)(2,1)S(1)}, u32[]{:S(2)}, u32[]{:S(2)}) collective-permute-start(bf16[144,768]{1,0:T(8,128)(2,1)S(1)} %get-tuple-element.127), channel_id=1, source_target_pairs={{0,3},{1,0},{2,1},{3,2},{4,7},{5,4},{6,5},{7,6},{8,11},{9,8},{10,9... | collective-permute-start | bytes 663560 | tf_op jit(solution)/shard_map/ppermute | solution.py:24
  122.1 39.4 %collective-permute-start.2 = (bf16[2048,144]{0,1:T(8,128)(2,1)}, bf16[2048,144]{0,1:T(8,128)(2,1)S(1)}, u32[]{:S(2)}, u32[]{:S(2)}) collective-permute-start(bf16[2048,144]{0,1:T(8,128)(2,1)} %fusion.91), channel_id=1, source_target_pairs={{0,3},{1,0},{2,1},{3,2},{4,7},{5,4},{6,5},{7,6},{8,11},{9,8},{10,9... | collective-permute-start | bytes 1769480 | tf_op jit(solution)/shard_map/ppermute | solution.py:24
  144.3 40.4 %collective-permute-start.1 = (bf16[2048,144]{0,1:T(8,128)(2,1)}, bf16[2048,144]{0,1:T(8,128)(2,1)}, u32[]{:S(2)}, u32[]{:S(2)}) collective-permute-start(bf16[2048,144]{0,1:T(8,128)(2,1)} %fusion.92), channel_id=1, source_target_pairs={{0,2},{1,3},{2,0},{3,1},{4,6},{5,7},{6,4},{7,5},{8,10},{9,11},{10,... | collective-permute-start | bytes 1769480 | tf_op jit(solution)/shard_map/ppermute | solution.py:24
  160.4 24.4 %collective-permute-start = (bf16[2048,144]{0,1:T(8,128)(2,1)}, bf16[2048,144]{0,1:T(8,128)(2,1)}, u32[]{:S(2)}, u32[]{:S(2)}) collective-permute-start(bf16[2048,144]{0,1:T(8,128)(2,1)} %fusion.93), channel_id=1, source_target_pairs={{0,1},{1,2},{2,3},{3,0},{4,5},{5,6},{6,7},{7,4},{8,9},{9,10},{10,1... | collective-permute-start | bytes 1769480 | tf_op jit(solution)/shard_map/ppermute | solution.py:24
  205.3 136.1 %all-reduce.7.cloned.1.call-start = ((), (), s32[]{:S(2)}) async-start(), calls=%async_computation.8 | async-start | bytes 589824 | tf_op jit(solution)/shard_map/psum | solution.py:288
  226.6 30.8 %collective-permute-start.10 = (bf16[256,768]{0,1:T(8,128)(2,1)S(1)}, bf16[256,768]{0,1:T(8,128)(2,1)S(1)}, u32[]{:S(2)}, u32[]{:S(2)}) collective-permute-start(bf16[256,768]{0,1:T(8,128)(2,1)S(1)} %pad_maximum_fusion.11), channel_id=1, source_target_pairs={{0,2},{1,3},{2,0},{3,1},{4,6},{5,7},{6,4},{7,5},{8,10},{9,11},{10,... | collective-permute-start | bytes 1179656 | tf_op jit(solution)/shard_map/ppermute | solution.py:24
  226.6 30.8 %collective-permute-start.9 = (bf16[256,768]{0,1:T(8,128)(2,1)S(1)}, bf16[256,768]{0,1:T(8,128)(2,1)S(1)}, u32[]{:S(2)}, u32[]{:S(2)}) collective-permute-start(bf16[256,768]{0,1:T(8,128)(2,1)S(1)} %pad_maximum_fusion.11), channel_id=1, source_target_pairs={{0,1},{1,2},{2,3},{3,0},{4,5},{5,6},{6,7},{7,4},{8,9},{9,10},{10,1... | collective-permute-start | bytes 1179656 | tf_op jit(solution)/shard_map/ppermute | solution.py:24
  303.7 96.1 %all-gather.15.cloned.1.call-start = ((), (), s32[]{:S(2)}) async-start(), calls=%async_computation.9 | async-start | bytes 2654208 | tf_op jit(solution)/shard_map/all_gather | solution.py:289
  341.5 180.0 %reduce-scatter.5.cloned.1.call-start = ((), (), s32[]{:S(2)}) async-start(), calls=%async_computation.10 | async-start | bytes 2654208 | tf_op jit(solution)/shard_map/reduce_scatter | solution.py:312
  359.4 20.2 %collective-permute-start.22 = (bf16[144,1000]{1,0:T(8,128)(2,1)}, bf16[144,1000]{1,0:T(8,128)(2,1)}, u32[]{:S(2)}, u32[]{:S(2)}) collective-permute-start(bf16[144,1000]{1,0:T(8,128)(2,1)} %bitcast.460), channel_id=1, source_target_pairs={{0,24},{4,28},{8,0},{12,4},{16,8},{20,12},{24,16},{28,20},{1,25},{... | collective-permute-start | bytes 864008 | tf_op jit(solution)/shard_map/ppermute | solution.py:24
  362.2 19.2 %collective-permute-start.23 = (bf16[144,1000]{1,0:T(8,128)(2,1)}, bf16[144,1000]{1,0:T(8,128)(2,1)}, u32[]{:S(2)}, u32[]{:S(2)}) collective-permute-start(bf16[144,1000]{1,0:T(8,128)(2,1)} %bitcast.459), channel_id=1, source_target_pairs={{0,20},{4,24},{8,28},{12,0},{16,4},{20,8},{24,12},{28,16},{1,21},{... | collective-permute-start | bytes 864008 | tf_op jit(solution)/shard_map/ppermute | solution.py:24
  363.4 32.0 %collective-permute-start.24 = (bf16[144,1000]{1,0:T(8,128)(2,1)}, bf16[144,1000]{1,0:T(8,128)(2,1)}, u32[]{:S(2)}, u32[]{:S(2)}) collective-permute-start(bf16[144,1000]{1,0:T(8,128)(2,1)} %bitcast.458), channel_id=1, source_target_pairs={{0,16},{4,20},{8,24},{12,28},{16,0},{20,4},{24,8},{28,12},{1,17},{... | collective-permute-start | bytes 864008 | tf_op jit(solution)/shard_map/ppermute | solution.py:24
  365.7 30.7 %collective-permute-start.25 = (bf16[144,1000]{1,0:T(8,128)(2,1)}, bf16[144,1000]{1,0:T(8,128)(2,1)}, u32[]{:S(2)}, u32[]{:S(2)}) collective-permute-start(bf16[144,1000]{1,0:T(8,128)(2,1)} %bitcast.457), channel_id=1, source_target_pairs={{0,12},{4,16},{8,20},{12,24},{16,28},{20,0},{24,4},{28,8},{1,13},{... | collective-permute-start | bytes 864008 | tf_op jit(solution)/shard_map/ppermute | solution.py:24
  373.0 24.4 %collective-permute-start.26 = (bf16[144,1000]{1,0:T(8,128)(2,1)}, bf16[144,1000]{1,0:T(8,128)(2,1)S(1)}, u32[]{:S(2)}, u32[]{:S(2)}) collective-permute-start(bf16[144,1000]{1,0:T(8,128)(2,1)} %bitcast.508), channel_id=1, source_target_pairs={{0,8},{4,12},{8,16},{12,20},{16,24},{20,28},{24,0},{28,4},{1,9},{5... | collective-permute-start | bytes 864008 | tf_op jit(solution)/shard_map/ppermute | solution.py:24
  482.4 77.2 %all-reduce.9.cloned.1.call-start = ((), (), s32[]{:S(2)}) async-start(), calls=%async_computation.11 | async-start | bytes 589824 | tf_op jit(solution)/shard_map/psum | solution.py:313
  521.5 115.0 %all-gather.17.cloned.1.call-start = ((), (), s32[]{:S(2)}) async-start(), calls=%async_computation.12 | async-start | bytes 14929920 | tf_op jit(solution)/shard_map/all_gather | solution.py:177
  522.4 286.3 %reduce-scatter.9.cloned.1.call-start = ((), (), s32[]{:S(2)}) async-start(), calls=%async_computation.15 | async-start | bytes 7962624 | tf_op jit(solution)/shard_map/reduce_scatter | solution.py:390
  644.8 212.9 %reduce-scatter.7.cloned.1.call-start = ((), (), s32[]{:S(2)}) async-start(), calls=%async_computation.13 | async-start | bytes 7962624 | tf_op jit(solution)/shard_map/reduce_scatter | solution.py:390
  693.5 20.7 %collective-permute-start.37 = (bf16[256,768]{0,1:T(8,128)(2,1)}, bf16[256,768]{0,1:T(8,128)(2,1)}, u32[]{:S(2)}, u32[]{:S(2)}) collective-permute-start(bf16[256,768]{0,1:T(8,128)(2,1)} %get-tuple-element.87), channel_id=1, source_target_pairs={{0,1},{1,2},{2,3},{3,0},{4,5},{5,6},{6,7},{7,4},{8,9},{9,10},{10,1... | collective-permute-start | bytes 1179656 | tf_op jit(solution)/shard_map/ppermute | solution.py:24
  695.0 28.8 %collective-permute-start.36 = (bf16[256,768]{0,1:T(8,128)(2,1)}, bf16[256,768]{0,1:T(8,128)(2,1)}, u32[]{:S(2)}, u32[]{:S(2)}) collective-permute-start(bf16[256,768]{0,1:T(8,128)(2,1)} %get-tuple-element.88), channel_id=1, source_target_pairs={{0,2},{1,3},{2,0},{3,1},{4,6},{5,7},{6,4},{7,5},{8,10},{9,11},{10,... | collective-permute-start | bytes 1179656 | tf_op jit(solution)/shard_map/ppermute | solution.py:24
  697.4 26.4 %collective-permute-start.35 = (bf16[256,768]{0,1:T(8,128)(2,1)}, bf16[256,768]{0,1:T(8,128)(2,1)}, u32[]{:S(2)}, u32[]{:S(2)}) collective-permute-start(bf16[256,768]{0,1:T(8,128)(2,1)} %get-tuple-element.86), channel_id=1, source_target_pairs={{0,3},{1,0},{2,1},{3,2},{4,7},{5,4},{6,5},{7,6},{8,11},{9,8},{10,9... | collective-permute-start | bytes 1179656 | tf_op jit(solution)/shard_map/ppermute | solution.py:24
  739.3 216.9 %reduce-scatter.11.cloned.1.call-start = ((), (), s32[]{:S(2)}) async-start(), calls=%async_computation.16 | async-start | bytes 15925248 | tf_op jit(solution)/shard_map/reduce_scatter | solution.py:390
  769.3 504.6 %all-gather.19.cloned.1.call-start = ((), (), s32[]{:S(2)}) async-start(), calls=%async_computation.14 | async-start | bytes 1990656 | tf_op jit(solution)/shard_map/all_gather | solution.py:433
  783.5 20.1 %collective-permute-start.29 = (bf16[144,1000]{1,0:T(8,128)(2,1)}, bf16[144,1000]{1,0:T(8,128)(2,1)S(1)}, u32[]{:S(2)}, u32[]{:S(2)}) collective-permute-start(bf16[144,1000]{1,0:T(8,128)(2,1)} %get-tuple-element.66), channel_id=1, source_target_pairs={{0,24},{4,28},{8,0},{12,4},{16,8},{20,12},{24,16},{28,20},{1,25},{... | collective-permute-start | bytes 864008 | tf_op jit(solution)/shard_map/ppermute | solution.py:24
  788.9 19.0 %collective-permute-start.32 = (bf16[144,1000]{1,0:T(8,128)(2,1)S(1)}, bf16[144,1000]{1,0:T(8,128)(2,1)S(1)}, u32[]{:S(2)}, u32[]{:S(2)}) collective-permute-start(bf16[144,1000]{1,0:T(8,128)(2,1)S(1)} %get-tuple-element.63), channel_id=1, source_target_pairs={{0,12},{4,16},{8,20},{12,24},{16,28},{20,0},{24,4},{28,8},{1,13},{... | collective-permute-start | bytes 864008 | tf_op jit(solution)/shard_map/ppermute | solution.py:24
  795.4 37.0 %collective-permute-start.33 = (bf16[144,1000]{1,0:T(8,128)(2,1)S(1)}, bf16[144,1000]{1,0:T(8,128)(2,1)S(1)}, u32[]{:S(2)}, u32[]{:S(2)}) collective-permute-start(bf16[144,1000]{1,0:T(8,128)(2,1)S(1)} %get-tuple-element.62), channel_id=1, source_target_pairs={{0,8},{4,12},{8,16},{12,20},{16,24},{20,28},{24,0},{28,4},{1,9},{5... | collective-permute-start | bytes 864008 | tf_op jit(solution)/shard_map/ppermute | solution.py:24
  809.8 26.0 %collective-permute-start.61 = (bf16[144,768]{1,0:T(8,128)(2,1)S(1)}, bf16[144,768]{1,0:T(8,128)(2,1)S(1)}, u32[]{:S(2)}, u32[]{:S(2)}) collective-permute-start(bf16[144,768]{1,0:T(8,128)(2,1)S(1)} %get-tuple-element.113), channel_id=1, source_target_pairs={{0,1},{1,2},{2,3},{3,0},{4,5},{5,6},{6,7},{7,4},{8,9},{9,10},{10,1... | collective-permute-start | bytes 663560 | tf_op jit(solution)/shard_map/ppermute | solution.py:24
  850.4 159.5 %collective-permute-start.64 = (bf16[144,768]{1,0:T(8,128)(2,1)}, bf16[144,768]{1,0:T(8,128)(2,1)}, u32[]{:S(2)}, u32[]{:S(2)}) collective-permute-start(bf16[144,768]{1,0:T(8,128)(2,1)} %get-tuple-element.110), channel_id=1, source_target_pairs={{0,3},{1,0},{2,1},{3,2},{4,7},{5,4},{6,5},{7,6},{8,11},{9,8},{10,9... | collective-permute-start | bytes 663560 | tf_op jit(solution)/shard_map/ppermute | solution.py:24
  857.7 152.8 %collective-permute-start.63 = (bf16[144,768]{1,0:T(8,128)(2,1)}, bf16[144,768]{1,0:T(8,128)(2,1)}, u32[]{:S(2)}, u32[]{:S(2)}) collective-permute-start(bf16[144,768]{1,0:T(8,128)(2,1)} %get-tuple-element.111), channel_id=1, source_target_pairs={{0,2},{1,3},{2,0},{3,1},{4,6},{5,7},{6,4},{7,5},{8,10},{9,11},{10,... | collective-permute-start | bytes 663560 | tf_op jit(solution)/shard_map/ppermute | solution.py:24
  859.6 23.7 %collective-permute-start.42 = (bf16[144,288]{1,0:T(8,128)(2,1)S(1)}, bf16[144,288]{1,0:T(8,128)(2,1)S(1)}, u32[]{:S(2)}, u32[]{:S(2)}) collective-permute-start(bf16[144,288]{1,0:T(8,128)(2,1)S(1)} %get-tuple-element.123), channel_id=1, source_target_pairs={{0,2},{1,3},{2,0},{3,1},{4,6},{5,7},{6,4},{7,5},{8,10},{9,11},{10,... | collective-permute-start | bytes 248840 | tf_op jit(solution)/shard_map/ppermute | solution.py:24
  862.1 21.3 %collective-permute-start.41 = (bf16[144,288]{1,0:T(8,128)(2,1)S(1)}, bf16[144,288]{1,0:T(8,128)(2,1)S(1)}, u32[]{:S(2)}, u32[]{:S(2)}) collective-permute-start(bf16[144,288]{1,0:T(8,128)(2,1)S(1)} %get-tuple-element.121), channel_id=1, source_target_pairs={{0,3},{1,0},{2,1},{3,2},{4,7},{5,4},{6,5},{7,6},{8,11},{9,8},{10,9... | collective-permute-start | bytes 248840 | tf_op jit(solution)/shard_map/ppermute | solution.py:24
  909.3 23.2 %collective-permute-start.55 = (bf16[144,480]{1,0:T(8,128)(2,1)}, bf16[144,480]{1,0:T(8,128)(2,1)}, u32[]{:S(2)}, u32[]{:S(2)}) collective-permute-start(bf16[144,480]{1,0:T(8,128)(2,1)} %get-tuple-element.139), channel_id=1, source_target_pairs={{0,3},{1,0},{2,1},{3,2},{4,7},{5,4},{6,5},{7,6},{8,11},{9,8},{10,9... | collective-permute-start | bytes 414728 | tf_op jit(solution)/shard_map/ppermute | solution.py:24
  910.7 21.8 %collective-permute-start.54 = (bf16[144,480]{1,0:T(8,128)(2,1)}, bf16[144,480]{1,0:T(8,128)(2,1)}, u32[]{:S(2)}, u32[]{:S(2)}) collective-permute-start(bf16[144,480]{1,0:T(8,128)(2,1)} %get-tuple-element.140), channel_id=1, source_target_pairs={{0,2},{1,3},{2,0},{3,1},{4,6},{5,7},{6,4},{7,5},{8,10},{9,11},{10,... | collective-permute-start | bytes 414728 | tf_op jit(solution)/shard_map/ppermute | solution.py:24
  958.5 18.8 %collective-permute-start.69 = (bf16[144,768]{1,0:T(8,128)(2,1)S(1)}, bf16[144,768]{1,0:T(8,128)(2,1)S(1)}, u32[]{:S(2)}, u32[]{:S(2)}) collective-permute-start(bf16[144,768]{1,0:T(8,128)(2,1)S(1)} %get-tuple-element.85), channel_id=1, source_target_pairs={{0,2},{1,3},{2,0},{3,1},{4,6},{5,7},{6,4},{7,5},{8,10},{9,11},{10,... | collective-permute-start | bytes 663560 | tf_op jit(solution)/shard_map/ppermute | solution.py:24
  967.7 27.4 %collective-permute-start.79 = (bf16[144,768]{1,0:T(8,128)(2,1)}, bf16[144,768]{1,0:T(8,128)(2,1)S(1)}, u32[]{:S(2)}, u32[]{:S(2)}) collective-permute-start(bf16[144,768]{1,0:T(8,128)(2,1)} %get-tuple-element.81), channel_id=1, source_target_pairs={{0,1},{1,2},{2,3},{3,0},{4,5},{5,6},{6,7},{7,4},{8,9},{9,10},{10,1... | collective-permute-start | bytes 663560 | tf_op jit(solution)/shard_map/ppermute | solution.py:24
  978.0 26.1 %collective-permute-start.77 = (bf16[144,768]{1,0:T(8,128)(2,1)S(1)}, bf16[144,768]{1,0:T(8,128)(2,1)S(1)}, u32[]{:S(2)}, u32[]{:S(2)}) collective-permute-start(bf16[144,768]{1,0:T(8,128)(2,1)S(1)} %get-tuple-element.83), channel_id=1, source_target_pairs={{0,3},{1,0},{2,1},{3,2},{4,7},{5,4},{6,5},{7,6},{8,11},{9,8},{10,9... | collective-permute-start | bytes 663560 | tf_op jit(solution)/shard_map/ppermute | solution.py:24
  995.1 18.6 %collective-permute-start.62 = (bf16[144,768]{1,0:T(8,128)(2,1)S(1)}, bf16[144,768]{1,0:T(8,128)(2,1)S(1)}, u32[]{:S(2)}, u32[]{:S(2)}) collective-permute-start(bf16[144,768]{1,0:T(8,128)(2,1)S(1)} %copy-done.56), channel_id=1, source_target_pairs={{0,1},{1,2},{2,3},{3,0},{4,5},{5,6},{6,7},{7,4},{8,9},{9,10},{10,1... | collective-permute-start | bytes 663560 | tf_op jit(solution)/shard_map/ppermute | solution.py:24
  995.7 23.1 %collective-permute-start.73 = (bf16[144,768]{1,0:T(8,128)(2,1)S(1)}, bf16[144,768]{1,0:T(8,128)(2,1)S(1)}, u32[]{:S(2)}, u32[]{:S(2)}) collective-permute-start(bf16[144,768]{1,0:T(8,128)(2,1)S(1)} %get-tuple-element.116), channel_id=1, source_target_pairs={{0,3},{1,0},{2,1},{3,2},{4,7},{5,4},{6,5},{7,6},{8,11},{9,8},{10,9... | collective-permute-start | bytes 663560 | tf_op jit(solution)/shard_map/ppermute | solution.py:24
  1004.0 27.0 %collective-permute-start.72 = (bf16[144,768]{1,0:T(8,128)(2,1)}, bf16[144,768]{1,0:T(8,128)(2,1)}, u32[]{:S(2)}, u32[]{:S(2)}) collective-permute-start(bf16[144,768]{1,0:T(8,128)(2,1)} %get-tuple-element.117), channel_id=1, source_target_pairs={{0,2},{1,3},{2,0},{3,1},{4,6},{5,7},{6,4},{7,5},{8,10},{9,11},{10,... | collective-permute-start | bytes 663560 | tf_op jit(solution)/shard_map/ppermute | solution.py:24
  1009.9 21.2 %collective-permute-start.71 = (bf16[144,768]{1,0:T(8,128)(2,1)S(1)}, bf16[144,768]{1,0:T(8,128)(2,1)}, u32[]{:S(2)}, u32[]{:S(2)}) collective-permute-start(bf16[144,768]{1,0:T(8,128)(2,1)S(1)} %get-tuple-element.115), channel_id=1, source_target_pairs={{0,1},{1,2},{2,3},{3,0},{4,5},{5,6},{6,7},{7,4},{8,9},{9,10},{10,1... | collective-permute-start | bytes 663560 | tf_op jit(solution)/shard_map/ppermute | solution.py:24
  1010.5 20.6 %collective-permute-start.82 = (bf16[144,768]{1,0:T(8,128)(2,1)}, bf16[144,768]{1,0:T(8,128)(2,1)}, u32[]{:S(2)}, u32[]{:S(2)}) collective-permute-start(bf16[144,768]{1,0:T(8,128)(2,1)} %get-tuple-element.119), channel_id=1, source_target_pairs={{0,3},{1,0},{2,1},{3,2},{4,7},{5,4},{6,5},{7,6},{8,11},{9,8},{10,9... | collective-permute-start | bytes 663560 | tf_op jit(solution)/shard_map/ppermute | solution.py:24
  1013.7 24.3 %collective-permute-start.81 = (bf16[144,768]{1,0:T(8,128)(2,1)}, bf16[144,768]{1,0:T(8,128)(2,1)}, u32[]{:S(2)}, u32[]{:S(2)}) collective-permute-start(bf16[144,768]{1,0:T(8,128)(2,1)} %get-tuple-element.120), channel_id=1, source_target_pairs={{0,2},{1,3},{2,0},{3,1},{4,6},{5,7},{6,4},{7,5},{8,10},{9,11},{10,... | collective-permute-start | bytes 663560 | tf_op jit(solution)/shard_map/ppermute | solution.py:24
  1019.5 18.5 %collective-permute-start.80 = (bf16[144,768]{1,0:T(8,128)(2,1)}, bf16[144,768]{1,0:T(8,128)(2,1)}, u32[]{:S(2)}, u32[]{:S(2)}) collective-permute-start(bf16[144,768]{1,0:T(8,128)(2,1)} %get-tuple-element.118), channel_id=1, source_target_pairs={{0,1},{1,2},{2,3},{3,0},{4,5},{5,6},{6,7},{7,4},{8,9},{9,10},{10,1... | collective-permute-start | bytes 663560 | tf_op jit(solution)/shard_map/ppermute | solution.py:24
  1021.1 259.7 %all-gather.21.cloned.1.call-start = ((), (), s32[]{:S(2)}) async-start(), calls=%async_computation.17 | async-start | bytes 5971968 | tf_op jit(solution)/shard_map/all_gather | solution.py:430
  1043.6 32.0 %collective-permute-start.84 = (bf16[144,768]{1,0:T(8,128)(2,1)S(1)}, bf16[144,768]{1,0:T(8,128)(2,1)S(1)}, u32[]{:S(2)}, u32[]{:S(2)}) collective-permute-start(bf16[144,768]{1,0:T(8,128)(2,1)S(1)} %get-tuple-element.59), channel_id=1, source_target_pairs={{0,2},{1,3},{2,0},{3,1},{4,6},{5,7},{6,4},{7,5},{8,10},{9,11},{10,... | collective-permute-start | bytes 663560 | tf_op jit(solution)/shard_map/ppermute | solution.py:24
  1045.7 36.6 %collective-permute-start.85 = (bf16[144,768]{1,0:T(8,128)(2,1)S(1)}, bf16[144,768]{1,0:T(8,128)(2,1)S(1)}, u32[]{:S(2)}, u32[]{:S(2)}) collective-permute-start(bf16[144,768]{1,0:T(8,128)(2,1)S(1)} %get-tuple-element.59), channel_id=1, source_target_pairs={{0,1},{1,2},{2,3},{3,0},{4,5},{5,6},{6,7},{7,4},{8,9},{9,10},{10,1... | collective-permute-start | bytes 663560 | tf_op jit(solution)/shard_map/ppermute | solution.py:24
  1047.7 36.0 %collective-permute-start.76 = (bf16[144,768]{1,0:T(8,128)(2,1)S(1)}, bf16[144,768]{1,0:T(8,128)(2,1)S(1)}, u32[]{:S(2)}, u32[]{:S(2)}) collective-permute-start(bf16[144,768]{1,0:T(8,128)(2,1)S(1)} %get-tuple-element.60), channel_id=1, source_target_pairs={{0,1},{1,2},{2,3},{3,0},{4,5},{5,6},{6,7},{7,4},{8,9},{9,10},{10,1... | collective-permute-start | bytes 663560 | tf_op jit(solution)/shard_map/ppermute | solution.py:24
  1047.8 38.2 %collective-permute-start.75 = (bf16[144,768]{1,0:T(8,128)(2,1)S(1)}, bf16[144,768]{1,0:T(8,128)(2,1)S(1)}, u32[]{:S(2)}, u32[]{:S(2)}) collective-permute-start(bf16[144,768]{1,0:T(8,128)(2,1)S(1)} %get-tuple-element.60), channel_id=1, source_target_pairs={{0,2},{1,3},{2,0},{3,1},{4,6},{5,7},{6,4},{7,5},{8,10},{9,11},{10,... | collective-permute-start | bytes 663560 | tf_op jit(solution)/shard_map/ppermute | solution.py:24
  1050.1 35.8 %collective-permute-start.74 = (bf16[144,768]{1,0:T(8,128)(2,1)S(1)}, bf16[144,768]{1,0:T(8,128)(2,1)S(1)}, u32[]{:S(2)}, u32[]{:S(2)}) collective-permute-start(bf16[144,768]{1,0:T(8,128)(2,1)S(1)} %get-tuple-element.60), channel_id=1, source_target_pairs={{0,3},{1,0},{2,1},{3,2},{4,7},{5,4},{6,5},{7,6},{8,11},{9,8},{10,9... | collective-permute-start | bytes 663560 | tf_op jit(solution)/shard_map/ppermute | solution.py:24
  1082.4 19.3 %collective-permute-start.66 = (bf16[144,768]{1,0:T(8,128)(2,1)S(1)}, bf16[144,768]{1,0:T(8,128)(2,1)S(1)}, u32[]{:S(2)}, u32[]{:S(2)}) collective-permute-start(bf16[144,768]{1,0:T(8,128)(2,1)S(1)} %get-tuple-element.58), channel_id=1, source_target_pairs={{0,2},{1,3},{2,0},{3,1},{4,6},{5,7},{6,4},{7,5},{8,10},{9,11},{10,... | collective-permute-start | bytes 663560 | tf_op jit(solution)/shard_map/ppermute | solution.py:24
  1126.1 53.9 %all-to-all-start.1 = ((bf16[256,8,144]{0,2,1:T(8,128)(2,1)}), bf16[256,8,144]{0,2,1:T(8,128)(2,1)S(1)}, u32[]{:S(2)}, u32[]{:S(2)}) async-start(bf16[256,8,144]{0,2,1:T(8,128)(2,1)} %bitcast.96), calls=%async_computation.2 | async-start | bytes 1179648 | tf_op jit(solution)/shard_map/all_to_all | solution.py:383
  1180.0 20.6 %collective-permute-start.40 = (bf16[2048,144]{0,1:T(8,128)(2,1)S(1)}, bf16[2048,144]{0,1:T(8,128)(2,1)S(1)}, u32[]{:S(2)}, u32[]{:S(2)}) collective-permute-start(bf16[2048,144]{0,1:T(8,128)(2,1)S(1)} %bitcast.499), channel_id=1, source_target_pairs={{0,3},{1,0},{2,1},{3,2},{4,7},{5,4},{6,5},{7,6},{8,11},{9,8},{10,9... | collective-permute-start | bytes 1769480 | tf_op jit(solution)/shard_map/ppermute | solution.py:24
  1181.6 51.4 %collective-permute-start.39 = (bf16[2048,144]{0,1:T(8,128)(2,1)S(1)}, bf16[2048,144]{0,1:T(8,128)(2,1)S(1)}, u32[]{:S(2)}, u32[]{:S(2)}) collective-permute-start(bf16[2048,144]{0,1:T(8,128)(2,1)S(1)} %bitcast.500), channel_id=1, source_target_pairs={{0,2},{1,3},{2,0},{3,1},{4,6},{5,7},{6,4},{7,5},{8,10},{9,11},{10,... | collective-permute-start | bytes 1769480 | tf_op jit(solution)/shard_map/ppermute | solution.py:24
  1182.8 65.9 %collective-permute-start.38 = (bf16[2048,144]{0,1:T(8,128)(2,1)S(1)}, bf16[2048,144]{0,1:T(8,128)(2,1)S(1)}, u32[]{:S(2)}, u32[]{:S(2)}) collective-permute-start(bf16[2048,144]{0,1:T(8,128)(2,1)S(1)} %bitcast.501), channel_id=1, source_target_pairs={{0,1},{1,2},{2,3},{3,0},{4,5},{5,6},{6,7},{7,4},{8,9},{9,10},{10,1... | collective-permute-start | bytes 1769480 | tf_op jit(solution)/shard_map/ppermute | solution.py:24
  (151 other events, 2195.4 us)
Sparse Core Ops, SparseCore 0:
  35.5 50.3 all-gather.10
  94.0 112.7 all-gather.12
  303.9 37.5 all-reduce.6
  343.2 35.0 all-gather.14
  482.5 38.8 reduce-scatter.4
  523.8 35.7 all-reduce.8
  561.7 74.7 all-gather.16
  644.9 65.4 reduce-scatter.8
  739.4 85.5 reduce-scatter.6
  828.8 104.6 reduce-scatter.10
  1021.2 27.2 all-gather.18
  1120.3 49.7 all-gather.20

commit v2 on v1

v2 whole, which is shorter than its diff:
```python
import functools

import jax
import jax.numpy as jnp
from jax import lax
from jax.experimental import pallas as pl
from jax.experimental.pallas import tpu as pltpu
from jax.sharding import PartitionSpec as P

Q_HEADS = 18
KV_HEADS = 6
HEAD = 64
LEN = 1024
PICK = 128


NORM_EPSILON = 1e-05
ADAM_EPSILON = 1e-08
MOMENT_BETA = 0.5
SOAP_RATE = 0.05
ADAM_RATE = 0.01
WEIGHT_DECAY = 0.1
MASK_VALUE = -1e30
MESH = pl.DeviceIdType.MESH
VMEM_LIMIT = 58 * 2**20
VOCAB_TILE = 1024
LOOK_STEP = 32
SMALL_BLOCK = 384


def greet(peers):
    barrier = pltpu.get_barrier_semaphore()
    for peer in peers:
        pl.semaphore_signal(barrier, inc=1, device_id=peer, device_id_type=MESH)
    pl.semaphore_wait(barrier, len(peers))


def push(source, target, sems, slot, peer):
    copy = pltpu.make_async_remote_copy(
        src_ref=source,
        dst_ref=target,
        send_sem=sems[0].at[slot],
        recv_sem=sems[1].at[slot],
        device_id=peer,
        device_id_type=MESH,
    )
    copy.start()
    return copy


def row_peer(row, col, rows, k):
    half = rows // 2
    if k < half:
        return ((row + 2 * k) % rows, col)
    return ((row // 2 * 2 + 2 * (k - half)) % rows + 1 - row % 2, col)


def share_kernel(rows, cols, x_ref, out_ref, col_send, col_recv, row_send, row_recv):
    row, col = lax.axis_index("row"), lax.axis_index("col")
    col_peers = [(row, (col + k) % cols) for k in range(1, cols)]
    row_peers = [((row + k) % rows, col) for k in range(1, rows)]
    greet(col_peers + row_peers)
    out_ref[row, col] = x_ref[...]
    copies = [
        push(out_ref.at[row, col], out_ref.at[row, col], (col_send, col_recv), k, peer)
        for k, peer in enumerate(col_peers)
    ]
    for copy in copies:
        copy.wait()
    copies = [
        push(out_ref.at[row], out_ref.at[row], (row_send, row_recv), k, peer)
        for k, peer in enumerate(row_peers)
    ]
    for copy in copies:
        copy.wait()


def share(value, collective_id):
    rows, cols = lax.axis_size("row"), lax.axis_size("col")
    return pl.pallas_call(
        functools.partial(share_kernel, rows, cols),
        out_shape=jax.ShapeDtypeStruct((rows, cols, *value.shape), value.dtype),
        in_specs=[pl.BlockSpec(memory_space=pltpu.VMEM)],
        out_specs=pl.BlockSpec(memory_space=pltpu.VMEM),
        scratch_shapes=[
            pltpu.SemaphoreType.DMA((cols - 1,)),
            pltpu.SemaphoreType.DMA((cols - 1,)),
            pltpu.SemaphoreType.DMA((rows - 1,)),
            pltpu.SemaphoreType.DMA((rows - 1,)),
        ],
        compiler_params=pltpu.CompilerParams(
            collective_id=collective_id, has_side_effects=True, vmem_limit_bytes=VMEM_LIMIT
        ),
    )(value)


def spread_kernel(
    rows, cols, x_ref, out_ref, landed, part_send, part_recv, col_send, col_recv,
    row_send, row_recv, core_send, core_recv,
):
    row, col = lax.axis_index("row"), lax.axis_index("col")
    half = rows // 2
    other = row // 2 * 2 + 1 - row % 2
    col_peers = [(row, (col + k) % cols) for k in range(1, cols)]
    row_peers = [((row + 2 * k) % rows, col) for k in range(1, half)]
    greet(col_peers + row_peers + [(other, col)])
    copies = [
        push(x_ref.at[(col + k + 1) % cols], landed.at[k], (part_send, part_recv), k, peer)
        for k, peer in enumerate(col_peers)
    ]
    for copy in copies:
        copy.wait()
    total = x_ref[col].astype(jnp.float32)
    for k in range(cols - 1):
        total = total + landed[k].astype(jnp.float32)
    out_ref[row, col] = total.astype(out_ref.dtype)
    copies = [
        push(out_ref.at[row, col], out_ref.at[row, col], (col_send, col_recv), k, peer)
        for k, peer in enumerate(col_peers)
    ]
    for copy in copies:
        copy.wait()
    across = [
        push(out_ref.at[row], out_ref.at[row], (row_send, row_recv), k, peer)
        for k, peer in enumerate(row_peers)
    ]
    between = [push(out_ref.at[row], out_ref.at[row], (core_send, core_recv), 0, (other, col))]
    for k in range(1, half):
        across[k - 1].wait_recv()
        source = (row + rows - 2 * k) % rows
        between.append(
            push(out_ref.at[source], out_ref.at[source], (core_send, core_recv), k, (other, col))
        )
    for copy in across:
        copy.wait_send()
    for copy in between:
        copy.wait()


def spread(value, collective_id):
    rows, cols = lax.axis_size("row"), lax.axis_size("col")
    count, width = value.shape
    part = count // cols
    dma = pltpu.SemaphoreType.DMA
    out = pl.pallas_call(
        functools.partial(spread_kernel, rows, cols),
        out_shape=jax.ShapeDtypeStruct((rows, cols, part, width), value.dtype),
        in_specs=[pl.BlockSpec(memory_space=pltpu.VMEM)],
        out_specs=pl.BlockSpec(memory_space=pltpu.VMEM),
        scratch_shapes=[pltpu.VMEM((cols - 1, part, width), value.dtype)]
        + [dma((cols - 1,))] * 4
        + [dma((rows // 2 - 1,))] * 2
        + [dma((rows // 2,))] * 2,
        compiler_params=pltpu.CompilerParams(
            collective_id=collective_id, has_side_effects=True, vmem_limit_bytes=VMEM_LIMIT
        ),
    )(value.reshape(cols, part, width))
    return out.reshape(rows * count, width)


def fold_kernel(
    rows, cols, x_ref, out_ref, from_core, to_row, from_row, mine, landed, core_send, core_recv,
    row_send, row_recv, part_send, part_recv, col_send, col_recv,
):
    row, col = lax.axis_index("row"), lax.axis_index("col")
    half = rows // 2
    core = row % 2
    other = row // 2 * 2 + 1 - core
    col_peers = [(row, (col + k) % cols) for k in range(1, cols)]
    row_peers = [((row + 2 * k) % rows, col) for k in range(1, half)]
    greet(col_peers + row_peers + [(other, col)])
    between = [
        push(
            x_ref.at[(row + 2 * k) % rows // 2 * 2 + 1 - core],
            from_core.at[k],
            (core_send, core_recv),
            k,
            (other, col),
        )
        for k in [*range(1, half), 0]
    ]
    across = []
    for k in range(1, half):
        between[k - 1].wait_recv()
        to_row[k - 1] = (
            x_ref[(row + 2 * k) % rows].astype(jnp.float32) + from_core[k].astype(jnp.float32)
        ).astype(to_row.dtype)
        across.append(
            push(to_row.at[k - 1], from_row.at[k - 1], (row_send, row_recv), k - 1, row_peers[k - 1])
        )
    between[half - 1].wait_recv()
    total = x_ref[row].astype(jnp.float32) + from_core[0].astype(jnp.float32)
    for k in range(half - 1):
        across[k].wait_recv()
        total = total + from_row[k].astype(jnp.float32)
    mine[...] = total.astype(mine.dtype)
    copies = [
        push(mine.at[(col + k + 1) % cols], landed.at[k], (part_send, part_recv), k, peer)
        for k, peer in enumerate(col_peers)
    ]
    for copy in copies:
        copy.wait()
    part = mine[col].astype(jnp.float32)
    for k in range(cols - 1):
        part = part + landed[k].astype(jnp.float32)
    out_ref[col] = part.astype(out_ref.dtype)
    copies = [
        push(out_ref.at[col], out_ref.at[col], (col_send, col_recv), k, peer)
        for k, peer in enumerate(col_peers)
    ]
    for copy in copies:
        copy.wait()
    for copy in between + across:
        copy.wait_send()


def fold(value, collective_id):
    rows, cols = lax.axis_size("row"), lax.axis_size("col")
    count, width = value.shape[0] // rows, value.shape[1]
    part = count // cols
    half = rows // 2
    dma = pltpu.SemaphoreType.DMA
    block = (cols, part, width)
    out = pl.pallas_call(
        functools.partial(fold_kernel, rows, cols),
        out_shape=jax.ShapeDtypeStruct(block, value.dtype),
        in_specs=[pl.BlockSpec(memory_space=pltpu.VMEM)],
        out_specs=pl.BlockSpec(memory_space=pltpu.VMEM),
        scratch_shapes=[
            pltpu.VMEM((half, *block), value.dtype),
            pltpu.VMEM((half - 1, *block), value.dtype),
            pltpu.VMEM((half - 1, *block), value.dtype),
            pltpu.VMEM(block, value.dtype),
            pltpu.VMEM((cols - 1, part, width), value.dtype),
        ]
        + [dma((half,))] * 2
        + [dma((half - 1,))] * 2
        + [dma((cols - 1,))] * 4,
        compiler_params=pltpu.CompilerParams(
            collective_id=collective_id, has_side_effects=True, vmem_limit_bytes=VMEM_LIMIT
        ),
    )(value.reshape(rows, *block))
    return out.reshape(count, width)


def flipped(index, entry):
    bit = 1
    while bit <= entry:
        if entry & bit:
            index = index + bit * (1 - 2 * (index // bit % 2))
        bit *= 2
    return index


class Matrix:
    def __init__(self, place, grad, basis, refs, adds_weight):
        self.row, self.col, self.rows, self.cols = place
        self.grad, self.basis = grad, basis
        (
            self.mean, self.square, self.weight, self.left,
            self.next, self.moment, self.scale,
            self.sums, self.work, self.inbox, self.steps, self.whole, self.sems, self.row_sems, self.core_sems,
        ) = refs
        self.adds_weight = adds_weight
        self.levels = [1 << k for k in range(self.cols.bit_length() - 1)]
        self.slot = 0
        self.started = []
        self.pending = []

    def send(self, source, target, bit):
        peer = (self.row, flipped(self.col, bit))
        slot = self.slot
        self.slot += 1
        copy = push(source, target, (self.sems.at[0], self.sems.at[1]), slot, peer)
        self.started.append(copy)
        return copy

    def arrive(self):
        for copy in self.pending:
            copy.wait_recv()
        self.pending = []

    def halving(self, phase):
        entries = list(range(self.cols))
        place = phase * (self.cols - 1)
        first = True
        for bit in self.levels:
            gone = [e for e in entries if e & bit]
            entries = [e for e in entries if not e & bit]
            for k, e in enumerate(gone):
                if first and phase == 0:
                    source = self.grad(e)
                elif first:
                    self.multiply(e)
                    source = self.work.at[e]
                else:
                    source = self.sums.at[e // 2] if phase == 0 else self.work.at[e]
                self.pending.append(self.send(source, self.inbox.at[place + k], bit))
            if first and phase == 1:
                for e in entries:
                    self.multiply(e)
            yield
            self.arrive()
            for k, e in enumerate(gone):
                mine = e - bit
                if first and phase == 0:
                    held = self.grad(mine)[...]
                else:
                    held = self.sums[mine // 2] if phase == 0 else self.work[mine]
                self.total = held.astype(jnp.float32) + self.inbox[place + k].astype(jnp.float32)
                if phase == 0:
                    self.sums[mine // 2] = self.total.astype(self.sums.dtype)
                elif bit != self.levels[-1]:
                    self.work[mine] = self.total.astype(self.work.dtype)
            place += len(gone)
            first = False

    def multiply(self, e):
        self.work[e] = jnp.dot(
            self.sums[0],
            self.basis(e),
            preferred_element_type=jnp.float32,
        ).astype(self.work.dtype)

    def go(self):
        yield from self.halving(0)
        yield from self.halving(1)
        rotated = self.total
        moment = MOMENT_BETA * self.mean[...] + (1.0 - MOMENT_BETA) * rotated
        scale = MOMENT_BETA * self.square[...] + (1.0 - MOMENT_BETA) * rotated * rotated
        self.moment[...] = moment
        self.scale[...] = scale
        self.steps[0] = (moment / (jnp.sqrt(scale) + ADAM_EPSILON)).astype(self.steps.dtype)
        arriving = [(0, None)]
        back = None
        while arriving:
            e, arrived = arriving.pop(0)
            if arrived is not None:
                arrived.wait_recv()
            for bit in reversed(self.levels):
                if e % (2 * bit) == 0:
                    copy = self.send(self.steps.at[e], self.steps.at[e + bit], bit)
                    arriving.append((e + bit, copy))
            term = lax.dot_general(
                self.steps[e],
                self.basis(e),
                (((1,), (1,)), ((), ())),
                preferred_element_type=jnp.float32,
            )
            back = term if back is None else back + term
            yield
        self.whole[self.row] = back.astype(self.whole.dtype)
        half = self.rows // 2
        other = (self.row // 2 * 2 + 1 - self.row % 2, self.col)
        own = self.whole.at[self.row]
        across = [
            push(own, own, (self.row_sems.at[0], self.row_sems.at[1]), k - 1, peer)
            for k, peer in enumerate(same_core(self.row, self.col, self.rows), 1)
        ]
        core_sems = (self.core_sems.at[0], self.core_sems.at[1])
        between = [push(own, own, core_sems, 0, other)]
        self.started += across + between
        yield
        for k in range(1, half):
            across[k - 1].wait_recv()
            block = self.whole.at[(self.row + self.rows - 2 * k) % self.rows]
            copy = push(block, block, core_sems, k, other)
            between.append(copy)
            self.started.append(copy)
        yield
        for copy in between:
            copy.wait_recv()
        depth, count = self.weight.shape
        everything = self.whole[...].reshape(self.rows * depth, count)
        update = jnp.dot(self.left[...], everything, preferred_element_type=jnp.float32)
        weight = self.weight[...]
        change = -(SOAP_RATE * (update + WEIGHT_DECAY * weight))
        self.next[...] = weight + change if self.adds_weight else change
        for copy in self.started:
            copy.wait_send()


def same_core(row, col, rows):
    return [((row + 2 * k) % rows, col) for k in range(1, rows // 2)]


def soap_kernel(rows, cols, adds, streamed, *refs):
    row, col = lax.axis_index("row"), lax.axis_index("col")
    peers = [(row, flipped(col, 1 << k)) for k in range(cols.bit_length() - 1)]
    greet(peers + same_core(row, col, rows) + [(row // 2 * 2 + 1 - row % 2, col)])
    count = len(adds)
    shared = 1 if streamed else count
    grads, bases, refs = refs[:shared], refs[shared : 2 * shared], refs[2 * shared :]
    inputs, refs = refs[: 4 * count], refs[4 * count :]
    outputs, refs = refs[: 3 * count], refs[3 * count :]
    scratch, refs = refs[: 8 * count], refs[8 * count :]
    running = []
    loads = []
    for m, add in enumerate(adds):
        grad, basis = grads[m % shared], bases[m % shared]
        others = inputs[4 * m : 4 * m + 4]
        width = others[0].shape[1]
        if streamed:
            held, stage, load_sems = refs

            def grad_of(e, grad=grad, m=m, width=width):
                at = pl.multiple_of((streamed.index(m) * cols + flipped(col, e)) * width, width)
                return grad.at[:, pl.ds(at, width)]

            def basis_of(e, held=held, m=m):
                return held[m, e]

            for e in [*range(1, cols, 2), *range(2, cols, 2), 0]:
                at = pl.multiple_of(flipped(col, e) * width, width)
                for part in range(2):
                    lines = pl.ds(part * (width // 2), width // 2)
                    copy = pltpu.make_async_copy(
                        basis.at[m, lines, pl.ds(at, width)], stage.at[part], load_sems.at[part]
                    )
                    loads.append((copy, part, m, e))
        else:

            def grad_of(e, grad=grad):
                return grad.at[flipped(col, e)]

            def basis_of(e, basis=basis):
                return basis[flipped(col, e)]

        refs_of = (*others, *outputs[3 * m : 3 * m + 3], *scratch[8 * m : 8 * m + 8])
        running.append(Matrix((row, col, rows, cols), grad_of, basis_of, refs_of, add).go())
    if streamed:
        running = [running[m] for m in streamed]
        loads = [load for m in streamed for load in loads if load[2] == m]
        for copy, *unused in loads[:2]:
            copy.start()
    for m in running:
        next(m)
    for k, (copy, slot, m, e) in enumerate(loads):
        copy.wait()
        lines = pl.ds(slot * stage.shape[1], stage.shape[1])
        held[m, e, lines] = stage[slot].astype(held.dtype)
        if k + 2 < len(loads):
            loads[k + 2][0].start()
    while running:
        running = [m for m in running if next(m, "done") != "done"]


def soap(grads, bases, matrices, adds, streamed, collective_id):
    rows, cols = lax.axis_size("row"), lax.axis_size("col")
    dma = pltpu.SemaphoreType.DMA
    vmem = pl.BlockSpec(memory_space=pltpu.VMEM)
    outs, scratch = [], []
    for mean, square, weight, left in matrices:
        outs += [jax.ShapeDtypeStruct(weight.shape, jnp.float32)] * 3
        block = weight.shape
        scratch += [
            pltpu.VMEM((cols // 2, *block), left.dtype),
            pltpu.VMEM((cols, *block), left.dtype),
            pltpu.VMEM((2 * (cols - 1), *block), left.dtype),
            pltpu.VMEM((cols, *block), left.dtype),
            pltpu.VMEM((rows, *block), left.dtype),
            dma((2, 3 * (cols - 1))),
            dma((2, rows // 2 - 1)),
            dma((2, rows // 2)),
        ]
    if streamed:
        width = matrices[0][2].shape[1]
        scratch += [
            pltpu.VMEM((len(matrices), cols, width, width), jnp.bfloat16),
            pltpu.VMEM((2, width // 2, width), jnp.float32),
            dma((2,)),
        ]
    got = pl.pallas_call(
        functools.partial(soap_kernel, rows, cols, adds, streamed),
        out_shape=outs,
        in_specs=[vmem] * len(grads)
        + [pl.BlockSpec(memory_space=pl.ANY) if streamed else vmem] * len(bases)
        + [vmem] * (4 * len(matrices)),
        out_specs=[vmem] * len(outs),
        scratch_shapes=scratch,
        compiler_params=pltpu.CompilerParams(
            collective_id=collective_id, has_side_effects=True, vmem_limit_bytes=VMEM_LIMIT
        ),
    )(*grads, *bases, *[part for matrix in matrices for part in matrix])
    return [got[k * 3 : k * 3 + 3] for k in range(len(matrices))]


def outer_kernel(values_ref, left_ref, other_ref, *refs):
    out_ref, turned = refs[-2:]

    @pl.when(pl.program_id(0) == 0)
    def _():
        turned[...] = jnp.dot(
            values_ref[...], left_ref[...], preferred_element_type=jnp.float32
        ).astype(turned.dtype)

    out_ref[...] = lax.dot_general(
        turned[...], other_ref[...], (((0,), (0,)), ((), ())), preferred_element_type=jnp.float32
    ).astype(out_ref.dtype)


def outer(values, left_full, basis, other, block, total, at, buffer):
    tokens, width = values.shape
    specs = [
        pl.BlockSpec((tokens, width), lambda j: (0, 0)),
        pl.BlockSpec((width, width), lambda j: (0, basis)),
        pl.BlockSpec((tokens, block), lambda j: (0, j)),
    ]
    operands = [values, left_full, other]
    aliases = {}
    if buffer is not None:
        specs.append(pl.BlockSpec(memory_space=pl.ANY))
        operands.append(buffer)
        aliases = {3: 0}
    return pl.pallas_call(
        outer_kernel,
        grid=(other.shape[1] // block,),
        out_shape=jax.ShapeDtypeStruct((width, total), values.dtype),
        in_specs=specs,
        out_specs=pl.BlockSpec((width, block), lambda j: (0, at + j)),
        scratch_shapes=[pltpu.VMEM((tokens, width), values.dtype)],
        input_output_aliases=aliases,
        compiler_params=pltpu.CompilerParams(vmem_limit_bytes=VMEM_LIMIT),
        cost_estimate=pl.CostEstimate(
            flops=2 * tokens * width * (width + other.shape[1]),
            bytes_accessed=2 * width * (width + other.shape[1] + tokens),
            transcendentals=0,
        ),
    )(*operands)


def one_hot_tile(ids, first, count):
    columns = lax.broadcasted_iota(jnp.int32, (ids.shape[0], count), 1)
    return jnp.where(ids - first == columns, 1.0, 0.0).astype(jnp.bfloat16)


def lookup_kernel(rows, cols, ids_ref, table_ref, out_ref, table, taken, found, inbox, sems, row_sems):
    row, col = lax.axis_index("row"), lax.axis_index("col")
    levels = [1 << k for k in range(cols.bit_length() - 1)]
    row_peers = [((row + k) % rows, col) for k in range(1, rows)]
    greet([(row, flipped(col, bit)) for bit in levels] + row_peers)
    features, tokens = out_ref.shape[1:]
    planes = [(k, min(128, features - 128 * k)) for k in range(table.shape[1])]

    def turn(v, carry):
        first = pl.multiple_of(v * 128, 128)
        entries = table_ref[:, pl.ds(first, 128)].astype(jnp.float32).T
        for k, lanes in planes:
            table[pl.ds(first, 128), k, pl.ds(0, lanes)] = entries[:, 128 * k : 128 * k + lanes]
        return carry

    lax.fori_loop(0, table_ref.shape[1] // 128, turn, 0)

    def look(e):
        source = flipped(col, e) * rows

        def block(k, carry):
            start = (source + k) * tokens

            def some(j, carry):
                for u in range(LOOK_STEP):
                    at = j * LOOK_STEP + u
                    taken[at] = table[ids_ref[start + at]]
                return carry

            lax.fori_loop(0, tokens // LOOK_STEP, some, 0)
            for p, lanes in planes:
                found[e, k, pl.ds(128 * p, lanes), :] = taken[:, p, :].T[:lanes].astype(found.dtype)
            return carry

        lax.fori_loop(0, rows, block, 0)

    entries = list(range(cols))
    started, slot = [], 0
    for bit in levels:
        gone = [e for e in entries if e & bit]
        entries = [e for e in entries if not e & bit]
        copies = []
        for e in gone:
            if bit == 1:
                look(e)
            peer = (row, flipped(col, bit))
            copies.append(push(found.at[e], inbox.at[slot], (sems.at[0], sems.at[1]), slot, peer))
            slot += 1
        if bit == 1:
            for e in reversed(entries):
                look(e)
        for k, e in enumerate(gone):
            copies[k].wait_recv()
            at = slot - len(gone) + k
            found[e - bit] = found[e - bit] + inbox[at]
        started += copies
    out_ref[row] = found[0, row]
    copies = [
        push(found.at[0, peer[0]], out_ref.at[row], (row_sems.at[0], row_sems.at[1]), k, peer)
        for k, peer in enumerate(row_peers)
    ]
    for copy in copies:
        copy.wait_recv()
    for copy in copies + started:
        copy.wait_send()


def lookup(ids, table, tokens, collective_id):
    rows, cols = lax.axis_size("row"), lax.axis_size("col")
    features, count = table.shape
    planes = -(-features // 128)
    dma = pltpu.SemaphoreType.DMA
    vmem = pl.BlockSpec(memory_space=pltpu.VMEM)
    block = (rows, features, tokens)
    return pl.pallas_call(
        functools.partial(lookup_kernel, rows, cols),
        out_shape=jax.ShapeDtypeStruct(block, table.dtype),
        in_specs=[pl.BlockSpec(memory_space=pltpu.SMEM), vmem],
        out_specs=vmem,
        scratch_shapes=[
            pltpu.VMEM((count, planes, 128), jnp.float32),
            pltpu.VMEM((tokens, planes, 128), jnp.float32),
            pltpu.VMEM((cols, *block), table.dtype),
            pltpu.VMEM((cols - 1, *block), table.dtype),
            dma((2, cols - 1)),
            dma((2, rows - 1)),
        ],
        compiler_params=pltpu.CompilerParams(
            collective_id=collective_id, has_side_effects=True, vmem_limit_bytes=VMEM_LIMIT
        ),
    )(ids, table)


def scatter_kernel(
    rows, cols, ids_ref, grad_ref, base_ref, out_ref, held, sems, row_sems
):
    row, col = lax.axis_index("row"), lax.axis_index("col")
    levels = [1 << k for k in range(cols.bit_length() - 1)]
    row_peers = [((row + k) % rows, col) for k in range(1, rows)]
    greet([(row, flipped(col, bit)) for bit in levels] + row_peers)
    held[0, row] = grad_ref[row]
    copies = [
        push(grad_ref.at[peer[0]], held.at[0, row], (row_sems.at[0], row_sems.at[1]), k, peer)
        for k, peer in enumerate(row_peers)
    ]
    count = out_ref.shape[1]

    def place(e, first_time):
        source = flipped(col, e)

        def block(v, carry):
            first = pl.multiple_of(v * VOCAB_TILE, VOCAB_TILE)
            total = base_ref[:, pl.ds(first, VOCAB_TILE)] if first_time else out_ref[:, pl.ds(first, VOCAB_TILE)]
            for k in range(rows):
                total = total + lax.dot_general(
                    held[e, k],
                    one_hot_tile(ids_ref[source, k], first, VOCAB_TILE),
                    (((1,), (0,)), ((), ())),
                    preferred_element_type=jnp.float32,
                )
            out_ref[:, pl.ds(first, VOCAB_TILE)] = total
            return carry

        lax.fori_loop(0, count // VOCAB_TILE, block, 0)

    for copy in copies:
        copy.wait_recv()
    started = list(copies)
    arriving, slot = [(0, None)], 0
    while arriving:
        e, arrived = arriving.pop(0)
        if arrived is not None:
            arrived.wait_recv()
        for bit in reversed(levels):
            if e % (2 * bit) == 0:
                copy = push(
                    held.at[e], held.at[e + bit], (sems.at[0], sems.at[1]), slot,
                    (row, flipped(col, bit)),
                )
                slot += 1
                started.append(copy)
                arriving.append((e + bit, copy))
        place(e, e == 0)
    for copy in started:
        copy.wait_send()


def scatter(ids, grad, base, collective_id):
    rows, cols = lax.axis_size("row"), lax.axis_size("col")
    dma = pltpu.SemaphoreType.DMA
    vmem = pl.BlockSpec(memory_space=pltpu.VMEM)
    return pl.pallas_call(
        functools.partial(scatter_kernel, rows, cols),
        out_shape=jax.ShapeDtypeStruct(base.shape, jnp.float32),
        in_specs=[vmem] * 3,
        out_specs=vmem,
        scratch_shapes=[
            pltpu.VMEM((cols, *grad.shape), grad.dtype),
            dma((2, cols - 1)),
            dma((2, rows - 1)),
        ],
        compiler_params=pltpu.CompilerParams(
            collective_id=collective_id, has_side_effects=True, vmem_limit_bytes=VMEM_LIMIT
        ),
    )(ids, grad, base)


def send(value, axis, shift):
    count = lax.axis_size(axis)
    return lax.ppermute(value, axis, [(k, (k + shift) % count) for k in range(count)])


def collect(value, axis):
    return [value] + [send(value, axis, k) for k in range(1, lax.axis_size(axis))]


def deliver(pieces, axis, sign):
    return [pieces[0]] + [send(pieces[k], axis, sign * k) for k in range(1, len(pieces))]


def summed(pieces):
    total = pieces[0].astype(jnp.float32)
    for piece in pieces[1:]:
        total = total + piece.astype(jnp.float32)
    return total


def to_absolute(pieces, index):
    count = len(pieces)
    order = [pieces[0]] + [pieces[count - k] for k in range(1, count)]
    return jnp.roll(jnp.stack(order), index, axis=0)


def pick_block(values, index, axis):
    return lax.dynamic_index_in_dim(values, index, axis, keepdims=False)


def rms_norm(values, gain_vec):
    return (
        values
        * lax.rsqrt(jnp.mean(values * values, axis=-1, keepdims=True) + NORM_EPSILON)
        * gain_vec
    )


def rotary(values, positions):
    half_width = values.shape[-1] // 2
    frequency = jnp.power(10000.0, -jnp.arange(half_width, dtype=jnp.float32) / half_width)
    angles = positions[:, None].astype(jnp.float32) * frequency[None, :]
    cosine = jnp.cos(angles)[:, None, :]
    sine_part = jnp.sin(angles)[:, None, :]
    first_half = values[..., :half_width]
    second_half = values[..., half_width:]
    return jnp.concatenate(
        [
            first_half * cosine - second_half * sine_part,
            second_half * cosine + first_half * sine_part,
        ],
        axis=-1,
    )


def swiglu(gate_part, upward):
    return jax.nn.silu(gate_part) * upward


def matmul(left_op, right_op):
    return jnp.dot(left_op, right_op, preferred_element_type=jnp.float32)


def matmul_last(left_op, right_op):
    return lax.dot_general(
        left_op, right_op, (((1,), (1,)), ((), ())), preferred_element_type=jnp.float32
    )


def matmul_first(left_op, right_op):
    return lax.dot_general(
        left_op, right_op, (((0,), (0,)), ((), ())), preferred_element_type=jnp.float32
    )


def norm_back(values, gain_vec, grad_output):
    unused, pull_back = jax.vjp(rms_norm, values, gain_vec)
    return pull_back(grad_output)


def adam_update(weight, gradient_value, moment, square_avg, decay_rate):
    moment_new = MOMENT_BETA * moment + (1.0 - MOMENT_BETA) * gradient_value
    square_new = MOMENT_BETA * square_avg + (1.0 - MOMENT_BETA) * gradient_value * gradient_value
    change = -(
        ADAM_RATE * (moment_new / (jnp.sqrt(square_new) + ADAM_EPSILON) + decay_rate * weight)
    )
    return (change, moment_new, square_new)


def per_device(
    token_ids,
    target_ids,
    loss_slots,
    valid_mask,
    prefix_lens,
    embed_table,
    norm_gains,
    qkv_weight,
    output_weight,
    mlp_weight,
    embed_mean,
    embed_square,
    gain_mean,
    gain_square,
    qkv_mean,
    qkv_square,
    out_mean,
    out_square,
    mlp_mean,
    mlp_square,
    left_bases,
    qkv_bases,
    out_bases,
    feedforward_bases,
):
    row_index = lax.axis_index("row")
    col_index = lax.axis_index("col")
    row_count = lax.axis_size("row")
    col_count = lax.axis_size("col")
    low = jnp.bfloat16
    group_tokens = token_ids.shape[0]
    pick_count = loss_slots.shape[0]
    device_tokens = group_tokens // col_count
    vocab_shard, features = embed_table.shape
    width = features * row_count
    query_width = Q_HEADS * HEAD
    kv_width = KV_HEADS * HEAD
    group_size = Q_HEADS // KV_HEADS
    scaling = HEAD ** (-0.5)
    qkv_cols, out_cols, ff_cols = qkv_weight.shape[1], output_weight.shape[1], mlp_weight.shape[2]
    vocab_part = vocab_shard // row_count

    ids_all = lax.all_gather(jnp.concatenate([token_ids, target_ids]), "row", axis=0)
    table_first, left_first, ids_all = lax.optimization_barrier((embed_table, left_bases, ids_all))

    qkv_width, ff_width = qkv_cols * col_count, ff_cols * col_count
    attn_full = lax.all_gather(
        jnp.concatenate([qkv_weight.astype(low), output_weight.astype(low)], axis=1),
        ("col", "row"),
        axis=0,
        tiled=True,
    ).reshape(col_count, width, qkv_cols + out_cols)
    mlp_low = mlp_weight.astype(low)
    mlp_full = lax.all_gather(
        jnp.concatenate([mlp_low[0], mlp_low[1], mlp_low[2]], axis=1),
        ("col", "row"),
        axis=0,
        tiled=True,
    ).reshape(col_count, width, 3 * ff_cols)
    bases_low = left_first.astype(low)
    left_block = jnp.concatenate([bases_low[k] for k in range(5)], axis=1)
    left_full = lax.all_gather(left_block, "row", axis=0, tiled=True)
    columns = range(col_count)
    qkv_full = [attn_full[c, :, :qkv_cols] for c in columns]
    out_full = [attn_full[c, :, qkv_cols:] for c in columns]
    gate_full, up_full, down_full = (
        [mlp_full[c, :, k * ff_cols : (k + 1) * ff_cols] for c in columns] for k in range(3)
    )

    def by_columns(values, weights, multiply):
        return jnp.concatenate([multiply(values, weight) for weight in weights], axis=1)

    def over_columns(values, weights):
        count = values.shape[1] // col_count
        terms = [
            matmul_last(values[:, c * count : (c + 1) * count], weight)
            for c, weight in enumerate(weights)
        ]
        return functools.reduce(jnp.add, terms)

    tokens_all = ids_all[:, :group_tokens].reshape(row_count, col_count, device_tokens)
    targets_all = ids_all[:, group_tokens:].reshape(row_count * pick_count)
    local_tokens = jnp.moveaxis(tokens_all, 1, 0) - col_index * vocab_shard
    inside = (local_tokens >= 0) & (local_tokens < vocab_shard)
    local_tokens = jnp.where(inside, local_tokens, vocab_shard)
    table_low_t = table_first.astype(low).T

    def reduce_rows(values):
        return lax.psum_scatter(values, "row", scatter_dimension=0, tiled=True)

    padded = jnp.pad(table_low_t, ((0, 0), (0, 128 - vocab_shard % 128)))
    found = lookup(local_tokens.reshape(-1), padded, device_tokens, 6)
    table_later, found = lax.optimization_barrier((table_low_t, found))
    embedded = found.reshape(width, device_tokens).T.astype(jnp.float32)

    table_parts = jnp.moveaxis(table_later.reshape(features, row_count, vocab_part), 1, 0)
    part_pieces = [
        pick_block(table_parts, (row_index + k) % row_count, 0) for k in range(row_count)
    ]
    table_part = to_absolute(deliver(part_pieces, "row", 1), row_index).reshape(width, vocab_part)

    normed = rms_norm(embedded, norm_gains[0]).astype(low)
    project = by_columns(normed, qkv_full, matmul).astype(low)
    first_token = col_index * device_tokens
    positions = first_token + jnp.arange(device_tokens, dtype=jnp.int32)
    seq_prefix = jnp.sum(
        jnp.where(jnp.arange(prefix_lens.shape[0], dtype=jnp.int32) == row_index, prefix_lens, 0)
    )

    def rotate_here(values):
        return rotary(values, positions)

    queries_raw = project[:, :query_width].astype(jnp.float32).reshape(device_tokens, Q_HEADS, HEAD)
    keys_raw = (
        project[:, query_width : query_width + kv_width]
        .astype(jnp.float32)
        .reshape(device_tokens, KV_HEADS, HEAD)
    )
    queries = rotate_here(queries_raw).astype(low).reshape(device_tokens, KV_HEADS, group_size, HEAD)
    keys_local = rotate_here(keys_raw).astype(low).reshape(device_tokens, kv_width)
    keys_values = jnp.concatenate(
        collect(
            jnp.concatenate([keys_local, project[:, query_width + kv_width :]], axis=1), "col"
        ),
        axis=0,
    )
    attn_keys = keys_values[:, :kv_width].reshape(LEN, KV_HEADS, HEAD)
    attn_values = keys_values[:, kv_width:].reshape(LEN, KV_HEADS, HEAD)
    key_blocks = (col_index - jnp.arange(col_count, dtype=jnp.int32)) % col_count
    key_positions = (
        key_blocks[:, None] * device_tokens + jnp.arange(device_tokens, dtype=jnp.int32)[None, :]
    ).reshape(LEN)
    allowed = (key_positions[None, :] <= positions[:, None]) | (key_positions[None, :] < seq_prefix)

    raw_scores = (
        jnp.einsum("qhgd,khd->hgqk", queries, attn_keys, preferred_element_type=jnp.float32)
        * scaling
    )
    scores = jnp.where(allowed, raw_scores, MASK_VALUE)
    largest = jnp.max(scores, axis=-1, keepdims=True)
    weights = jnp.exp(scores - largest)
    attn_probs = weights / jnp.sum(weights, axis=-1, keepdims=True)
    attended = (
        jnp.einsum(
            "hgqk,khd->qhgd",
            attn_probs.astype(low),
            attn_values,
            preferred_element_type=jnp.float32,
        )
        .astype(low)
        .reshape(device_tokens, query_width)
    )
    hidden_one = embedded + over_columns(attended, out_full)
    middle = rms_norm(hidden_one, norm_gains[1]).astype(low)
    gate_part = by_columns(middle, gate_full, matmul)
    upward = by_columns(middle, up_full, matmul)
    inner_act = swiglu(gate_part, upward).astype(low)
    hidden_two = hidden_one + over_columns(inner_act, down_full)
    final = rms_norm(hidden_two, norm_gains[2]).astype(low)

    pick_hit = (loss_slots[:, None] == positions[None, :]).astype(low)
    final_here = matmul(pick_hit, final).astype(low)
    final_pick = spread(final_here, 0)
    logits = matmul(final_pick, table_part)
    local_max = jnp.max(logits, axis=-1)
    local_sum = jnp.sum(jnp.exp(logits - local_max[:, None]), axis=-1)
    part_first = col_index * vocab_shard + row_index * vocab_part
    target_hit = (
        jnp.arange(vocab_part, dtype=jnp.int32)[None, :] == (targets_all - part_first)[:, None]
    )
    local_target = jnp.sum(jnp.where(target_hit, logits, 0.0), axis=-1)
    own_stats = jnp.stack([local_max, local_sum, local_target]).reshape(-1, 128)
    everyone = share(own_stats, 1).reshape(row_count * col_count, 3, row_count * pick_count)
    top = jnp.max(everyone[:, 0], axis=0)
    log_total = top + jnp.log(jnp.sum(everyone[:, 1] * jnp.exp(everyone[:, 0] - top), axis=0))
    target_logit = jnp.sum(everyone[:, 2], axis=0)
    valid_count = jnp.maximum(jnp.sum(valid_mask).astype(jnp.float32), 1.0)
    row_weights = valid_mask.astype(jnp.float32) / valid_count
    loss_value = jnp.sum(row_weights * (log_total - target_logit))
    grad_logits = (
        (jnp.exp(logits - log_total[:, None]) - target_hit.astype(jnp.float32))
        * row_weights[:, None]
    ).astype(low)
    grad_pick = matmul_last(grad_logits, table_part).astype(low)
    grad_seq = fold(grad_pick, 2)
    grad_final = matmul_first(pick_hit, grad_seq)

    table_grad_part = matmul_first(final_pick, grad_logits).astype(low)
    grad_parts = table_grad_part.reshape(row_count, features, vocab_part)
    grad_pieces = [pick_block(grad_parts, (row_index + k) % row_count, 0) for k in range(row_count)]
    table_grad = to_absolute(deliver(grad_pieces, "row", 1), row_index)
    table_grad = jnp.moveaxis(table_grad, 0, 1).reshape(features, vocab_shard).astype(jnp.float32)

    grad_two, gain_two = norm_back(hidden_two, norm_gains[2], grad_final)
    grad_two_low = grad_two.astype(low)
    ff_blocks = ff_width // ff_cols
    mlp_grad = outer(grad_two_low, left_full, 4, inner_act, ff_cols, 3 * ff_width, 0, None)
    grad_inner = by_columns(grad_two_low, down_full, matmul)
    unused, pull_swiglu = jax.vjp(swiglu, gate_part, upward)
    grad_gate, grad_up = pull_swiglu(grad_inner)
    grad_gate = grad_gate.astype(low)
    grad_up = grad_up.astype(low)
    mlp_grad = outer(middle, left_full, 2, grad_gate, ff_cols, 3 * ff_width, ff_blocks, mlp_grad)
    mlp_grad = outer(middle, left_full, 3, grad_up, ff_cols, 3 * ff_width, 2 * ff_blocks, mlp_grad)
    grad_gate, grad_up, mlp_grad = lax.optimization_barrier((grad_gate, grad_up, mlp_grad))
    mlp_rows = reduce_rows(mlp_grad)
    grad_middle = over_columns(grad_gate, gate_full) + over_columns(grad_up, up_full)
    grad_middle_in, gain_one = norm_back(hidden_one, norm_gains[1], grad_middle)
    grad_one = grad_two + grad_middle_in
    grad_one_low = grad_one.astype(low)
    attn_width = query_width + qkv_width
    attn_grad = outer(
        grad_one_low, left_full, 1, attended, SMALL_BLOCK, attn_width, 0, None
    )
    grad_attended = by_columns(grad_one_low, out_full, matmul).astype(low).reshape(
        device_tokens, KV_HEADS, group_size, HEAD
    )
    grad_probs = jnp.einsum(
        "qhgd,khd->hgqk", grad_attended, attn_values, preferred_element_type=jnp.float32
    )
    inner_sum = jnp.sum(attn_probs * grad_probs, axis=-1, keepdims=True)
    grad_scores = (attn_probs * (grad_probs - inner_sum)).astype(low)
    grad_queries = (
        jnp.einsum("hgqk,khd->qhgd", grad_scores, attn_keys, preferred_element_type=jnp.float32)
        * scaling
    )
    grad_keys = (
        jnp.einsum("hgqk,qhgd->khd", grad_scores, queries, preferred_element_type=jnp.float32)
        * scaling
    )
    grad_values = jnp.einsum(
        "hgqk,qhgd->khd",
        attn_probs.astype(low),
        grad_attended,
        preferred_element_type=jnp.float32,
    )
    grad_pairs = (
        jnp.concatenate([grad_keys.reshape(LEN, kv_width), grad_values.reshape(LEN, kv_width)], axis=1)
        .astype(low)
        .reshape(col_count, device_tokens, 2 * kv_width)
    )
    grad_pairs = summed(deliver([grad_pairs[k] for k in range(col_count)], "col", -1))
    unused, pull_query = jax.vjp(rotate_here, queries_raw)
    grad_query_raw = pull_query(grad_queries.reshape(device_tokens, Q_HEADS, HEAD))[0]
    unused, pull_key = jax.vjp(rotate_here, keys_raw)
    grad_key_raw = pull_key(grad_pairs[:, :kv_width].reshape(device_tokens, KV_HEADS, HEAD))[0]
    grad_project = jnp.concatenate(
        [
            grad_query_raw.reshape(device_tokens, query_width),
            grad_key_raw.reshape(device_tokens, kv_width),
            grad_pairs[:, kv_width:],
        ],
        axis=1,
    ).astype(low)
    attn_grad = outer(
        normed, left_full, 0, grad_project, SMALL_BLOCK, attn_width,
        query_width // SMALL_BLOCK, attn_grad,
    )
    attn_rows = reduce_rows(attn_grad)
    grad_normed = over_columns(grad_project, qkv_full)
    grad_embed_in, gain_zero = norm_back(embedded, norm_gains[0], grad_normed)
    grad_embedded = (grad_one + grad_embed_in).astype(low)
    own_gains = jnp.stack([gain_zero, gain_one, gain_two]).reshape(-1, 128)
    gain_grads = jnp.sum(
        share(own_gains, 3).reshape(row_count * col_count, 3, width), axis=0
    )
    by_feature = grad_embedded.T.reshape(row_count, features, device_tokens)
    vocab_room = -(-(vocab_shard + 1) // VOCAB_TILE) * VOCAB_TILE
    table_grad = scatter(
        local_tokens[:, :, :, None],
        by_feature,
        jnp.pad(table_grad, ((0, 0), (0, vocab_room - vocab_shard))),
        7,
    )[:, :vocab_shard]

    mlp_rows, table_grad = lax.optimization_barrier((mlp_rows, table_grad))
    mlp_new = soap(
        [mlp_rows],
        [feedforward_bases],
        [(mlp_mean[j], mlp_square[j], mlp_weight[j], bases_low[2 + j]) for j in range(3)],
        (True, True, True),
        (2, 0, 1),
        4,
    )
    mlp_next, mlp_moment, mlp_scale = (
        jnp.stack([entry[k] for entry in mlp_new]) for k in range(3)
    )

    attn_rows, mlp_next = lax.optimization_barrier((attn_rows, mlp_next))

    def blocks(values):
        return jnp.moveaxis(values.reshape(values.shape[0], col_count, -1), 1, 0)

    (out_update, out_moment, out_scale), (qkv_next, qkv_moment, qkv_scale) = soap(
        [blocks(attn_rows[:, :query_width]), blocks(attn_rows[:, query_width:])],
        [blocks(out_bases.astype(low)), blocks(qkv_bases.astype(low))],
        [
            (out_mean, out_square, output_weight, bases_low[1]),
            (qkv_mean, qkv_square, qkv_weight, bases_low[0]),
        ],
        (False, True),
        (),
        5,
    )
    embed_change, embed_moment, embed_scale = adam_update(
        embed_table, table_grad.T, embed_mean, embed_square, WEIGHT_DECAY
    )
    embed_next = embed_table + embed_change
    gain_update, gain_moment, gain_scale = adam_update(
        norm_gains, gain_grads, gain_mean, gain_square, 0.0
    )
    return (
        loss_value,
        embed_next,
        embed_moment,
        embed_scale,
        gain_update,
        gain_moment,
        gain_scale,
        qkv_next,
        qkv_moment,
        qkv_scale,
        out_update,
        out_moment,
        out_scale,
        mlp_next,
        mlp_moment,
        mlp_scale,
    )


def solution(mesh):
    placed = (
        P("row"),
        P("row"),
        P("row"),
        P(),
        P(),
        P("col", "row"),
        P(),
        P("row", "col"),
        P("row", "col"),
        P(None, "row", "col"),
        P("col", "row"),
        P("col", "row"),
        P(),
        P(),
        P("row", "col"),
        P("row", "col"),
        P("row", "col"),
        P("row", "col"),
        P(None, "row", "col"),
        P(None, "row", "col"),
        P(None, "row", None),
        P("col", None),
        P("col", None),
        P(None, "col", None),
    )
    return jax.shard_map(
        per_device,
        mesh=mesh,
        in_specs=placed,
        out_specs=(
            P(),
            P("col", "row"),
            P("col", "row"),
            P("col", "row"),
            P(),
            P(),
            P(),
            P("row", "col"),
            P("row", "col"),
            P("row", "col"),
            P("row", "col"),
            P("row", "col"),
            P("row", "col"),
            P(None, "row", "col"),
            P(None, "row", "col"),
            P(None, "row", "col"),
        ),
        check_vma=False,
    )
```

time: 1310 us -> 1070 us (0.82)
  Pallas kernels: 0 us -> 582 us
  waiting for transfers between devices: 425 us -> 116 us
  matrix products: 346 us -> 153 us
  starting transfers between devices: 200 us -> 26.7 us
  blocking collectives: 126 us -> 10.6 us
  local copies, waits for them, and re-layouts: 99.6 us -> 83.1 us
    pallas_call x0 -> x13, Pallas kernels: none -> 582 us  [the longest x2 248 us: soap(): pl.pallas_call(functools.partial(soap_kernel, rows, cols, adds, streamed)...]
    ppermute x86 -> x20, starting transfers between devices: 190 us -> 26.1 us  [send(): lax.ppermute(value, axis, [(k, (k + shift) % count) for k in range(count)])]
    ppermute x86 -> x20, waiting for transfers between devices: 260 us -> 116 us  [send(): lax.ppermute(value, axis, [(k, (k + shift) % count) for k in range(count)])]
    dot_general x11 -> x2, matrix products: 117 us -> 6.24 us  [matmul_first(): lax.dot_general(left_op, right_op, (((0,), (0,)), ((), ())), preferred_el...]
    psum x2 -> x0, waiting for transfers between devices: 74.5 us -> none  [the longest x1 37.6 us: per_device(): final_seq = lax.psum(final_here, 'col')]
    all_gather x1 -> x0, blocking collectives: 69.5 us -> none  [per_device(): lax.all_gather(jnp.stack([local_max, local_sum, local_target]), ('row', '...]
    dot_general x15 -> x21, matrix products: 112 us -> 52.7 us  [matmul_last(): lax.dot_general(left_op, right_op, (((1,), (1,)), ((), ())), preferred_el...]
    psum x1 -> x0, blocking collectives: 47.3 us -> none  [per_device(): lax.psum(jnp.stack([gain_zero, gain_one, gain_two]), ('row', 'col'))]
  transfers between devices with their start and end apart: 100 -> 25, of which waited for: 40 -> 9; matrix products, arithmetic and copies ran while one was open for 36% -> 26% of each run, Pallas kernels for 0% -> 45%
where the time goes in v2:
time: 1070 us; the launch traced here: 1060 us
  Pallas kernels  582 us (54%)
  matrix products  153 us (14%)
  waiting for transfers between devices  116 us (11%)
  local copies, waits for them, and re-layouts  83.1 us (8%)
  other arithmetic  69.1 us (6%)
  starting transfers between devices  26.7 us (2%)
  between operations  17.1 us (2%)
    pallas_call x2, Pallas kernels, soap(): pl.pallas_call(functools.partial(soap_kernel, rows, cols, adds, streamed)...  248 us
    ppermute x20, waiting for transfers between devices, send(): lax.ppermute(value, axis, [(k, (k + shift) % count) for k in range(count)])  116 us
    pallas_call x1, Pallas kernels, lookup(): pl.pallas_call(functools.partial(lookup_kernel, rows, cols), out_shape=ja...  114 us
    pallas_call x1, Pallas kernels, scatter(): pl.pallas_call(functools.partial(scatter_kernel, rows, cols), out_shape=j...  74.3 us
    dot_general x21, matrix products, matmul_last(): lax.dot_general(left_op, right_op, (((1,), (1,)), ((), ())), preferred_el...  52.7 us
    pallas_call x1, Pallas kernels, spread(): pl.pallas_call(functools.partial(spread_kernel, rows, cols), out_shape=ja...  46.6 us
    dot_general x22, matrix products, matmul(): return jnp.dot(left_op, right_op, preferred_element_type=jnp.float32)  43.7 us
    pallas_call x5, Pallas kernels, outer(): pl.pallas_call(outer_kernel, grid=(other.shape[1] // block,), out_shape=j...  38.5 us
  transfers between devices with their start and end apart: 25, of which 9 were waited for; matrix products, arithmetic and copies ran while one was open for 26% of the time, Pallas kernels for 45%

profile of v2, /device:TPU:0, one launch (start us, length us, event | category | flops | bytes accessed | tf_op | source)
XLA Modules:
  0.0 1058.3 jit_solution(9364823464265082627)
XLA Ops:
  11.4 10.6 all-gather.1
  23.2 2.6 convert_bitcast_fusion
  28.0 113.7 %shard_map.351 = bf16[8,144,256]{2,1,0:T(8,128)(2,1)} custom-call(s32[8192]{0:T(1024)} %bitcast.496, bf16[144,8064]{1,0:T(8,128)(2,1)} %pad.22.table_ref), custom_call_target="tpu_custom_call" | custom-call | tf_op jit(solution)/shard_map/pallas_call | solution.py:611
  141.6 5.7 reshape.380
  147.4 6.0 constant_dynamic-slice_fusion
  154.2 2.8 collective-permute-start.3
  179.6 2.8 collective-permute-start.8
  187.9 3.7 collective-permute-done.8
  191.6 2.6 collective-permute-done.9
  194.2 2.5 fusion.20
  196.7 2.6 convolution_convert_fusion.5
  210.9 18.2 %collective-permute-done.2 = bf16[256,768]{0,1:T(8,128)(2,1)S(1)} collective-permute-done((bf16[256,768]{0,1:T(8,128)(2,1)S(1)}, bf16[256,768]{0,1:T(8,128)(2,1)S(1)}, u32[]{:S(2)}, u32[]{:S(2)}) %collective-permute-start.2) | collective-permute-done | bytes 393248 | tf_op jit(solution)/shard_map/ppermute | solution.py:706
  229.1 51.4 %collective-permute-done.1 = bf16[256,768]{0,1:T(8,128)(2,1)S(1)} collective-permute-done((bf16[256,768]{0,1:T(8,128)(2,1)S(1)}, bf16[256,768]{0,1:T(8,128)(2,1)S(1)}, u32[]{:S(2)}, u32[]{:S(2)}) %collective-permute-start.1) | collective-permute-done | bytes 393248 | tf_op jit(solution)/shard_map/ppermute | solution.py:706
  280.8 10.9 %fusion.115 = (f32[6,3,256]{2,1,0:T(4,128)S(1)}, f32[6,3,256,1024]{2,3,1,0:T(8,128)}) fusion(pred[256,1024]{0,1:T(8,128)(4,1)} %compare_or_fusion, bf16[1024,6,64,1]{0,2,3,1:T(8,128)(2,1)S(1)} %bitcast.450, bf16[256,6,3,32]{0,3,2,1:T(8,128)(2,1)S(1)} %bitcast.473, bf16[256,6,3,32]{0,3,2,1:T(8,128)(2,1)S(1)} %bitcast.471), kind=kOutput, calls=%fused_computation.336 | convolution fusion | flops 624034816 | bytes 20531200 | tf_op jit(solution)/shard_map/sub | solution.py:934
  291.8 8.1 fusion.41
  306.2 3.0 multiply_reduce_fusion.6
  309.4 2.4 fusion.33
  311.8 3.1 fusion.32
  314.9 3.1 fusion.31
  318.0 2.4 fusion.30
  320.5 2.4 fusion.28
  322.9 2.4 fusion.27
  333.1 46.6 %shard_map.352 = bf16[8,4,32,1152]{3,2,1,0:T(8,128)(2,1)} custom-call(bf16[4,32,1152]{2,1,0:T(8,128)(2,1)} %bitcast.476), custom_call_target="tpu_custom_call" | custom-call | tf_op jit(solution)/shard_map/pallas_call | solution.py:145
  379.7 4.5 fusion.116
  386.8 12.8 %shard_map.353 = f32[8,4,24,128]{3,2,1,0:T(8,128)} custom-call(f32[24,128]{1,0:T(8,128)} %reshape.382.x_ref), custom_call_target="tpu_custom_call" | custom-call | tf_op jit(solution)/shard_map/pallas_call | solution.py:80
  401.8 8.0 convolution_convert_fusion
  409.8 35.4 %shard_map.354 = bf16[4,32,1152]{2,1,0:T(8,128)(2,1)} custom-call(bf16[8,4,32,1152]{3,2,1,0:T(8,128)(2,1)} %bitcast.463), custom_call_target="tpu_custom_call" | custom-call | tf_op jit(solution)/shard_map/pallas_call | solution.py:224
  447.7 2.4 fusion.38
  454.5 2.3 fusion.34
  461.4 8.0 shard_map.355.refs_0_
  469.3 8.1 shard_map.356.refs_0_
  477.4 8.1 shard_map.357
  488.1 2.4 fusion.24
  490.5 2.8 fusion.29
  493.4 2.7 convolution_add_fusion.5
  496.1 2.6 convolution_add_fusion.4
  498.8 2.6 convolution_add_fusion.3
  501.4 2.8 convolution_add_fusion.2
  504.2 3.0 convolution_add_fusion.1
  507.2 3.6 multiply_reduce_fusion.1
  515.8 12.6 %fusion.1 = (f32[6,3,256]{2,1,0:T(4,128)S(1)}, f32[6,1024,256,3]{2,1,3,0:T(8,128)}) fusion(f32[6,3,256,1024]{2,3,1,0:T(8,128)} %get-tuple-element.152, f32[6,3,256]{2,1,0:T(4,128)S(1)} %copy-done.96, bf16[1024,6,64,1]{0,2,3,1:T(8,128)(2,1)S(1)} %bitcast.479, bf16[256,6,3,64]{0,3,2,1:T(8,128)(2,1)S(1)} %bitcast.481), kind=kOutput, calls=%fused_computation.3 | convolution fusion | flops 618130944 | bytes 39161856 | tf_op jit(solution)/shard_map/qhgd,khd->hgqk/dot_general | solution.py:1011
  528.4 14.1 %fusion.3 = bf16[6,3,256,1024]{2,3,1,0:T(8,128)(2,1)S(1)} fusion(f32[6,1024,256,3]{2,1,3,0:T(8,128)} %get-tuple-element.160, f32[6,3,256]{2,1,0:T(4,128)S(1)} %get-tuple-element.159, f32[6,3,256,1024]{2,3,1,0:T(8,128)} %get-tuple-element.152, f32[6,3,256]{2,1,0:T(4,128)S(1)} %copy-done.96), kind=kLoop, calls=%fused_computation.5 | loop fusion | flops 18874368 | bytes 47222784 | tf_op jit(solution)/shard_map/convert_element_type | solution.py:1015
  542.5 2.9 fusion.23
  546.6 10.6 %bitcast_convert_fusion = bf16[6,64,1024]{2,1,0:T(8,128)(2,1)} fusion(bf16[256,6,3,64]{0,3,2,1:T(8,128)(2,1)S(1)} %bitcast.482, f32[6,3,256,1024]{2,3,1,0:T(8,128)} %get-tuple-element.152, f32[6,3,256]{2,1,0:T(4,128)S(1)} %copy-done.96), kind=kOutput, calls=%fused_computation.89 | convolution fusion | flops 613810176 | bytes 20269056 | tf_op jit(solution)/shard_map/hgqk,qhgd->khd/dot_general | solution.py:1024
  565.2 5.7 convolution_multiply_fusion
  572.2 6.3 shard_map.360.refs_0_
  578.6 10.1 collective-permute-done.11
  592.4 8.0 shard_map.361
  601.2 2.7 copy.125.ids_ref
  607.1 3.3 copy.132
  612.7 2.5 slice_bitcast_fusion.62
  620.4 4.1 convolution_convert_fusion.1
  624.5 2.8 copy.123
  632.1 2.9 convolution_add_fusion.11
  644.5 22.1 %collective-permute-done.16 = bf16[144,1000]{1,0:T(8,128)(2,1)S(1)} collective-permute-done((bf16[144,1000]{1,0:T(8,128)(2,1)S(1)}, bf16[144,1000]{1,0:T(8,128)(2,1)S(1)}, u32[]{:S(2)}, u32[]{:S(2)}) %collective-permute-start.16) | collective-permute-done | bytes 288032 | tf_op jit(solution)/shard_map/ppermute | solution.py:706
  666.6 4.1 collective-permute-done.17
  673.0 5.1 convert_element_type.185
  678.1 4.6 pad_convert_fusion.base_ref
  689.1 74.3 %shard_map.358 = f32[144,8192]{1,0:T(8,128)} custom-call(s32[4,8,256,1]{3,2,1,0:T(8,128)} %copy.125.ids_ref, bf16[8,144,256]{2,1,0:T(8,128)(2,1)} %bitcast.452, f32[144,8192]{1,0:T(8,128)} %pad_convert_fusion.base_ref), custom_call_target="tpu_custom_call" | custom-call | tf_op jit(solution)/shard_map/pallas_call | solution.py:688
  764.8 13.7 %shard_map.359 = f32[8,4,27,128]{3,2,1,0:T(8,128)} custom-call(f32[27,128]{1,0:T(8,128)} %reshape.397.x_ref), custom_call_target="tpu_custom_call" | custom-call | tf_op jit(solution)/shard_map/pallas_call | solution.py:80
  780.2 170.5 %shard_map.362 = (f32[144,768]{1,0:T(8,128)}, f32[144,768]{1,0:T(8,128)}, f32[144,768]{1,0:T(8,128)}, f32[144,768]{1,0:T(8,128)}, f32[144,768]{1,0:T(8,128)}, /*...) custom-call(bf16[144,9216]{1,0:T(8,128)(2,1)} %reduce-scatter.3.cloned.1.call-done.refs_0_, ...), custom_call_target="tpu_custom_call" | custom-call | tf_op jit(solution)/shard_map/pallas_call | solution.py:473
  950.8 2.4 pad_maximum_fusion.4
  957.3 77.1 %shard_map.363 = (f32[144,288]{1,0:T(8,128)}, f32[144,288]{1,0:T(8,128)}, f32[144,288]{1,0:T(8,128)}, f32[144,480]{1,0:T(8,128)}, f32[144,480]{1,0:T(8,128)}, /*index=5*/f32[144,480]{1,0:T(8,128)}) custom-call(bf16[4,144,288]{2,1,0:T(8,128)(2,1)} %bitcast.467, bf16[4,144,480]{2,1,0:T(8,128)(2,1)} %bitcast.458, bf16[4,288,288]{2,1,0:T(8,128)(2,1)} %bitcast.449, ...), custom_call_target="tpu_custom_call" | custom-call | tf_op jit(solution)/shard_map/pallas_call | solution.py:473
  1034.4 9.9 negate_add_fusion
  (469 shorter events, 147.2 us)
Async XLA Ops:
  7.2 189.5 %all-gather.6.cloned.1.call-start = ((), (), s32[]{:S(2)}) async-start(), calls=%async_computation.2 | async-start | bytes 7299072 | tf_op jit(solution)/shard_map/all_gather | solution.py:840
  10.1 299.3 %all-gather.8.cloned.1.call-start = ((), (), s32[]{:S(2)}) async-start(), calls=%async_computation.3 | async-start | bytes 21897216 | tf_op jit(solution)/shard_map/all_gather | solution.py:847
  11.2 450.2 %all-gather.10.cloned.1.call-start = ((), (), s32[]{:S(2)}) async-start(), calls=%async_computation.4 | async-start | bytes 14929920 | tf_op jit(solution)/shard_map/all_gather | solution.py:855
  154.2 8.0 copy-start.31
  154.2 25.4 %collective-permute-start.3 = (bf16[144,1000]{1,0:T(8,128)(2,1)}, bf16[144,1000]{1,0:T(8,128)(2,1)}, u32[]{:S(2)}, u32[]{:S(2)}) collective-permute-start(bf16[144,1000]{1,0:T(8,128)(2,1)} %bitcast.396), channel_id=1, source_target_pairs={{0,28},{4,0},{8,4},{12,8},{16,12},{20,16},{24,20},{28,24},{1,29},{... | collective-permute-start | bytes 864008 | tf_op jit(solution)/shard_map/ppermute | solution.py:706
  157.8 25.5 %collective-permute-start.4 = (bf16[144,1000]{1,0:T(8,128)(2,1)}, bf16[144,1000]{1,0:T(8,128)(2,1)}, u32[]{:S(2)}, u32[]{:S(2)}) collective-permute-start(bf16[144,1000]{1,0:T(8,128)(2,1)} %bitcast.395), channel_id=1, source_target_pairs={{0,24},{4,28},{8,0},{12,4},{16,8},{20,12},{24,16},{28,20},{1,25},{... | collective-permute-start | bytes 864008 | tf_op jit(solution)/shard_map/ppermute | solution.py:706
  158.6 26.3 %collective-permute-start.5 = (bf16[144,1000]{1,0:T(8,128)(2,1)}, bf16[144,1000]{1,0:T(8,128)(2,1)}, u32[]{:S(2)}, u32[]{:S(2)}) collective-permute-start(bf16[144,1000]{1,0:T(8,128)(2,1)} %bitcast.394), channel_id=1, source_target_pairs={{0,20},{4,24},{8,28},{12,0},{16,4},{20,8},{24,12},{28,16},{1,21},{... | collective-permute-start | bytes 864008 | tf_op jit(solution)/shard_map/ppermute | solution.py:706
  159.4 26.4 %collective-permute-start.6 = (bf16[144,1000]{1,0:T(8,128)(2,1)}, bf16[144,1000]{1,0:T(8,128)(2,1)}, u32[]{:S(2)}, u32[]{:S(2)}) collective-permute-start(bf16[144,1000]{1,0:T(8,128)(2,1)} %bitcast.393), channel_id=1, source_target_pairs={{0,16},{4,20},{8,24},{12,28},{16,0},{20,4},{24,8},{28,12},{1,17},{... | collective-permute-start | bytes 864008 | tf_op jit(solution)/shard_map/ppermute | solution.py:706
  162.0 24.9 %collective-permute-start.7 = (bf16[144,1000]{1,0:T(8,128)(2,1)}, bf16[144,1000]{1,0:T(8,128)(2,1)}, u32[]{:S(2)}, u32[]{:S(2)}) collective-permute-start(bf16[144,1000]{1,0:T(8,128)(2,1)} %bitcast.392), channel_id=1, source_target_pairs={{0,12},{4,16},{8,20},{12,24},{16,28},{20,0},{24,4},{28,8},{1,13},{... | collective-permute-start | bytes 864008 | tf_op jit(solution)/shard_map/ppermute | solution.py:706
  164.8 615.4 %reduce-scatter.3.cloned.1.call-start = ((), (), s32[]{:S(2)}) async-start(), calls=%async_computation.5 | async-start | bytes 23887872 | tf_op jit(solution)/shard_map/reduce_scatter | solution.py:882
  165.4 140.7 %copy-start.1 = (f32[1152,256]{0,1:T(8,128)}, f32[1152,256]{0,1:T(8,128)S(1)}, u32[]{:S(2)}) copy-start(f32[1152,256]{0,1:T(8,128)S(1)} %copy.102) | copy-start | bytes 3538948
  179.6 12.0 %collective-permute-start.8 = (bf16[144,1000]{1,0:T(8,128)(2,1)}, bf16[144,1000]{1,0:T(8,128)(2,1)S(1)}, u32[]{:S(2)}, u32[]{:S(2)}) collective-permute-start(bf16[144,1000]{1,0:T(8,128)(2,1)} %bitcast.493), channel_id=1, source_target_pairs={{0,8},{4,12},{8,16},{12,20},{16,24},{20,28},{24,0},{28,4},{1,9},{5... | collective-permute-start | bytes 864008 | tf_op jit(solution)/shard_map/ppermute | solution.py:706
  183.4 10.8 %collective-permute-start.9 = (bf16[144,1000]{1,0:T(8,128)(2,1)}, bf16[144,1000]{1,0:T(8,128)(2,1)S(1)}, u32[]{:S(2)}, u32[]{:S(2)}) collective-permute-start(bf16[144,1000]{1,0:T(8,128)(2,1)} %bitcast.492), channel_id=1, source_target_pairs={{0,4},{4,8},{8,12},{12,16},{16,20},{20,24},{24,28},{28,0},{1,5},{5... | collective-permute-start | bytes 864008 | tf_op jit(solution)/shard_map/ppermute | solution.py:706
  201.4 27.6 %collective-permute-start.2 = (bf16[256,768]{0,1:T(8,128)(2,1)S(1)}, bf16[256,768]{0,1:T(8,128)(2,1)S(1)}, u32[]{:S(2)}, u32[]{:S(2)}) collective-permute-start(bf16[256,768]{0,1:T(8,128)(2,1)S(1)} %pad_maximum_fusion.14), channel_id=1, source_target_pairs={{0,3},{1,0},{2,1},{3,2},{4,7},{5,4},{6,5},{7,6},{8,11},{9,8},{10,9... | collective-permute-start | bytes 1179656 | tf_op jit(solution)/shard_map/ppermute | solution.py:706
  203.0 77.4 %collective-permute-start.1 = (bf16[256,768]{0,1:T(8,128)(2,1)S(1)}, bf16[256,768]{0,1:T(8,128)(2,1)S(1)}, u32[]{:S(2)}, u32[]{:S(2)}) collective-permute-start(bf16[256,768]{0,1:T(8,128)(2,1)S(1)} %pad_maximum_fusion.14), channel_id=1, source_target_pairs={{0,2},{1,3},{2,0},{3,1},{4,6},{5,7},{6,4},{7,5},{8,10},{9,11},{10,... | collective-permute-start | bytes 1179656 | tf_op jit(solution)/shard_map/ppermute | solution.py:706
  204.9 75.6 %collective-permute-start = (bf16[256,768]{0,1:T(8,128)(2,1)S(1)}, bf16[256,768]{0,1:T(8,128)(2,1)S(1)}, u32[]{:S(2)}, u32[]{:S(2)}) collective-permute-start(bf16[256,768]{0,1:T(8,128)(2,1)S(1)} %pad_maximum_fusion.14), channel_id=1, source_target_pairs={{0,1},{1,2},{2,3},{3,0},{4,5},{5,6},{6,7},{7,4},{8,9},{9,10},{10,1... | collective-permute-start | bytes 1179656 | tf_op jit(solution)/shard_map/ppermute | solution.py:706
  210.9 69.9 %copy-start.58 = (bf16[256,18,32]{0,2,1:T(8,128)(2,1)}, bf16[256,18,32]{0,2,1:T(8,128)(2,1)S(1)}, u32[]{:S(2)}) copy-start(bf16[256,18,32]{0,2,1:T(8,128)(2,1)S(1)} %get-tuple-element.134) | copy-start | bytes 884740
  210.9 69.9 %copy-start.60 = (bf16[256,18,32]{0,2,1:T(8,128)(2,1)}, bf16[256,18,32]{0,2,1:T(8,128)(2,1)S(1)}, u32[]{:S(2)}) copy-start(bf16[256,18,32]{0,2,1:T(8,128)(2,1)S(1)} %get-tuple-element.135) | copy-start | bytes 884740
  280.8 11.0 %copy-start.32 = (bf16[1024,384]{0,1:T(8,128)(2,1)}, bf16[1024,384]{0,1:T(8,128)(2,1)S(1)}, u32[]{:S(2)}) copy-start(bf16[1024,384]{0,1:T(8,128)(2,1)S(1)} %get-tuple-element.121) | copy-start | bytes 2359300
  280.8 11.0 %copy-start.66 = (bf16[1024,384]{0,1:T(8,128)(2,1)}, bf16[1024,384]{0,1:T(8,128)(2,1)S(1)}, u32[]{:S(2)}) copy-start(bf16[1024,384]{0,1:T(8,128)(2,1)S(1)} %get-tuple-element.122) | copy-start | bytes 2359300
  291.7 8.1 copy-start.95
  309.4 16.7 %copy-start.25 = (bf16[256,1152]{1,0:T(8,128)(2,1)}, bf16[256,1152]{1,0:T(8,128)(2,1)S(1)}, u32[]{:S(2)}) copy-start(bf16[256,1152]{1,0:T(8,128)(2,1)S(1)} %multiply_convert_fusion.4.values_ref) | copy-start | bytes 1769476
  309.4 16.0 %copy-start.6 = (bf16[4608,2304]{1,0:T(8,128)(2,1)S(1)}, bf16[4608,2304]{1,0:T(8,128)(2,1)}, u32[]{:S(2)}) copy-start(bf16[4608,2304]{1,0:T(8,128)(2,1)} %all-gather.8.cloned.1.call-done) | copy-start | bytes 63700996
  311.8 14.9 %copy-start.34 = (f32[256,768]{1,0:T(8,128)}, f32[256,768]{1,0:T(8,128)S(1)}, u32[]{:S(2)}) copy-start(f32[256,768]{1,0:T(8,128)S(1)} %fusion.33) | copy-start | bytes 2359300
  314.9 11.9 %copy-start.36 = (f32[256,768]{1,0:T(8,128)}, f32[256,768]{1,0:T(8,128)S(1)}, u32[]{:S(2)}) copy-start(f32[256,768]{1,0:T(8,128)S(1)} %fusion.32) | copy-start | bytes 2359300
  318.0 8.8 copy-start.38
  320.5 6.3 copy-start.40
  331.9 47.7 %copy-start.115 = (f32[256]{0:T(256)}, f32[256]{0:T(256)S(1)}, u32[]{:S(2)}) copy-start(f32[256]{0:T(256)S(1)} %get-tuple-element.93) | copy-start | bytes 3076
  332.0 47.7 %copy-start.86 = (f32[256]{0:T(256)}, f32[256]{0:T(256)S(1)}, u32[]{:S(2)}) copy-start(f32[256]{0:T(256)S(1)} %fusion.98) | copy-start | bytes 3076
  332.0 47.7 %copy-start.45 = (bf16[8,144,1000]{2,1,0:T(8,128)(2,1)S(1)}, bf16[8,144,1000]{2,1,0:T(8,128)(2,1)}, u32[]{:S(2)}) copy-start(bf16[8,144,1000]{2,1,0:T(8,128)(2,1)} %fusion.20) | copy-start | bytes 6912004
  386.2 15.0 %copy-start.105 = (s32[1024]{0:T(1024)S(1)}, s32[1024]{0:T(1024)}, u32[]{:S(2)}) copy-start(s32[1024]{0:T(1024)} %param.29) | copy-start | bytes 12292
  401.8 8.0 copy-start.120
  401.8 8.0 copy-start.122
  409.8 35.4 %copy-start.87 = (f32[256]{0:T(256)S(1)}, f32[256]{0:T(256)}, u32[]{:S(2)}) copy-start(f32[256]{0:T(256)} %copy-done.86) | copy-start | bytes 3076
  409.8 35.4 %copy-start.108 = (s32[256]{0:T(256)S(1)}, s32[256]{0:T(256)}, u32[]{:S(2)}) copy-start(s32[256]{0:T(256)} %copy-done.106) | copy-start | bytes 3076
  409.8 35.4 %copy-start.125 = (s32[128]{0:T(128)S(1)}, s32[128]{0:T(128)}, u32[]{:S(2)}) copy-start(s32[128]{0:T(128)} %param.28) | copy-start | bytes 1540
  447.7 6.7 copy-start.50
  485.5 467.7 %reduce-scatter.5.cloned.1.call-start = ((), (), s32[]{:S(2)}) async-start(), calls=%async_computation.6 | async-start | bytes 7962624 | tf_op jit(solution)/shard_map/reduce_scatter | solution.py:882
  501.4 10.5 slice-start.1
  528.4 14.1 %copy-start.59 = (bf16[256,18,32]{0,2,1:T(8,128)(2,1)S(1)}, bf16[256,18,32]{0,2,1:T(8,128)(2,1)}, u32[]{:S(2)}) copy-start(bf16[256,18,32]{0,2,1:T(8,128)(2,1)} %copy-done.58) | copy-start | bytes 884740
  528.4 14.1 %copy-start.61 = (bf16[256,18,32]{0,2,1:T(8,128)(2,1)S(1)}, bf16[256,18,32]{0,2,1:T(8,128)(2,1)}, u32[]{:S(2)}) copy-start(bf16[256,18,32]{0,2,1:T(8,128)(2,1)} %copy-done.60) | copy-start | bytes 884740
  558.7 6.4 copy-start.33
  559.8 18.7 %collective-permute-start.12 = (bf16[256,768]{1,0:T(8,128)(2,1)}, bf16[256,768]{1,0:T(8,128)(2,1)}, u32[]{:S(2)}, u32[]{:S(2)}) collective-permute-start(bf16[256,768]{1,0:T(8,128)(2,1)} %get-tuple-element.119), channel_id=1, source_target_pairs={{0,1},{1,2},{2,3},{3,0},{4,5},{5,6},{6,7},{7,4},{8,9},{9,10},{10,1... | collective-permute-start | bytes 1179656 | tf_op jit(solution)/shard_map/ppermute | solution.py:706
  561.4 27.2 %collective-permute-start.11 = (bf16[256,768]{1,0:T(8,128)(2,1)}, bf16[256,768]{1,0:T(8,128)(2,1)}, u32[]{:S(2)}, u32[]{:S(2)}) collective-permute-start(bf16[256,768]{1,0:T(8,128)(2,1)} %get-tuple-element.120), channel_id=1, source_target_pairs={{0,2},{1,3},{2,0},{3,1},{4,6},{5,7},{6,4},{7,5},{8,10},{9,11},{10,... | collective-permute-start | bytes 1179656 | tf_op jit(solution)/shard_map/ppermute | solution.py:706
  563.7 7.2 copy-start.63
  563.7 7.2 copy-start.65
  563.7 24.9 %collective-permute-start.10 = (bf16[256,768]{1,0:T(8,128)(2,1)}, bf16[256,768]{1,0:T(8,128)(2,1)}, u32[]{:S(2)}, u32[]{:S(2)}) collective-permute-start(bf16[256,768]{1,0:T(8,128)(2,1)} %get-tuple-element.118), channel_id=1, source_target_pairs={{0,3},{1,0},{2,1},{3,2},{4,7},{5,4},{6,5},{7,6},{8,11},{9,8},{10,9... | collective-permute-start | bytes 1179656 | tf_op jit(solution)/shard_map/ppermute | solution.py:706
  571.2 7.4 copy-start.12
  590.4 10.0 copy-start.51
  591.4 9.1 copy-start.55
  627.6 11.0 %collective-permute-start.13 = (bf16[144,1000]{1,0:T(8,128)(2,1)S(1)}, bf16[144,1000]{1,0:T(8,128)(2,1)S(1)}, u32[]{:S(2)}, u32[]{:S(2)}) collective-permute-start(bf16[144,1000]{1,0:T(8,128)(2,1)S(1)} %get-tuple-element.103), channel_id=1, source_target_pairs={{0,28},{4,0},{8,4},{12,8},{16,12},{20,16},{24,20},{28,24},{1,29},{... | collective-permute-start | bytes 864008 | tf_op jit(solution)/shard_map/ppermute | solution.py:706
  629.4 13.0 %collective-permute-start.14 = (bf16[144,1000]{1,0:T(8,128)(2,1)S(1)}, bf16[144,1000]{1,0:T(8,128)(2,1)S(1)}, u32[]{:S(2)}, u32[]{:S(2)}) collective-permute-start(bf16[144,1000]{1,0:T(8,128)(2,1)S(1)} %get-tuple-element.102), channel_id=1, source_target_pairs={{0,24},{4,28},{8,0},{12,4},{16,8},{20,12},{24,16},{28,20},{1,25},{... | collective-permute-start | bytes 864008 | tf_op jit(solution)/shard_map/ppermute | solution.py:706
  635.1 9.4 collective-permute-start.15
  635.7 30.8 %collective-permute-start.16 = (bf16[144,1000]{1,0:T(8,128)(2,1)S(1)}, bf16[144,1000]{1,0:T(8,128)(2,1)S(1)}, u32[]{:S(2)}, u32[]{:S(2)}) collective-permute-start(bf16[144,1000]{1,0:T(8,128)(2,1)S(1)} %get-tuple-element.100), channel_id=1, source_target_pairs={{0,16},{4,20},{8,24},{12,28},{16,0},{20,4},{24,8},{28,12},{1,17},{... | collective-permute-start | bytes 864008 | tf_op jit(solution)/shard_map/ppermute | solution.py:706
  636.4 34.3 %collective-permute-start.17 = (bf16[144,1000]{1,0:T(8,128)(2,1)S(1)}, bf16[144,1000]{1,0:T(8,128)(2,1)S(1)}, u32[]{:S(2)}, u32[]{:S(2)}) collective-permute-start(bf16[144,1000]{1,0:T(8,128)(2,1)S(1)} %get-tuple-element.99), channel_id=1, source_target_pairs={{0,12},{4,16},{8,20},{12,24},{16,28},{20,0},{24,4},{28,8},{1,13},{... | collective-permute-start | bytes 864008 | tf_op jit(solution)/shard_map/ppermute | solution.py:706
  638.6 32.1 %collective-permute-start.18 = (bf16[144,1000]{1,0:T(8,128)(2,1)S(1)}, bf16[144,1000]{1,0:T(8,128)(2,1)S(1)}, u32[]{:S(2)}, u32[]{:S(2)}) collective-permute-start(bf16[144,1000]{1,0:T(8,128)(2,1)S(1)} %get-tuple-element.98), channel_id=1, source_target_pairs={{0,8},{4,12},{8,16},{12,20},{16,24},{20,28},{24,0},{28,4},{1,9},{5... | collective-permute-start | bytes 864008 | tf_op jit(solution)/shard_map/ppermute | solution.py:706
  642.4 28.4 %collective-permute-start.19 = (bf16[144,1000]{1,0:T(8,128)(2,1)S(1)}, bf16[144,1000]{1,0:T(8,128)(2,1)S(1)}, u32[]{:S(2)}, u32[]{:S(2)}) collective-permute-start(bf16[144,1000]{1,0:T(8,128)(2,1)S(1)} %get-tuple-element.97), channel_id=1, source_target_pairs={{0,4},{4,8},{8,12},{12,16},{16,20},{20,24},{24,28},{28,0},{1,5},{5... | collective-permute-start | bytes 864008 | tf_op jit(solution)/shard_map/ppermute | solution.py:706
  763.5 16.1 %copy-start.85 = (f32[3,1152]{1,0:T(4,128)S(1)}, f32[3,1152]{1,0:T(4,128)}, u32[]{:S(2)}) copy-start(f32[3,1152]{1,0:T(4,128)} %param.32) | copy-start | bytes 41476
  763.5 16.1 %copy-start.99 = (f32[3,1152]{1,0:T(4,128)S(1)}, f32[3,1152]{1,0:T(4,128)}, u32[]{:S(2)}) copy-start(f32[3,1152]{1,0:T(4,128)} %param.39) | copy-start | bytes 41476
  763.5 16.1 %copy-start.100 = (f32[3,1152]{1,0:T(4,128)S(1)}, f32[3,1152]{1,0:T(4,128)}, u32[]{:S(2)}) copy-start(f32[3,1152]{1,0:T(4,128)} %param.38) | copy-start | bytes 41476
  957.3 77.1 %slice-start = ((f32[144,8192]{1,0:T(8,128)}), f32[144,8000]{1,0:T(8,128)S(1)}, s32[]{:S(2)}) async-start(f32[144,8192]{1,0:T(8,128)} %shard_map.358), calls=%async_computation.7 | async-start | bytes 9289728 | tf_op jit(solution)/shard_map/slice | solution.py:1062
  1034.4 10.0 copy-start.71
  1034.4 10.0 copy-start.72
  1034.4 10.0 copy-start.73
  (94 other events, 235.6 us)
Sparse Core Ops, SparseCore 0:
  11.5 87.6 all-gather.5
  102.7 188.5 all-gather.7
  293.2 86.6 all-gather.9
  485.6 137.4 reduce-scatter.2
  626.5 87.6 reduce-scatter.4

commit v3 on v2

--- a/solution.py
+++ b/solution.py
@@ -25,6 +25,7 @@
 VMEM_LIMIT = 58 * 2**20
 VOCAB_TILE = 1024
 LOOK_STEP = 32
+TILES_AT_ONCE = 3
 SMALL_BLOCK = 384
 
 
@@ -243,13 +244,115 @@
     return out.reshape(count, width)
 
 
-def flipped(index, entry):
-    bit = 1
-    while bit <= entry:
-        if entry & bit:
-            index = index + bit * (1 - 2 * (index // bit % 2))
-        bit *= 2
-    return index
+def line_peers(row, col, cols):
+    return [(row, (col + 1) % cols), (row, (col + cols - 1) % cols)]
+
+
+def line_ways(place):
+    row, col, cols = place
+    return ((0, col), (1, cols - 1 - col))
+
+
+def line_copy(place, down, source, target, sems, at, step):
+    row, col, cols = place
+    slot = at + down * (cols - 1) + step
+    return pltpu.make_async_remote_copy(
+        src_ref=source,
+        dst_ref=target,
+        send_sem=sems.at[0, slot],
+        recv_sem=sems.at[1, slot],
+        device_id=(row, (col + (cols - 1 if down else 1)) % cols),
+        device_id_type=MESH,
+    )
+
+
+def line_sum(place, term, work, inbox, at, sems, sem_at, result):
+    row, col, cols = place
+
+    def block_of(down, step):
+        return jnp.clip(step - (cols - 1 - col) if down else cols - 1 - step + col, 0, cols - 1)
+
+    def copy_of(down, step):
+        landing = inbox.at[at + down * (cols - 1) + step]
+        return line_copy(place, down, work.at[block_of(down, step)], landing, sems, sem_at, step)
+
+    for step in range(cols - 1):
+        for down, index in line_ways(place):
+            d = block_of(down, step)
+
+            @pl.when(index == 0)
+            def _(d=d, down=down, step=step):
+                if term is not None:
+                    work[d] = term(d)
+                copy_of(down, step).start()
+
+            if step > 0:
+                @pl.when((index > 0) & (index <= step))
+                def _(d=d, down=down, step=step):
+                    copy_of(down, step - 1).wait_recv()
+                    arrived = inbox[at + down * (cols - 1) + step - 1]
+                    own = work[d] if term is None else term(d)
+                    work[d] = (own.astype(jnp.float32) + arrived.astype(jnp.float32)).astype(work.dtype)
+                    copy_of(down, step).start()
+
+        yield
+    own = work[col] if term is None else term(col)
+    result[...] = own.astype(result.dtype)
+    for down, index in line_ways(place):
+        @pl.when(index > 0)
+        def _(down=down):
+            copy_of(down, cols - 2).wait_recv()
+            arrived = inbox[at + down * (cols - 1) + cols - 2]
+            result[...] = (result[...].astype(jnp.float32) + arrived.astype(jnp.float32)).astype(result.dtype)
+
+    for step in range(cols - 1):
+        for down, index in line_ways(place):
+            @pl.when(index <= step)
+            def _(down=down, step=step):
+                copy_of(down, step).wait_send()
+
+
+def line_spread(place, block, sems, sem_at):
+    row, col, cols = place
+
+    def copy_of(down, step):
+        lies = block(jnp.clip(col + step if down else col - step, 0, cols - 1))
+        return line_copy(place, down, lies, lies, sems, sem_at, step)
+
+    for step in range(cols):
+        if step > 0:
+            for down, index in line_ways(place):
+                @pl.when(index >= step)
+                def _(down=down, step=step):
+                    copy_of(down, step - 1).wait_recv()
+
+        if step < cols - 1:
+            for down, index in line_ways(place):
+                @pl.when((index >= step) & (index < cols - 1))
+                def _(down=down, step=step):
+                    copy_of(down, step).start()
+
+            yield
+    for step in range(cols - 1):
+        for down, index in line_ways(place):
+            @pl.when((index >= step) & (index < cols - 1))
+            def _(down=down, step=step):
+                copy_of(down, step).wait_send()
+
+
+def swap_go(place, part_of, lies_at, sems, local_sem):
+    row, col, rows, cols = place
+    own = pltpu.make_async_copy(part_of(row), lies_at(row), local_sem)
+    own.start()
+    copies = [
+        push(part_of((row + k) % rows), lies_at(row), (sems.at[0], sems.at[1]), k - 1, ((row + k) % rows, col))
+        for k in range(1, rows)
+    ]
+    for _ in range(2 * cols):
+        yield
+    own.wait()
+    for copy in copies:
+        copy.wait()
 
 
 class Matrix:
@@ -259,96 +362,35 @@
         (
             self.mean, self.square, self.weight, self.left,
             self.next, self.moment, self.scale,
-            self.sums, self.work, self.inbox, self.steps, self.whole, self.sems, self.row_sems, self.core_sems,
+            self.work, self.inbox, self.sum, self.total, self.whole, self.sems, self.row_sems, self.core_sems,
         ) = refs
         self.adds_weight = adds_weight
-        self.levels = [1 << k for k in range(self.cols.bit_length() - 1)]
-        self.slot = 0
-        self.started = []
-        self.pending = []
-
-    def send(self, source, target, bit):
-        peer = (self.row, flipped(self.col, bit))
-        slot = self.slot
-        self.slot += 1
-        copy = push(source, target, (self.sems.at[0], self.sems.at[1]), slot, peer)
-        self.started.append(copy)
-        return copy
-
-    def arrive(self):
-        for copy in self.pending:
-            copy.wait_recv()
-        self.pending = []
-
-    def halving(self, phase):
-        entries = list(range(self.cols))
-        place = phase * (self.cols - 1)
-        first = True
-        for bit in self.levels:
-            gone = [e for e in entries if e & bit]
-            entries = [e for e in entries if not e & bit]
-            for k, e in enumerate(gone):
-                if first and phase == 0:
-                    source = self.grad(e)
-                elif first:
-                    self.multiply(e)
-                    source = self.work.at[e]
-                else:
-                    source = self.sums.at[e // 2] if phase == 0 else self.work.at[e]
-                self.pending.append(self.send(source, self.inbox.at[place + k], bit))
-            if first and phase == 1:
-                for e in entries:
-                    self.multiply(e)
-            yield
-            self.arrive()
-            for k, e in enumerate(gone):
-                mine = e - bit
-                if first and phase == 0:
-                    held = self.grad(mine)[...]
-                else:
-                    held = self.sums[mine // 2] if phase == 0 else self.work[mine]
-                self.total = held.astype(jnp.float32) + self.inbox[place + k].astype(jnp.float32)
-                if phase == 0:
-                    self.sums[mine // 2] = self.total.astype(self.sums.dtype)
-                elif bit != self.levels[-1]:
-                    self.work[mine] = self.total.astype(self.work.dtype)
-            place += len(gone)
-            first = False
-
-    def multiply(self, e):
-        self.work[e] = jnp.dot(
-            self.sums[0],
-            self.basis(e),
-            preferred_element_type=jnp.float32,
-        ).astype(self.work.dtype)
 
     def go(self):
-        yield from self.halving(0)
-        yield from self.halving(1)
-        rotated = self.total
+        line = (self.row, self.col, self.cols)
+        links = 2 * (self.cols - 1)
+        yield from line_sum(
+            line, lambda d: self.grad(d)[...], self.work, self.inbox, 0, self.sems, 0, self.sum
+        )
+        for d in range(self.cols):
+            self.work[d] = jnp.dot(
+                self.sum[...], self.basis(d), preferred_element_type=jnp.float32
+            ).astype(self.work.dtype)
+        yield from line_sum(line, None, self.work, self.inbox, links, self.sems, links, self.total)
+        rotated = self.total[...]
         moment = MOMENT_BETA * self.mean[...] + (1.0 - MOMENT_BETA) * rotated
         scale = MOMENT_BETA * self.square[...] + (1.0 - MOMENT_BETA) * rotated * rotated
         self.moment[...] = moment
         self.scale[...] = scale
-        self.steps[0] = (moment / (jnp.sqrt(scale) + ADAM_EPSILON)).astype(self.steps.dtype)
-        arriving = [(0, None)]
+        steps = self.inbox
+        steps[self.col] = (moment / (jnp.sqrt(scale) + ADAM_EPSILON)).astype(steps.dtype)
+        yield from line_spread(line, lambda d: steps.at[d], self.sems, 2 * links)
         back = None
-        while arriving:
-            e, arrived = arriving.pop(0)
-            if arrived is not None:
-                arrived.wait_recv()
-            for bit in reversed(self.levels):
-                if e % (2 * bit) == 0:
-                    copy = self.send(self.steps.at[e], self.steps.at[e + bit], bit)
-                    arriving.append((e + bit, copy))
+        for d in range(self.cols):
             term = lax.dot_general(
-                self.steps[e],
-                self.basis(e),
-                (((1,), (1,)), ((), ())),
-                preferred_element_type=jnp.float32,
+                steps[d], self.basis(d), (((1,), (1,)), ((), ())), preferred_element_type=jnp.float32
             )
             back = term if back is None else back + term
-            yield
         self.whole[self.row] = back.astype(self.whole.dtype)
         half = self.rows // 2
         other = (self.row // 2 * 2 + 1 - self.row % 2, self.col)
@@ -359,14 +401,11 @@
         ]
         core_sems = (self.core_sems.at[0], self.core_sems.at[1])
         between = [push(own, own, core_sems, 0, other)]
-        self.started += across + between
         yield
         for k in range(1, half):
             across[k - 1].wait_recv()
             block = self.whole.at[(self.row + self.rows - 2 * k) % self.rows]
-            copy = push(block, block, core_sems, k, other)
-            between.append(copy)
-            self.started.append(copy)
+            between.append(push(block, block, core_sems, k, other))
         yield
         for copy in between:
             copy.wait_recv()
@@ -376,7 +415,7 @@
         weight = self.weight[...]
         change = -(SOAP_RATE * (update + WEIGHT_DECAY * weight))
         self.next[...] = weight + change if self.adds_weight else change
-        for copy in self.started:
+        for copy in across + between:
             copy.wait_send()
 
 
@@ -386,13 +425,17 @@
 
 def soap_kernel(rows, cols, adds, streamed, *refs):
     row, col = lax.axis_index("row"), lax.axis_index("col")
-    peers = [(row, flipped(col, 1 << k)) for k in range(cols.bit_length() - 1)]
-    greet(peers + same_core(row, col, rows) + [(row // 2 * 2 + 1 - row % 2, col)])
+    place = (row, col, rows, cols)
+    greet(line_peers(row, col, cols) + [((row + k) % rows, col) for k in range(1, rows)])
     count = len(adds)
     shared = 1 if streamed else count
     grads, bases, refs = refs[:shared], refs[shared : 2 * shared], refs[2 * shared :]
     inputs, refs = refs[: 4 * count], refs[4 * count :]
+    extra = 1 if streamed else 4
+    others_in, refs = refs[:extra], refs[extra:]
     outputs, refs = refs[: 3 * count], refs[3 * count :]
+    extra = 1 if streamed else 2
+    others_out, refs = refs[:extra], refs[extra:]
     scratch, refs = refs[: 8 * count], refs[8 * count :]
     running = []
     loads = []
@@ -401,17 +444,17 @@
         others = inputs[4 * m : 4 * m + 4]
         width = others[0].shape[1]
         if streamed:
-            held, stage, load_sems = refs
-
-            def grad_of(e, grad=grad, m=m, width=width):
-                at = pl.multiple_of((streamed.index(m) * cols + flipped(col, e)) * width, width)
+            held, stage, load_sems = refs[:3]
+
+            def grad_of(d, grad=grad, m=m, width=width):
+                at = pl.multiple_of((streamed.index(m) * cols + d) * width, width)
                 return grad.at[:, pl.ds(at, width)]
 
-            def basis_of(e, held=held, m=m):
-                return held[m, e]
-
-            for e in [*range(1, cols, 2), *range(2, cols, 2), 0]:
-                at = pl.multiple_of(flipped(col, e) * width, width)
+            def basis_of(d, held=held, m=m):
+                return held[m, d]
+
+            for e in range(cols):
+                at = e * width
                 for part in range(2):
                     lines = pl.ds(part * (width // 2), width // 2)
                     copy = pltpu.make_async_copy(
@@ -420,19 +463,31 @@
                     loads.append((copy, part, m, e))
         else:
 
-            def grad_of(e, grad=grad):
-                return grad.at[flipped(col, e)]
-
-            def basis_of(e, basis=basis):
-                return basis[flipped(col, e)]
+            def grad_of(d, grad=grad):
+                return grad.at[d]
+
+            def basis_of(d, basis=basis):
+                return basis[d]
 
         refs_of = (*others, *outputs[3 * m : 3 * m + 3], *scratch[8 * m : 8 * m + 8])
-        running.append(Matrix((row, col, rows, cols), grad_of, basis_of, refs_of, add).go())
+        running.append(Matrix(place, grad_of, basis_of, refs_of, add).go())
     if streamed:
         running = [running[m] for m in streamed]
         loads = [load for m in streamed for load in loads if load[2] == m]
         for copy, *unused in loads[:2]:
             copy.start()
+    if streamed:
+        count = others_in[0].shape[2]
+
+        def lies_at(k):
+            return others_out[0].at[:, pl.ds(pl.multiple_of(k * count, count), count)]
+
+        running.append(swap_go(place, lambda k: others_in[0].at[k], lies_at, *refs[3:]))
+    else:
+        running = [
+            scatter_go(place, *others_in[:3], others_out[0], *refs[:3]),
+            share_go(place, others_in[3], others_out[1], *refs[3:]),
+        ] + running
     for m in running:
         next(m)
     for k, (copy, slot, m, e) in enumerate(loads):
@@ -445,7 +500,7 @@
         running = [m for m in running if next(m, "done") != "done"]
 
 
-def soap(grads, bases, matrices, adds, streamed, collective_id):
+def soap(grads, bases, matrices, adds, streamed, others, collective_id):
     rows, cols = lax.axis_size("row"), lax.axis_size("col")
     dma = pltpu.SemaphoreType.DMA
     vmem = pl.BlockSpec(memory_space=pltpu.VMEM)
@@ -454,12 +509,12 @@
         outs += [jax.ShapeDtypeStruct(weight.shape, jnp.float32)] * 3
         block = weight.shape
         scratch += [
-            pltpu.VMEM((cols // 2, *block), left.dtype),
             pltpu.VMEM((cols, *block), left.dtype),
-            pltpu.VMEM((2 * (cols - 1), *block), left.dtype),
-            pltpu.VMEM((cols, *block), left.dtype),
+            pltpu.VMEM((4 * (cols - 1), *block), left.dtype),
+            pltpu.VMEM(block, left.dtype),
+            pltpu.VMEM(block, jnp.float32),
             pltpu.VMEM((rows, *block), left.dtype),
-            dma((2, 3 * (cols - 1))),
+            dma((2, 6 * (cols - 1))),
             dma((2, rows // 2 - 1)),
             dma((2, rows // 2)),
         ]
@@ -470,19 +525,35 @@
             pltpu.VMEM((2, width // 2, width), jnp.float32),
             dma((2,)),
         ]
+    anywhere = pl.BlockSpec(memory_space=pl.ANY)
+    other_spec = anywhere if streamed else vmem
+    out_specs = [vmem] * len(outs) + [other_spec] * (1 if streamed else 2)
+    if streamed:
+        parts, depth, count = others[0].shape
+        outs += [jax.ShapeDtypeStruct((depth, parts * count), others[0].dtype)]
+        scratch += [dma((2, rows - 1)), dma]
+    else:
+        ids, grad, base, own = others
+        outs += [
+            jax.ShapeDtypeStruct(base.shape, jnp.float32),
+            jax.ShapeDtypeStruct((rows, cols, *own.shape), own.dtype),
+        ]
+        scratch += [pltpu.VMEM((cols, *grad.shape), grad.dtype)]
+        scratch += [dma((2, 2 * (cols - 1))), dma((2, rows - 1))] * 2
     got = pl.pallas_call(
         functools.partial(soap_kernel, rows, cols, adds, streamed),
         out_shape=outs,
         in_specs=[vmem] * len(grads)
-        + [pl.BlockSpec(memory_space=pl.ANY) if streamed else vmem] * len(bases)
-        + [vmem] * (4 * len(matrices)),
-        out_specs=[vmem] * len(outs),
+        + [anywhere if streamed else vmem] * len(bases)
+        + [vmem] * (4 * len(matrices))
+        + [other_spec] * len(others),
+        out_specs=out_specs,
         scratch_shapes=scratch,
         compiler_params=pltpu.CompilerParams(
             collective_id=collective_id, has_side_effects=True, vmem_limit_bytes=VMEM_LIMIT
         ),
-    )(*grads, *bases, *[part for matrix in matrices for part in matrix])
-    return [got[k * 3 : k * 3 + 3] for k in range(len(matrices))]
+    )(*grads, *bases, *[part for matrix in matrices for part in matrix], *others)
+    return [got[k * 3 : k * 3 + 3] for k in range(len(matrices))] + list(got[3 * len(matrices) :])
 
 
 def outer_kernel(values_ref, left_ref, other_ref, *refs):
@@ -534,11 +605,20 @@
     return jnp.where(ids - first == columns, 1.0, 0.0).astype(jnp.bfloat16)
 
 
-def lookup_kernel(rows, cols, ids_ref, table_ref, out_ref, table, taken, found, inbox, sems, row_sems):
+def lookup_kernel(
+    rows, cols, ids_ref, table_ref, weight_ref, out_ref, whole_ref,
+    table, taken, found, inbox, summed_ref, sems, row_sems, local_sem, col_sems, chip_sems, core_sems,
+):
     row, col = lax.axis_index("row"), lax.axis_index("col")
-    levels = [1 << k for k in range(cols.bit_length() - 1)]
     row_peers = [((row + k) % rows, col) for k in range(1, rows)]
-    greet([(row, flipped(col, bit)) for bit in levels] + row_peers)
+    other = (row // 2 * 2 + 1 - row % 2, col)
+    line = (row, col, cols)
+    greet(line_peers(row, col, cols) + row_peers)
+    own = pltpu.make_async_copy(weight_ref, whole_ref.at[col, row], local_sem)
+    own.start()
+    own.wait()
+    spreading = line_spread(line, lambda d: whole_ref.at[d, row], col_sems, 0)
+    next(spreading)
     features, tokens = out_ref.shape[1:]
     planes = [(k, min(128, features - 128 * k)) for k in range(table.shape[1])]
 
@@ -552,7 +632,7 @@
     lax.fori_loop(0, table_ref.shape[1] // 128, turn, 0)
 
     def look(e):
-        source = flipped(col, e) * rows
+        source = e * rows
 
         def block(k, carry):
             start = (source + k) * tokens
@@ -570,38 +650,42 @@
 
         lax.fori_loop(0, rows, block, 0)
 
-    entries = list(range(cols))
-    started, slot = [], 0
-    for bit in levels:
-        gone = [e for e in entries if e & bit]
-        entries = [e for e in entries if not e & bit]
-        copies = []
-        for e in gone:
-            if bit == 1:
-                look(e)
-            peer = (row, flipped(col, bit))
-            copies.append(push(found.at[e], inbox.at[slot], (sems.at[0], sems.at[1]), slot, peer))
-            slot += 1
-        if bit == 1:
-            for e in reversed(entries):
-                look(e)
-        for k, e in enumerate(gone):
-            copies[k].wait_recv()
-            at = slot - len(gone) + k
-            found[e - bit] = found[e - bit] + inbox[at]
-        started += copies
-    out_ref[row] = found[0, row]
+    orders = [sorted(range(cols), key=lambda d, i=i: -abs(d - i)) for i in range(cols)]
+    summing = line_sum(line, None, found, inbox, 0, sems, 0, summed_ref)
+    for k in range(cols - 1):
+        e = jnp.int32(orders[0][k])
+        for i in range(1, cols):
+            e = jnp.where(col == i, orders[i][k], e)
+        look(e)
+        next(summing)
+        next(spreading, None)
+    for unused in spreading:
+        pass
+    mine = whole_ref.at[:, row]
+    chips = [
+        push(mine, mine, (chip_sems.at[0], chip_sems.at[1]), k - 1, peer)
+        for k, peer in enumerate(same_core(row, col, rows), 1)
+    ]
+    core = [push(mine, mine, (core_sems.at[0], core_sems.at[1]), 0, other)]
+    look(col)
+    for unused in summing:
+        pass
+    out_ref[row] = summed_ref[row]
     copies = [
-        push(found.at[0, peer[0]], out_ref.at[row], (row_sems.at[0], row_sems.at[1]), k, peer)
+        push(summed_ref.at[peer[0]], out_ref.at[row], (row_sems.at[0], row_sems.at[1]), k, peer)
         for k, peer in enumerate(row_peers)
     ]
-    for copy in copies:
+    for k, arrived in enumerate(chips, 1):
+        arrived.wait_recv()
+        block = whole_ref.at[:, (row + rows - 2 * k) % rows]
+        core.append(push(block, block, (core_sems.at[0], core_sems.at[1]), k, other))
+    for copy in copies + core:
         copy.wait_recv()
-    for copy in copies + started:
+    for copy in copies + core + chips:
         copy.wait_send()
 
 
-def lookup(ids, table, tokens, collective_id):
+def lookup(ids, table, weight, tokens, collective_id):
     rows, cols = lax.axis_size("row"), lax.axis_size("col")
     features, count = table.shape
     planes = -(-features // 128)
@@ -610,95 +694,127 @@
     block = (rows, features, tokens)
     return pl.pallas_call(
         functools.partial(lookup_kernel, rows, cols),
-        out_shape=jax.ShapeDtypeStruct(block, table.dtype),
-        in_specs=[pl.BlockSpec(memory_space=pltpu.SMEM), vmem],
-        out_specs=vmem,
+        out_shape=[
+            jax.ShapeDtypeStruct(block, table.dtype),
+            jax.ShapeDtypeStruct((cols, rows, *weight.shape), weight.dtype),
+        ],
+        in_specs=[pl.BlockSpec(memory_space=pltpu.SMEM), vmem, pl.BlockSpec(memory_space=pl.ANY)],
+        out_specs=[vmem, pl.BlockSpec(memory_space=pl.ANY)],
         scratch_shapes=[
             pltpu.VMEM((count, planes, 128), jnp.float32),
             pltpu.VMEM((tokens, planes, 128), jnp.float32),
             pltpu.VMEM((cols, *block), table.dtype),
-            pltpu.VMEM((cols - 1, *block), table.dtype),
-            dma((2, cols - 1)),
+            pltpu.VMEM((2 * (cols - 1), *block), table.dtype),
+            pltpu.VMEM(block, table.dtype),
+            dma((2, 2 * (cols - 1))),
             dma((2, rows - 1)),
+            dma,
+            dma((2, 2 * (cols - 1))),
+            dma((2, rows // 2 - 1)),
+            dma((2, rows // 2)),
         ],
         compiler_params=pltpu.CompilerParams(
             collective_id=collective_id, has_side_effects=True, vmem_limit_bytes=VMEM_LIMIT
         ),
-    )(ids, table)
-
-
-def scatter_kernel(
-    rows, cols, ids_ref, grad_ref, base_ref, out_ref, held, sems, row_sems
-):
-    row, col = lax.axis_index("row"), lax.axis_index("col")
-    levels = [1 << k for k in range(cols.bit_length() - 1)]
+    )(ids, table, weight)
+
+
+def scatter_go(place, ids_ref, grad_ref, base_ref, out_ref, held, sems, row_sems):
+    row, col, rows, cols = place
     row_peers = [((row + k) % rows, col) for k in range(1, rows)]
-    greet([(row, flipped(col, bit)) for bit in levels] + row_peers)
-    held[0, row] = grad_ref[row]
-    copies = [
-        push(grad_ref.at[peer[0]], held.at[0, row], (row_sems.at[0], row_sems.at[1]), k, peer)
+    held[col, row] = grad_ref[row]
+    started = [
+        push(grad_ref.at[peer[0]], held.at[col, row], (row_sems.at[0], row_sems.at[1]), k, peer)
         for k, peer in enumerate(row_peers)
     ]
-    count = out_ref.shape[1]
-
-    def place(e, first_time):
-        source = flipped(col, e)
-
-        def block(v, carry):
+    tiles = out_ref.shape[1] // VOCAB_TILE
+
+    def tile_of(d, source_ref):
+        def tile(v, carry):
             first = pl.multiple_of(v * VOCAB_TILE, VOCAB_TILE)
-            total = base_ref[:, pl.ds(first, VOCAB_TILE)] if first_time else out_ref[:, pl.ds(first, VOCAB_TILE)]
+            total = source_ref[:, pl.ds(first, VOCAB_TILE)].astype(jnp.float32)
             for k in range(rows):
                 total = total + lax.dot_general(
-                    held[e, k],
-                    one_hot_tile(ids_ref[source, k], first, VOCAB_TILE),
+                    held[d, k],
+                    one_hot_tile(ids_ref[d, k], first, VOCAB_TILE),
                     (((1,), (0,)), ((), ())),
                     preferred_element_type=jnp.float32,
                 )
             out_ref[:, pl.ds(first, VOCAB_TILE)] = total
             return carry
 
-        lax.fori_loop(0, count // VOCAB_TILE, block, 0)
-
-    for copy in copies:
+        return tile
+
+    yield
+    for copy in started:
         copy.wait_recv()
-    started = list(copies)
-    arriving, slot = [(0, None)], 0
-    while arriving:
-        e, arrived = arriving.pop(0)
-        if arrived is not None:
-            arrived.wait_recv()
-        for bit in reversed(levels):
-            if e % (2 * bit) == 0:
-                copy = push(
-                    held.at[e], held.at[e + bit], (sems.at[0], sems.at[1]), slot,
-                    (row, flipped(col, bit)),
-                )
-                slot += 1
-                started.append(copy)
-                arriving.append((e + bit, copy))
-        place(e, e == 0)
+    spreading = line_spread((row, col, cols), lambda d: held.at[d], sems, 0)
+    next(spreading)
+    for first in range(0, tiles, TILES_AT_ONCE):
+        lax.fori_loop(first, min(tiles, first + TILES_AT_ONCE), tile_of(col, base_ref), 0)
+        next(spreading, None)
+        yield
+    for unused in spreading:
+        yield
+    for k in range(1, cols):
+        for first in range(0, tiles, TILES_AT_ONCE):
+            lax.fori_loop(
+                first, min(tiles, first + TILES_AT_ONCE), tile_of((col + k) % cols, out_ref), 0
+            )
+            yield
     for copy in started:
         copy.wait_send()
 
 
-def scatter(ids, grad, base, collective_id):
+def share_go(place, x_ref, out_ref, sems, row_sems):
+    row, col, rows, cols = place
+    out_ref[row, col] = x_ref[...]
+    yield from line_spread((row, col, cols), lambda d: out_ref.at[row, d], sems, 0)
+    copies = [
+        push(out_ref.at[row], out_ref.at[row], (row_sems.at[0], row_sems.at[1]), k - 1, ((row + k) % rows, col))
+        for k in range(1, rows)
+    ]
+    yield
+    for copy in copies:
+        copy.wait()
+
+
+def gather_kernel(rows, cols, x_ref, table_ref, out_ref, swapped_ref, sems, row_sems, local_sem):
+    row, col = lax.axis_index("row"), lax.axis_index("col")
+    greet(line_peers(row, col, cols) + [((row + k) % rows, col) for k in range(1, rows)])
+    out_ref[col] = x_ref[...]
+    spreading = line_spread((row, col, cols), lambda d: out_ref.at[d], sems, 0)
+    next(spreading)
+    count = swapped_ref.shape[2]
+
+    def part_of(k):
+        return table_ref.at[:, pl.ds(pl.multiple_of(k * count, count), count)]
+
+    swapping = swap_go((row, col, rows, cols), part_of, lambda k: swapped_ref.at[k], row_sems, local_sem)
+    next(swapping)
+    for unused in spreading:
+        pass
+    for unused in swapping:
+        pass
+
+
+def gather(value, table, collective_id):
     rows, cols = lax.axis_size("row"), lax.axis_size("col")
     dma = pltpu.SemaphoreType.DMA
-    vmem = pl.BlockSpec(memory_space=pltpu.VMEM)
+    vmem, anywhere = pl.BlockSpec(memory_space=pltpu.VMEM), pl.BlockSpec(memory_space=pl.ANY)
     return pl.pallas_call(
-        functools.partial(scatter_kernel, rows, cols),
-        out_shape=jax.ShapeDtypeStruct(base.shape, jnp.float32),
-        in_specs=[vmem] * 3,
-        out_specs=vmem,
-        scratch_shapes=[
-            pltpu.VMEM((cols, *grad.shape), grad.dtype),
-            dma((2, cols - 1)),
-            dma((2, rows - 1)),
+        functools.partial(gather_kernel, rows, cols),
+        out_shape=[
+            jax.ShapeDtypeStruct((cols, *value.shape), value.dtype),
+            jax.ShapeDtypeStruct((rows, table.shape[0], table.shape[1] // rows), table.dtype),
         ],
+        in_specs=[vmem, anywhere],
+        out_specs=[vmem, anywhere],
+        scratch_shapes=[dma((2, 2 * (cols - 1))), dma((2, rows - 1)), dma],
         compiler_params=pltpu.CompilerParams(
             collective_id=collective_id, has_side_effects=True, vmem_limit_bytes=VMEM_LIMIT
         ),
-    )(ids, grad, base)
+    )(value, table)
 
 
 def send(value, axis, shift):
@@ -831,18 +947,13 @@
     group_size = Q_HEADS // KV_HEADS
     scaling = HEAD ** (-0.5)
     qkv_cols, out_cols, ff_cols = qkv_weight.shape[1], output_weight.shape[1], mlp_weight.shape[2]
-    vocab_part = vocab_shard // row_count
+    vocab_part = -(-(vocab_shard + 1) // (128 * row_count)) * 128
+    vocab_room = vocab_part * row_count
 
     ids_all = lax.all_gather(jnp.concatenate([token_ids, target_ids]), "row", axis=0)
-    table_first, left_first, ids_all = lax.optimization_barrier((embed_table, left_bases, ids_all))
+    table_first, ids_all = lax.optimization_barrier((embed_table, ids_all))
 
     qkv_width, ff_width = qkv_cols * col_count, ff_cols * col_count
-    attn_full = lax.all_gather(
-        jnp.concatenate([qkv_weight.astype(low), output_weight.astype(low)], axis=1),
-        ("col", "row"),
-        axis=0,
-        tiled=True,
-    ).reshape(col_count, width, qkv_cols + out_cols)
     mlp_low = mlp_weight.astype(low)
     mlp_full = lax.all_gather(
         jnp.concatenate([mlp_low[0], mlp_low[1], mlp_low[2]], axis=1),
@@ -850,12 +961,9 @@
         axis=0,
         tiled=True,
     ).reshape(col_count, width, 3 * ff_cols)
-    bases_low = left_first.astype(low)
+    bases_low = left_bases.astype(low)
     left_block = jnp.concatenate([bases_low[k] for k in range(5)], axis=1)
-    left_full = lax.all_gather(left_block, "row", axis=0, tiled=True)
     columns = range(col_count)
-    qkv_full = [attn_full[c, :, :qkv_cols] for c in columns]
-    out_full = [attn_full[c, :, qkv_cols:] for c in columns]
     gate_full, up_full, down_full = (
         [mlp_full[c, :, k * ff_cols : (k + 1) * ff_cols] for c in columns] for k in range(3)
     )
@@ -881,16 +989,13 @@
     def reduce_rows(values):
         return lax.psum_scatter(values, "row", scatter_dimension=0, tiled=True)
 
-    padded = jnp.pad(table_low_t, ((0, 0), (0, 128 - vocab_shard % 128)))
-    found = lookup(local_tokens.reshape(-1), padded, device_tokens, 6)
-    table_later, found = lax.optimization_barrier((table_low_t, found))
+    padded = jnp.pad(table_low_t, ((0, 0), (0, vocab_room - vocab_shard)))
+    attn_block = jnp.concatenate([qkv_weight.astype(low), output_weight.astype(low)], axis=1)
+    found, attn_full = lookup(local_tokens.reshape(-1), padded, attn_block, device_tokens, 6)
+    attn_full = attn_full.reshape(col_count, width, qkv_cols + out_cols)
+    qkv_full = [attn_full[c, :, :qkv_cols] for c in columns]
+    out_full = [attn_full[c, :, qkv_cols:] for c in columns]
     embedded = found.reshape(width, device_tokens).T.astype(jnp.float32)
-
-    table_parts = jnp.moveaxis(table_later.reshape(features, row_count, vocab_part), 1, 0)
-    part_pieces = [
-        pick_block(table_parts, (row_index + k) % row_count, 0) for k in range(row_count)
-    ]
-    table_part = to_absolute(deliver(part_pieces, "row", 1), row_index).reshape(width, vocab_part)
 
     normed = rms_norm(embedded, norm_gains[0]).astype(low)
     project = by_columns(normed, qkv_full, matmul).astype(low)
@@ -911,18 +1016,15 @@
     )
     queries = rotate_here(queries_raw).astype(low).reshape(device_tokens, KV_HEADS, group_size, HEAD)
     keys_local = rotate_here(keys_raw).astype(low).reshape(device_tokens, kv_width)
-    keys_values = jnp.concatenate(
-        collect(
-            jnp.concatenate([keys_local, project[:, query_width + kv_width :]], axis=1), "col"
-        ),
-        axis=0,
-    )
+    own_pairs = jnp.concatenate([keys_local, project[:, query_width + kv_width :]], axis=1)
+    keys_values, table_part = gather(own_pairs, padded, 8)
+    left_block, keys_values = lax.optimization_barrier((left_block, keys_values))
+    left_full = lax.all_gather(left_block, "row", axis=0, tiled=True)
+    keys_values = keys_values.reshape(LEN, 2 * kv_width)
+    table_part = table_part.reshape(width, vocab_part)
     attn_keys = keys_values[:, :kv_width].reshape(LEN, KV_HEADS, HEAD)
     attn_values = keys_values[:, kv_width:].reshape(LEN, KV_HEADS, HEAD)
-    key_blocks = (col_index - jnp.arange(col_count, dtype=jnp.int32)) % col_count
-    key_positions = (
-        key_blocks[:, None] * device_tokens + jnp.arange(device_tokens, dtype=jnp.int32)[None, :]
-    ).reshape(LEN)
+    key_positions = jnp.arange(LEN, dtype=jnp.int32)
     allowed = (key_positions[None, :] <= positions[:, None]) | (key_positions[None, :] < seq_prefix)
 
     raw_scores = (
@@ -955,12 +1057,13 @@
     final_here = matmul(pick_hit, final).astype(low)
     final_pick = spread(final_here, 0)
     logits = matmul(final_pick, table_part)
+    part_line = jnp.arange(vocab_part, dtype=jnp.int32)
+    real = part_line < vocab_shard - row_index * vocab_part
+    logits = jnp.where(real[None, :], logits, MASK_VALUE)
     local_max = jnp.max(logits, axis=-1)
     local_sum = jnp.sum(jnp.exp(logits - local_max[:, None]), axis=-1)
     part_first = col_index * vocab_shard + row_index * vocab_part
-    target_hit = (
-        jnp.arange(vocab_part, dtype=jnp.int32)[None, :] == (targets_all - part_first)[:, None]
-    )
+    target_hit = (part_line[None, :] == (targets_all - part_first)[:, None]) & real[None, :]
     local_target = jnp.sum(jnp.where(target_hit, logits, 0.0), axis=-1)
     own_stats = jnp.stack([local_max, local_sum, local_target]).reshape(-1, 128)
     everyone = share(own_stats, 1).reshape(row_count * col_count, 3, row_count * pick_count)
@@ -980,9 +1083,6 @@
 
     table_grad_part = matmul_first(final_pick, grad_logits).astype(low)
     grad_parts = table_grad_part.reshape(row_count, features, vocab_part)
-    grad_pieces = [pick_block(grad_parts, (row_index + k) % row_count, 0) for k in range(row_count)]
-    table_grad = to_absolute(deliver(grad_pieces, "row", 1), row_index)
-    table_grad = jnp.moveaxis(table_grad, 0, 1).reshape(features, vocab_shard).astype(jnp.float32)
 
     grad_two, gain_two = norm_back(hidden_two, norm_gains[2], grad_final)
     grad_two_low = grad_two.astype(low)
@@ -1032,7 +1132,10 @@
         .astype(low)
         .reshape(col_count, device_tokens, 2 * kv_width)
     )
-    grad_pairs = summed(deliver([grad_pairs[k] for k in range(col_count)], "col", -1))
+    pair_pieces = [
+        pick_block(grad_pairs, (col_index + col_count - k) % col_count, 0) for k in range(col_count)
+    ]
+    grad_pairs = summed(deliver(pair_pieces, "col", -1))
     unused, pull_query = jax.vjp(rotate_here, queries_raw)
     grad_query_raw = pull_query(grad_queries.reshape(device_tokens, Q_HEADS, HEAD))[0]
     unused, pull_key = jax.vjp(rotate_here, keys_raw)
@@ -1049,32 +1152,23 @@
         normed, left_full, 0, grad_project, SMALL_BLOCK, attn_width,
         query_width // SMALL_BLOCK, attn_grad,
     )
-    attn_rows = reduce_rows(attn_grad)
     grad_normed = over_columns(grad_project, qkv_full)
     grad_embed_in, gain_zero = norm_back(embedded, norm_gains[0], grad_normed)
     grad_embedded = (grad_one + grad_embed_in).astype(low)
     own_gains = jnp.stack([gain_zero, gain_one, gain_two]).reshape(-1, 128)
-    gain_grads = jnp.sum(
-        share(own_gains, 3).reshape(row_count * col_count, 3, width), axis=0
-    )
     by_feature = grad_embedded.T.reshape(row_count, features, device_tokens)
-    vocab_room = -(-(vocab_shard + 1) // VOCAB_TILE) * VOCAB_TILE
-    table_grad = scatter(
-        local_tokens[:, :, :, None],
-        by_feature,
-        jnp.pad(table_grad, ((0, 0), (0, vocab_room - vocab_shard))),
-        7,
-    )[:, :vocab_shard]
-
-    mlp_rows, table_grad = lax.optimization_barrier((mlp_rows, table_grad))
+    mlp_mean_later, by_feature, attn_grad = lax.optimization_barrier((mlp_mean, by_feature, attn_grad))
+    attn_rows = reduce_rows(attn_grad)
     mlp_new = soap(
         [mlp_rows],
         [feedforward_bases],
-        [(mlp_mean[j], mlp_square[j], mlp_weight[j], bases_low[2 + j]) for j in range(3)],
+        [(mlp_mean_later[j], mlp_square[j], mlp_weight[j], bases_low[2 + j]) for j in range(3)],
         (True, True, True),
         (2, 0, 1),
+        (grad_parts,),
         4,
     )
+    mlp_new, table_base = mlp_new[:3], mlp_new[3]
     mlp_next, mlp_moment, mlp_scale = (
         jnp.stack([entry[k] for entry in mlp_new]) for k in range(3)
     )
@@ -1084,7 +1178,7 @@
     def blocks(values):
         return jnp.moveaxis(values.reshape(values.shape[0], col_count, -1), 1, 0)
 
-    (out_update, out_moment, out_scale), (qkv_next, qkv_moment, qkv_scale) = soap(
+    out_new, qkv_new, table_grad, all_gains = soap(
         [blocks(attn_rows[:, :query_width]), blocks(attn_rows[:, query_width:])],
         [blocks(out_bases.astype(low)), blocks(qkv_bases.astype(low))],
         [
@@ -1093,8 +1187,13 @@
         ],
         (False, True),
         (),
+        (local_tokens[:, :, :, None], by_feature, table_base, own_gains),
         5,
     )
+    out_update, out_moment, out_scale = out_new
+    qkv_next, qkv_moment, qkv_scale = qkv_new
+    table_grad = table_grad[:, :vocab_shard]
+    gain_grads = jnp.sum(all_gains.reshape(row_count * col_count, 3, width), axis=0)
     embed_change, embed_moment, embed_scale = adam_update(
         embed_table, table_grad.T, embed_mean, embed_square, WEIGHT_DECAY
     )

time: 1070 us -> 935 us (0.87)
  waiting for transfers between devices: 116 us -> 7.62 us
  starting transfers between devices: 26.7 us -> 4.9 us
  local copies, waits for them, and re-layouts: 83.1 us -> 61.6 us
  Pallas kernels: 582 us -> 600 us
    ppermute x20 -> x3, waiting for transfers between devices: 116 us -> 7.53 us  [send(): lax.ppermute(value, axis, [(k, (k + shift) % count) for k in range(count)])]
    pallas_call x2, Pallas kernels: 248 us -> 284 us  [soap(): pl.pallas_call(functools.partial(soap_kernel, rows, cols, adds, streamed)...]
    ppermute x20 -> x3, starting transfers between devices: 26.1 us -> 4.21 us  [send(): lax.ppermute(value, axis, [(k, (k + shift) % count) for k in range(count)])]
    pallas_call x1, Pallas kernels: 46.6 us -> 28.5 us  [spread(): pl.pallas_call(functools.partial(spread_kernel, rows, cols), out_shape=ja...]
    unnamed x295 -> x264, local copies, waits for them, and re-layouts: 33.5 us -> 21.7 us
    pallas_call x2 -> x1, Pallas kernels: 26.4 us -> 16.6 us  [share(): pl.pallas_call(functools.partial(share_kernel, rows, cols), out_shape=jax...]
  transfers between devices with their start and end apart: 25 -> 7, of which waited for: 9 -> 1; matrix products, arithmetic and copies ran while one was open for 26% -> 27% of each run, Pallas kernels for 45% -> 50%
where the time goes in v3:
time: 935 us; the launch traced here: 929 us
  Pallas kernels  600 us (64%)
  matrix products  156 us (17%)
  other arithmetic  71.2 us (8%)
  local copies, waits for them, and re-layouts  61.6 us (7%)
  between operations  16.8 us (2%)
  blocking collectives  10.6 us (1%)
    pallas_call x2, Pallas kernels, soap(): pl.pallas_call(functools.partial(soap_kernel, rows, cols, adds, streamed)...  284 us
    pallas_call x1, Pallas kernels, lookup(): pl.pallas_call(functools.partial(lookup_kernel, rows, cols), out_shape=[j...  136 us
    pallas_call x1, Pallas kernels, gather(): pl.pallas_call(functools.partial(gather_kernel, rows, cols), out_shape=[j...  60.5 us
    dot_general x21, matrix products, matmul_last(): lax.dot_general(left_op, right_op, (((1,), (1,)), ((), ())), preferred_el...  52.1 us
    dot_general x22, matrix products, matmul(): return jnp.dot(left_op, right_op, preferred_element_type=jnp.float32)  43.7 us
    pallas_call x5, Pallas kernels, outer(): pl.pallas_call(outer_kernel, grid=(other.shape[1] // block,), out_shape=j...  38.9 us
    pallas_call x1, Pallas kernels, fold(): pl.pallas_call(functools.partial(fold_kernel, rows, cols), out_shape=jax....  35.1 us
    pallas_call x1, Pallas kernels, spread(): pl.pallas_call(functools.partial(spread_kernel, rows, cols), out_shape=ja...  28.5 us
  transfers between devices with their start and end apart: 7, of which 1 were waited for; matrix products, arithmetic and copies ran while one was open for 27% of the time, Pallas kernels for 50%

profile of v3, /device:TPU:0, one launch (start us, length us, event | category | flops | bytes accessed | tf_op | source)
XLA Modules:
  0.0 928.5 jit_solution(1268521900582497145)
XLA Ops:
  9.7 10.6 %all-gather.1 = s32[8,1,1152]{2,1,0:T(1,128)S(1)} all-gather(s32[1,1,1152]{2,1,0:T(1,128)S(1)} %reshape.351), channel_id=2, replica_groups=mesh['row'=8,'col'=4] {'row'}, dimensions={0}, use_global_device_ids=true | all-gather | bytes 41472 | tf_op jit(solution)/shard_map/all_gather | solution.py:953
  21.6 2.9 convert_bitcast_fusion
  27.0 136.3 %shard_map.351 = (bf16[8,144,256]{2,1,0:T(8,128)(2,1)}, bf16[4,8,144,768]{3,2,1,0:T(8,128)(2,1)}) custom-call(s32[8192]{0:T(1024)} %bitcast.434, bf16[144,8192]{1,0:T(8,128)(2,1)} %pad.16.table_ref, bf16[144,768]{1,0:T(8,128)(2,1)} %pad_maximum_fusion.15.weight_ref), custom_call_target="tpu_custom_call" | custom-call | tf_op jit(solution)/shard_map/pallas_call | solution.py:695
  164.9 3.8 convert_element_type.151
  169.0 2.0 convolution_convert_fusion.3
  175.1 60.5 %shard_map.352 = (bf16[4,256,768]{2,1,0:T(8,128)(2,1)}, bf16[8,144,1024]{2,1,0:T(8,128)(2,1)}) custom-call(bf16[256,768]{1,0:T(8,128)(2,1)} %pad_maximum_fusion.10.x_ref, bf16[144,8192]{1,0:T(8,128)(2,1)} %pad.16.table_ref), custom_call_target="tpu_custom_call" | custom-call | tf_op jit(solution)/shard_map/pallas_call | solution.py:805
  243.8 2.4 convolution_convert_fusion.6
  257.2 11.1 %fusion.123 = (f32[6,3,256]{2,1,0:T(4,128)S(1)}, f32[6,3,256,1024]{2,3,1,0:T(8,128)}) fusion(pred[256,1024]{0,1:T(8,128)(4,1)} %fusion.54, bf16[1024,6,64,1]{0,2,3,1:T(8,128)(2,1)S(1)} %bitcast.393, bf16[256,6,3,32]{0,3,2,1:T(8,128)(2,1)} %bitcast.414, bf16[256,6,3,32]{0,3,2,1:T(8,128)(2,1)S(1)} %bitcast.412), kind=kOutput, calls=%fused_computation.296 | convolution fusion | flops 624034816 | bytes 20531200 | tf_op jit(solution)/shard_map/sub | solution.py:1036
  268.3 10.1 %fusion.39 = bf16[6,64,3,256]{3,1,2,0:T(8,128)(2,1)S(1)} fusion(bf16[1024,6,64,1]{0,2,3,1:T(8,128)(2,1)S(1)} %bitcast.418, f32[6,3,256,1024]{2,3,1,0:T(8,128)} %get-tuple-element.149, f32[6,3,256]{2,1,0:T(4,128)S(1)} %get-tuple-element.148), kind=kOutput, calls=%fused_computation.106 | convolution fusion | flops 613711872 | bytes 20269056 | tf_op jit(solution)/shard_map/hgqk,khd->qhgd/dot_general | solution.py:1039
  278.4 2.1 fusion.58
  280.5 1.9 convolution_add_fusion.14
  282.5 1.9 convolution_add_fusion.13
  284.4 3.0 multiply_reduce_fusion.6
  288.9 2.4 fusion.31
  291.3 3.1 fusion.30
  294.4 3.2 fusion.29
  297.6 2.4 fusion.28
  300.1 2.4 fusion.26
  302.5 2.4 fusion.25
  312.8 28.5 %shard_map.353 = bf16[8,4,32,1152]{3,2,1,0:T(8,128)(2,1)} custom-call(bf16[4,32,1152]{2,1,0:T(8,128)(2,1)} %bitcast.417), custom_call_target="tpu_custom_call" | custom-call | tf_op jit(solution)/shard_map/pallas_call | solution.py:146
  341.3 4.6 select_reduce_fusion.1
  346.0 2.4 exponential_reduce_fusion
  349.0 16.6 %shard_map.354 = f32[8,4,24,128]{3,2,1,0:T(8,128)} custom-call(f32[24,128]{1,0:T(8,128)} %reshape.325.x_ref), custom_call_target="tpu_custom_call" | custom-call | tf_op jit(solution)/shard_map/pallas_call | solution.py:81
  367.9 8.5 convolution_convert_fusion.1
  376.4 35.1 %shard_map.355 = bf16[4,32,1152]{2,1,0:T(8,128)(2,1)} custom-call(bf16[8,4,32,1152]{3,2,1,0:T(8,128)(2,1)} %bitcast.405), custom_call_target="tpu_custom_call" | custom-call | tf_op jit(solution)/shard_map/pallas_call | solution.py:225
  411.6 2.2 multiply_reduce_fusion
  414.0 2.4 fusion.36
  416.4 2.2 fusion.35
  418.6 2.2 fusion.34
  420.8 2.3 fusion.32
  425.6 2.1 fusion.16.other_ref
  427.7 8.0 shard_map.356.refs_0_
  435.6 8.2 shard_map.357.refs_0_
  443.9 8.1 shard_map.358
  452.0 2.1 copy.149.other_ref
  454.2 2.4 fusion.22
  456.6 2.3 fusion.27
  459.0 2.2 convolution_add_fusion.5
  461.2 2.6 convolution_add_fusion.4
  463.9 2.6 convolution_add_fusion.3
  466.5 2.7 convolution_add_fusion.2
  469.3 3.0 convolution_add_fusion.1
  472.3 3.7 multiply_reduce_fusion.1
  481.5 12.8 %fusion.1 = (f32[6,3,256]{2,1,0:T(4,128)S(1)}, f32[6,1024,256,3]{2,1,3,0:T(8,128)}) fusion(f32[6,3,256,1024]{2,3,1,0:T(8,128)} %get-tuple-element.149, f32[6,3,256]{2,1,0:T(4,128)S(1)} %copy-done.91, bf16[1024,6,64,1]{0,2,3,1:T(8,128)(2,1)S(1)} %bitcast.419, bf16[256,6,3,64]{0,3,2,1:T(8,128)(2,1)S(1)} %bitcast.421), kind=kOutput, calls=%fused_computation.3 | convolution fusion | flops 618130944 | bytes 39161856 | tf_op jit(solution)/shard_map/qhgd,khd->hgqk/dot_general | solution.py:1111
  494.3 13.9 %fusion.3 = bf16[6,3,256,1024]{2,3,1,0:T(8,128)(2,1)S(1)} fusion(f32[6,1024,256,3]{2,1,3,0:T(8,128)} %get-tuple-element.157, f32[6,3,256]{2,1,0:T(4,128)S(1)} %get-tuple-element.156, f32[6,3,256,1024]{2,3,1,0:T(8,128)} %get-tuple-element.149, f32[6,3,256]{2,1,0:T(4,128)S(1)} %copy-done.91), kind=kLoop, calls=%fused_computation.5 | loop fusion | flops 18874368 | bytes 47222784 | tf_op jit(solution)/shard_map/convert_element_type | solution.py:1115
  508.2 3.7 copy-done
  511.9 2.9 fusion.45
  517.9 10.1 %fusion.42 = bf16[1024,6,64]{0,2,1:T(8,128)(2,1)S(1)} fusion(bf16[256,6,3,64]{0,3,2,1:T(8,128)(2,1)} %bitcast.422, f32[6,3,256,1024]{2,3,1,0:T(8,128)} %get-tuple-element.149, f32[6,3,256]{2,1,0:T(4,128)S(1)} %copy-done.91), kind=kOutput, calls=%fused_computation.107 | convolution fusion | flops 613810176 | bytes 20269056 | tf_op jit(solution)/shard_map/hgqk,qhgd->khd/dot_general | solution.py:1124
  536.3 5.7 convolution_multiply_fusion
  544.5 6.6 shard_map.359.refs_0_
  551.1 2.9 convolution_add_fusion.11
  554.1 7.5 collective-permute-done.1
  564.4 1.9 copy.143
  569.9 2.0 convolution_add_fusion.10
  572.1 2.3 multiply_reduce_fusion.2
  577.5 8.0 shard_map.360
  588.7 3.1 copy.153
  591.9 2.3 copy.154
  594.2 2.7 copy.155.refs_12_
  603.1 4.9 convolution_convert_fusion
  609.8 168.1 %shard_map.361 = (f32[144,768]{1,0:T(8,128)}, f32[144,768]{1,0:T(8,128)}, f32[144,768]{1,0:T(8,128)}, f32[144,768]{1,0:T(8,128)}, f32[144,768]{1,0:T(8,128)}, /*...) custom-call(bf16[144,9216]{1,0:T(8,128)(2,1)} %reduce-scatter.5.clon, ...), custom_call_target="tpu_custom_call" | custom-call | tf_op jit(solution)/shard_map/pallas_call | solution.py:543
  777.9 2.4 pad_maximum_fusion.3
  784.2 116.2 %shard_map.362 = (f32[144,288]{1,0:T(8,128)}, f32[144,288]{1,0:T(8,128)}, f32[144,288]{1,0:T(8,128)}, f32[144,480]{1,0:T(8,128)}, f32[144,480]{1,0:T(8,128)}, /*...) custom-call(bf16[4,144,288]{2,1,0:T(8,128)(2,1)} %bitcast.408, bf16[4,144,480]{2,1,0:T(8,128)(2,1)} %bitcast.402, ...), custom_call_target="tpu_custom_call" | custom-call | tf_op jit(solution)/shard_map/pallas_call | solution.py:543
  901.6 12.8 %negate_add_fusion = (f32[8000,144]{0,1:T(8,128)}, f32[8000,144]{0,1:T(8,128)}, f32[8000,144]{0,1:T(8,128)}) fusion(f32[8000,144]{0,1:T(8,128)} %param.29, f32[144,8192]{1,0:T(8,128)} %get-tuple-element.69, f32[8000,144]{0,1:T(8,128)} %param.35, f32[8000,144]{0,1:T(8,128)} %param.34), kind=kLoop, calls=%fused_computation.21 | loop fusion | flops 14976000 | bytes 32256000 | tf_op jit(solution)/shard_map/add | solution.py:1200
  (393 shorter events, 97.2 us)
Async XLA Ops:
  7.2 281.7 %all-gather.5.cloned.1.call-start = ((), (), s32[]{:S(2)}) async-start(), calls=%async_computation.2 | async-start | bytes 21897216 | tf_op jit(solution)/shard_map/all_gather | solution.py:958
  8.6 12.9 %copy-start.55 = (f32[144,288]{1,0:T(8,128)S(1)}, f32[144,288]{1,0:T(8,128)}, u32[]{:S(2)}) copy-start(f32[144,288]{1,0:T(8,128)} %refs_6_.1) | copy-start | bytes 497668
  8.7 12.9 %copy-start.54 = (f32[144,480]{1,0:T(8,128)S(1)}, f32[144,480]{1,0:T(8,128)}, u32[]{:S(2)}) copy-start(f32[144,480]{1,0:T(8,128)} %refs_10_.1) | copy-start | bytes 829444
  9.6 418.0 %all-gather.7.cloned.1.call-start = ((), (), s32[]{:S(2)}) async-start(), calls=%async_computation.3 | async-start | bytes 14929920 | tf_op jit(solution)/shard_map/all_gather | solution.py:1022
  20.3 4.2 copy-start.75
  164.8 119.6 %copy-start.1 = (f32[1152,256]{0,1:T(8,128)}, f32[1152,256]{0,1:T(8,128)S(1)}, u32[]{:S(2)}) copy-start(f32[1152,256]{0,1:T(8,128)S(1)} %copy.125) | copy-start | bytes 3538948
  164.8 3.8 copy-start.79
  169.0 3.8 copy-start.41
  174.0 61.5 %copy-start.56 = (f32[256,32]{0,1:T(8,128)}, f32[256,32]{0,1:T(8,128)S(1)}, u32[]{:S(2)}) copy-start(f32[256,32]{0,1:T(8,128)S(1)} %get-tuple-element.146) | copy-start | bytes 98308
  174.0 61.5 %copy-start.58 = (f32[256,32]{0,1:T(8,128)}, f32[256,32]{0,1:T(8,128)S(1)}, u32[]{:S(2)}) copy-start(f32[256,32]{0,1:T(8,128)S(1)} %get-tuple-element.147) | copy-start | bytes 98308
  174.3 61.3 %copy-start.3 = (bf16[5,144,1152]{2,1,0:T(8,128)(2,1)S(1)}, bf16[5,144,1152]{2,1,0:T(8,128)(2,1)}, u32[]{:S(2)}) copy-start(bf16[5,144,1152]{2,1,0:T(8,128)(2,1)} %convert_element_type.151) | copy-start | bytes 4976644
  239.4 370.4 %reduce-scatter.5.cloned.1.call-start = ((), (), s32[]{:S(2)}) async-start(), calls=%async_computation.5 | async-start | bytes 23887872 | tf_op jit(solution)/shard_map/reduce_scatter | solution.py:990
  249.3 7.8 copy-start.28
  257.2 11.1 %copy-start.51 = (bf16[256,18,32]{0,2,1:T(8,128)(2,1)}, bf16[256,18,32]{0,2,1:T(8,128)(2,1)S(1)}, u32[]{:S(2)}) copy-start(bf16[256,18,32]{0,2,1:T(8,128)(2,1)S(1)} %get-tuple-element.131) | copy-start | bytes 884740
  257.2 11.1 %copy-start.60 = (bf16[1024,384]{0,1:T(8,128)(2,1)S(1)}, bf16[1024,384]{0,1:T(8,128)(2,1)}, u32[]{:S(2)}) copy-start(bf16[1024,384]{0,1:T(8,128)(2,1)} %copy.130) | copy-start | bytes 2359300
  268.3 10.1 %copy-start.90 = (f32[6,3,256]{2,1,0:T(4,128)}, f32[6,3,256]{2,1,0:T(4,128)S(1)}, u32[]{:S(2)}) copy-start(f32[6,3,256]{2,1,0:T(4,128)S(1)} %get-tuple-element.148) | copy-start | bytes 55300
  278.4 6.0 copy-start.38
  287.4 3.9 copy-start.106
  287.4 3.9 copy-start.87
  288.9 16.8 %copy-start.22 = (bf16[256,1152]{1,0:T(8,128)(2,1)}, bf16[256,1152]{1,0:T(8,128)(2,1)S(1)}, u32[]{:S(2)}) copy-start(bf16[256,1152]{1,0:T(8,128)(2,1)S(1)} %multiply_convert_fusion.4.values_ref) | copy-start | bytes 1769476
  288.9 16.1 %copy-start.5 = (bf16[4608,2304]{1,0:T(8,128)(2,1)S(1)}, bf16[4608,2304]{1,0:T(8,128)(2,1)}, u32[]{:S(2)}) copy-start(bf16[4608,2304]{1,0:T(8,128)(2,1)} %all-gather.5.cloned.1.call-done) | copy-start | bytes 63700996
  291.3 15.1 %copy-start.30 = (f32[256,768]{1,0:T(8,128)}, f32[256,768]{1,0:T(8,128)S(1)}, u32[]{:S(2)}) copy-start(f32[256,768]{1,0:T(8,128)S(1)} %fusion.31) | copy-start | bytes 2359300
  294.4 12.0 %copy-start.32 = (f32[256,768]{1,0:T(8,128)}, f32[256,768]{1,0:T(8,128)S(1)}, u32[]{:S(2)}) copy-start(f32[256,768]{1,0:T(8,128)S(1)} %fusion.30) | copy-start | bytes 2359300
  297.6 8.8 copy-start.34
  300.1 6.3 copy-start.36
  302.5 3.9 copy-start.13
  311.7 29.6 %copy-start.81 = (f32[256]{0:T(256)}, f32[256]{0:T(256)S(1)}, u32[]{:S(2)}) copy-start(f32[256]{0:T(256)S(1)} %fusion.108) | copy-start | bytes 3076
  311.7 29.6 %copy-start.119 = (pred[1024]{0:T(1024)(128)(4,1)S(1)}, pred[1024]{0:T(1024)(128)(4,1)}, u32[]{:S(2)}) copy-start(pred[1024]{0:T(1024)(128)(4,1)} %iota_compare_fusion.3) | copy-start | bytes 3076
  311.7 29.6 %copy-start.122 = (bf16[8,144,1024]{2,1,0:T(8,128)(2,1)S(1)}, bf16[8,144,1024]{2,1,0:T(8,128)(2,1)}, u32[]{:S(2)}) copy-start(bf16[8,144,1024]{2,1,0:T(8,128)(2,1)} %get-tuple-element.56) | copy-start | bytes 7077892
  341.3 4.6 copy-start.99
  348.4 18.8 %copy-start.101 = (s32[1024]{0:T(1024)S(1)}, s32[1024]{0:T(1024)}, u32[]{:S(2)}) copy-start(s32[1024]{0:T(1024)} %param.27) | copy-start | bytes 12292
  367.9 8.5 copy-start.113
  367.9 8.5 copy-start.115
  376.4 35.2 %copy-start.82 = (f32[256]{0:T(256)S(1)}, f32[256]{0:T(256)}, u32[]{:S(2)}) copy-start(f32[256]{0:T(256)} %copy-done.81) | copy-start | bytes 3076
  376.4 35.2 %copy-start.103 = (s32[256]{0:T(256)S(1)}, s32[256]{0:T(256)}, u32[]{:S(2)}) copy-start(s32[256]{0:T(256)} %get-tuple-element.159) | copy-start | bytes 3076
  376.4 35.2 %copy-start.118 = (s32[128]{0:T(128)S(1)}, s32[128]{0:T(128)}, u32[]{:S(2)}) copy-start(s32[128]{0:T(128)} %param.26) | copy-start | bytes 1540
  414.0 6.7 copy-start.43
  451.9 328.4 %reduce-scatter.3.cloned.1.call-start = ((), (), s32[]{:S(2)}) async-start(), calls=%async_computation.4 | async-start | bytes 7962624 | tf_op jit(solution)/shard_map/reduce_scatter | solution.py:990
  466.5 10.7 %slice-start = ((s8[7077888]{0:T(1024)(128)(4,1)}), s8[4194304]{0:T(1024)(128)(4,1)S(1)}, s32[]{:S(2)}) async-start(s8[7077888]{0:T(1024)(128)(4,1)} %bitcast.378), calls=%async_computation.6 | async-start | bytes 8388608
  472.3 4.4 copy-start.83
  472.3 4.3 copy-start.95
  472.3 4.9 slice-start.1
  481.1 13.2 %copy-start.62 = (bf16[256,1152]{0,1:T(8,128)(2,1)}, bf16[256,1152]{0,1:T(8,128)(2,1)S(1)}, u32[]{:S(2)}) copy-start(bf16[256,1152]{0,1:T(8,128)(2,1)S(1)} %pad_maximum_fusion.9) | copy-start | bytes 1769476
  494.3 17.6 %copy-start.52 = (bf16[256,18,32]{0,2,1:T(8,128)(2,1)S(1)}, bf16[256,18,32]{0,2,1:T(8,128)(2,1)}, u32[]{:S(2)}) copy-start(bf16[256,18,32]{0,2,1:T(8,128)(2,1)} %copy-done.51) | copy-start | bytes 884740
  494.3 17.6 %copy-start.53 = (bf16[256,18,32]{0,2,1:T(8,128)(2,1)S(1)}, bf16[256,18,32]{0,2,1:T(8,128)(2,1)}, u32[]{:S(2)}) copy-start(bf16[256,18,32]{0,2,1:T(8,128)(2,1)} %get-tuple-element.132) | copy-start | bytes 884740
  531.0 11.1 %copy-start.11 = (bf16[4,256,384]{2,1,0:T(8,128)(2,1)}, bf16[4,256,384]{2,1,0:T(8,128)(2,1)S(1)}, u32[]{:S(2)}) copy-start(bf16[4,256,384]{2,1,0:T(8,128)(2,1)S(1)} %copy.142) | copy-start | bytes 2359300
  531.0 5.3 copy-start.29
  532.1 21.9 %collective-permute-start.2 = (bf16[256,768]{1,0:T(8,128)(2,1)}, bf16[256,768]{1,0:T(8,128)(2,1)S(1)}, u32[]{:S(2)}, u32[]{:S(2)}) collective-permute-start(bf16[256,768]{1,0:T(8,128)(2,1)} %get-tuple-element.117), channel_id=1, source_target_pairs={{0,1},{1,2},{2,3},{3,0},{4,5},{5,6},{6,7},{7,4},{8,9},{9,10},{10,1... | collective-permute-start | bytes 1179656 | tf_op jit(solution)/shard_map/ppermute | solution.py:822
  533.8 27.8 %collective-permute-start.1 = (bf16[256,768]{1,0:T(8,128)(2,1)}, bf16[256,768]{1,0:T(8,128)(2,1)}, u32[]{:S(2)}, u32[]{:S(2)}) collective-permute-start(bf16[256,768]{1,0:T(8,128)(2,1)} %get-tuple-element.116), channel_id=1, source_target_pairs={{0,2},{1,3},{2,0},{3,1},{4,6},{5,7},{6,4},{7,5},{8,10},{9,11},{10,... | collective-permute-start | bytes 1179656 | tf_op jit(solution)/shard_map/ppermute | solution.py:822
  535.3 6.7 copy-start.57
  535.3 6.7 copy-start.59
  535.3 26.2 %collective-permute-start = (bf16[256,768]{1,0:T(8,128)(2,1)}, bf16[256,768]{1,0:T(8,128)(2,1)}, u32[]{:S(2)}, u32[]{:S(2)}) collective-permute-start(bf16[256,768]{1,0:T(8,128)(2,1)} %get-tuple-element.115), channel_id=1, source_target_pairs={{0,3},{1,0},{2,1},{3,2},{4,7},{5,4},{6,5},{7,6},{8,11},{9,8},{10,9... | collective-permute-start | bytes 1179656 | tf_op jit(solution)/shard_map/ppermute | solution.py:822
  551.1 10.5 %copy-start.12 = (bf16[4,256,384]{2,1,0:T(8,128)(2,1)S(1)}, bf16[4,256,384]{2,1,0:T(8,128)(2,1)}, u32[]{:S(2)}) copy-start(bf16[4,256,384]{2,1,0:T(8,128)(2,1)} %copy-done.11) | copy-start | bytes 2359300
  562.9 7.0 copy-start.25
  596.9 4.9 copy-start.27
  599.3 3.7 copy-start.39
  599.3 3.7 copy-start.100
  603.1 5.6 copy-start.49
  901.5 12.9 %copy-start.80 = (f32[3,1152]{1,0:T(4,128)S(1)}, f32[3,1152]{1,0:T(4,128)}, u32[]{:S(2)}) copy-start(f32[3,1152]{1,0:T(4,128)} %param.30) | copy-start | bytes 41476
  901.5 12.9 %copy-start.92 = (f32[3,1152]{1,0:T(4,128)S(1)}, f32[3,1152]{1,0:T(4,128)}, u32[]{:S(2)}) copy-start(f32[3,1152]{1,0:T(4,128)} %param.37) | copy-start | bytes 41476
  901.5 12.9 %copy-start.93 = (f32[3,1152]{1,0:T(4,128)S(1)}, f32[3,1152]{1,0:T(4,128)}, u32[]{:S(2)}) copy-start(f32[3,1152]{1,0:T(4,128)} %param.36) | copy-start | bytes 41476
  901.6 13.5 %copy-start.66 = (f32[144,768]{1,0:T(8,128)S(1)}, f32[144,768]{1,0:T(8,128)}, u32[]{:S(2)}) copy-start(f32[144,768]{1,0:T(8,128)} %get-tuple-element.78) | copy-start | bytes 1327108
  901.6 13.5 %copy-start.67 = (f32[144,768]{1,0:T(8,128)S(1)}, f32[144,768]{1,0:T(8,128)}, u32[]{:S(2)}) copy-start(f32[144,768]{1,0:T(8,128)} %get-tuple-element.79) | copy-start | bytes 1327108
  901.6 13.5 %copy-start.68 = (f32[144,768]{1,0:T(8,128)S(1)}, f32[144,768]{1,0:T(8,128)}, u32[]{:S(2)}) copy-start(f32[144,768]{1,0:T(8,128)} %get-tuple-element.80) | copy-start | bytes 1327108
  (70 other events, 154.2 us)
Sparse Core Ops, SparseCore 0:
  11.5 202.9 all-gather.4
  239.5 72.9 all-gather.6
  452.1 137.9 reduce-scatter.4
  593.4 89.6 reduce-scatter.2

commit v4 on v3

--- a/solution.py
+++ b/solution.py
@@ -26,6 +26,8 @@
 VOCAB_TILE = 1024
 LOOK_STEP = 32
 TILES_AT_ONCE = 3
+SKEW = 2
+SOAP_VMEM = 62 * 2**20
 SMALL_BLOCK = 384
 
 
@@ -348,8 +350,8 @@
         push(part_of((row + k) % rows), lies_at(row), (sems.at[0], sems.at[1]), k - 1, ((row + k) % rows, col))
         for k in range(1, rows)
     ]
-    for _ in range(2 * cols):
-        yield
+    yield
+    yield
     own.wait()
     for copy in copies:
         copy.wait()
@@ -361,7 +363,7 @@
         self.grad, self.basis = grad, basis
         (
             self.mean, self.square, self.weight, self.left,
-            self.next, self.moment, self.scale,
+            self.moment, self.scale, self.next,
             self.work, self.inbox, self.sum, self.total, self.whole, self.sems, self.row_sems, self.core_sems,
         ) = refs
         self.adds_weight = adds_weight
@@ -428,67 +430,71 @@
     place = (row, col, rows, cols)
     greet(line_peers(row, col, cols) + [((row + k) % rows, col) for k in range(1, rows)])
     count = len(adds)
+
+    def take(number):
+        nonlocal refs
+        first, refs = refs[:number], refs[number:]
+        return first
+
     shared = 1 if streamed else count
-    grads, bases, refs = refs[:shared], refs[shared : 2 * shared], refs[2 * shared :]
-    inputs, refs = refs[: 4 * count], refs[4 * count :]
-    extra = 1 if streamed else 4
-    others_in, refs = refs[:extra], refs[extra:]
-    outputs, refs = refs[: 3 * count], refs[3 * count :]
-    extra = 1 if streamed else 2
-    others_out, refs = refs[:extra], refs[extra:]
-    scratch, refs = refs[: 8 * count], refs[8 * count :]
-    running = []
-    loads = []
+    grads, bases, kept, lefts = take(shared), take(shared), take(3 * shared), take(count)
+    others_in = take(3)
+    made = take(3 * shared)
+    others_out = take(3 if streamed else 1)
+    scratch = take(8 * count)
+    running, loads = [], []
     for m, add in enumerate(adds):
-        grad, basis = grads[m % shared], bases[m % shared]
-        others = inputs[4 * m : 4 * m + 4]
-        width = others[0].shape[1]
         if streamed:
+            grad, basis = grads[0], bases[0]
+            own = (*(ref.at[m] for ref in kept), lefts[m], *(ref.at[m] for ref in made))
             held, stage, load_sems = refs[:3]
-
-            def grad_of(d, grad=grad, m=m, width=width):
+            width = kept[0].shape[2]
+
+            def grad_of(d, m=m):
                 at = pl.multiple_of((streamed.index(m) * cols + d) * width, width)
                 return grad.at[:, pl.ds(at, width)]
 
-            def basis_of(d, held=held, m=m):
+            def basis_of(d, m=m):
                 return held[m, d]
 
             for e in range(cols):
-                at = e * width
                 for part in range(2):
                     lines = pl.ds(part * (width // 2), width // 2)
                     copy = pltpu.make_async_copy(
-                        basis.at[m, lines, pl.ds(at, width)], stage.at[part], load_sems.at[part]
+                        basis.at[m, lines, pl.ds(e * width, width)], stage.at[part], load_sems.at[part]
                     )
                     loads.append((copy, part, m, e))
         else:
-
-            def grad_of(d, grad=grad):
+            own = (*kept[3 * m : 3 * m + 3], lefts[m], *made[3 * m : 3 * m + 3])
+
+            def grad_of(d, grad=grads[m]):
                 return grad.at[d]
 
-            def basis_of(d, basis=basis):
+            def basis_of(d, basis=bases[m]):
                 return basis[d]
 
-        refs_of = (*others, *outputs[3 * m : 3 * m + 3], *scratch[8 * m : 8 * m + 8])
+        refs_of = (*own, *scratch[8 * m : 8 * m + 8])
         running.append(Matrix(place, grad_of, basis_of, refs_of, add).go())
+    beside = []
     if streamed:
         running = [running[m] for m in streamed]
         loads = [load for m in streamed for load in loads if load[2] == m]
         for copy, *unused in loads[:2]:
             copy.start()
-    if streamed:
-        count = others_in[0].shape[2]
+        parts, landed = others_in[1], others_out[1]
+        span = parts.shape[2]
 
         def lies_at(k):
-            return others_out[0].at[:, pl.ds(pl.multiple_of(k * count, count), count)]
-
-        running.append(swap_go(place, lambda k: others_in[0].at[k], lies_at, *refs[3:]))
+            return landed.at[:, pl.ds(pl.multiple_of(k * span, span), span)]
+
+        beside = [
+            swap_go(place, lambda k: parts.at[k], lies_at, *refs[3:5]),
+            reach_go(place, others_in[0], others_out[0], *refs[5:7]),
+            share_go(place, others_in[2], others_out[2], *refs[7:]),
+        ]
     else:
-        running = [
-            scatter_go(place, *others_in[:3], others_out[0], *refs[:3]),
-            share_go(place, others_in[3], others_out[1], *refs[3:]),
-        ] + running
-    for m in running:
+        beside = [scatter_go(place, *others_in, *others_out)]
+    for m in running + beside:
         next(m)
     for k, (copy, slot, m, e) in enumerate(loads):
         copy.wait()
@@ -496,64 +502,227 @@
         held[m, e, lines] = stage[slot].astype(held.dtype)
         if k + 2 < len(loads):
             loads[k + 2][0].start()
-    while running:
-        running = [m for m in running if next(m, "done") != "done"]
-
-
-def soap(grads, bases, matrices, adds, streamed, others, collective_id):
+    turn = 0
+    while running or beside:
+        left = []
+        for k, m in running if turn else list(enumerate(running)):
+            if turn < SKEW * k or next(m, "done") != "done":
+                left.append((k, m))
+        running = left
+        beside = [m for m in beside if next(m, "done") != "done"]
+        turn += 1
+
+
+def soap(grads, bases, kept, lefts, adds, streamed, others, collective_id):
     rows, cols = lax.axis_size("row"), lax.axis_size("col")
     dma = pltpu.SemaphoreType.DMA
-    vmem = pl.BlockSpec(memory_space=pltpu.VMEM)
-    outs, scratch = [], []
-    for mean, square, weight, left in matrices:
-        outs += [jax.ShapeDtypeStruct(weight.shape, jnp.float32)] * 3
-        block = weight.shape
+    vmem, anywhere = pl.BlockSpec(memory_space=pltpu.VMEM), pl.BlockSpec(memory_space=pl.ANY)
+    low = lefts[0].dtype
+    scratch = []
+    outs = [jax.ShapeDtypeStruct(array.shape, jnp.float32) for array in kept]
+    for m in range(len(adds)):
+        block = kept[0].shape[1:] if streamed else kept[3 * m].shape
         scratch += [
-            pltpu.VMEM((cols, *block), left.dtype),
-            pltpu.VMEM((4 * (cols - 1), *block), left.dtype),
-            pltpu.VMEM(block, left.dtype),
+            pltpu.VMEM((cols, *block), low),
+            pltpu.VMEM((4 * (cols - 1), *block), low),
+            pltpu.VMEM(block, low),
             pltpu.VMEM(block, jnp.float32),
-            pltpu.VMEM((rows, *block), left.dtype),
+            pltpu.VMEM((rows, *block), low),
             dma((2, 6 * (cols - 1))),
             dma((2, rows // 2 - 1)),
             dma((2, rows // 2)),
         ]
+    specs = [vmem] * len(grads)
+    specs += [anywhere if streamed else vmem] * len(bases)
+    specs += [vmem] * (len(kept) + len(lefts))
     if streamed:
-        width = matrices[0][2].shape[1]
+        width = kept[0].shape[2]
+        grad, parts, own = others
+        specs += [vmem, anywhere, vmem]
+        outs += [
+            jax.ShapeDtypeStruct((cols, *grad.shape), grad.dtype),
+            jax.ShapeDtypeStruct((parts.shape[1], parts.shape[0] * parts.shape[2]), parts.dtype),
+            jax.ShapeDtypeStruct((rows, cols, *own.shape), own.dtype),
+        ]
+        out_specs = [vmem] * (len(outs) - 2) + [anywhere, vmem]
         scratch += [
-            pltpu.VMEM((len(matrices), cols, width, width), jnp.bfloat16),
+            pltpu.VMEM((len(adds), cols, width, width), low),
             pltpu.VMEM((2, width // 2, width), jnp.float32),
             dma((2,)),
+            dma((2, rows - 1)),
+            dma,
+            *[dma((2, 2 * (cols - 1))), dma((2, rows - 1))] * 2,
         ]
-    anywhere = pl.BlockSpec(memory_space=pl.ANY)
-    other_spec = anywhere if streamed else vmem
-    out_specs = [vmem] * len(outs) + [other_spec] * (1 if streamed else 2)
-    if streamed:
-        parts, depth, count = others[0].shape
-        outs += [jax.ShapeDtypeStruct((depth, parts * count), others[0].dtype)]
-        scratch += [dma((2, rows - 1)), dma]
     else:
-        ids, grad, base, own = others
-        outs += [
-            jax.ShapeDtypeStruct(base.shape, jnp.float32),
-            jax.ShapeDtypeStruct((rows, cols, *own.shape), own.dtype),
-        ]
-        scratch += [pltpu.VMEM((cols, *grad.shape), grad.dtype)]
-        scratch += [dma((2, 2 * (cols - 1))), dma((2, rows - 1))] * 2
-    got = pl.pallas_call(
+        specs += [vmem] * 3
+        outs += [jax.ShapeDtypeStruct(others[2].shape, jnp.float32)]
+        out_specs = [vmem] * len(outs)
+    return pl.pallas_call(
         functools.partial(soap_kernel, rows, cols, adds, streamed),
         out_shape=outs,
-        in_specs=[vmem] * len(grads)
-        + [anywhere if streamed else vmem] * len(bases)
-        + [vmem] * (4 * len(matrices))
-        + [other_spec] * len(others),
+        in_specs=specs,
         out_specs=out_specs,
         scratch_shapes=scratch,
         compiler_params=pltpu.CompilerParams(
-            collective_id=collective_id, has_side_effects=True, vmem_limit_bytes=VMEM_LIMIT
+            collective_id=collective_id, has_side_effects=True, vmem_limit_bytes=SOAP_VMEM
         ),
-    )(*grads, *bases, *[part for matrix in matrices for part in matrix], *others)
-    return [got[k * 3 : k * 3 + 3] for k in range(len(matrices))] + list(got[3 * len(matrices) :])
+    )(*grads, *bases, *kept, *lefts, *others)
+
+
+def mask_bias(places_ref, keys, tokens):
+    key = lax.broadcasted_iota(jnp.int32, (keys, tokens), 0)
+    token = lax.broadcasted_iota(jnp.int32, (keys, tokens), 1) + places_ref[0]
+    return jnp.where((key <= token) | (key < places_ref[1]), 0.0, MASK_VALUE)
+
+
+def matmul_nt(left_op, right_op):
+    return lax.dot_general(
+        left_op, right_op, (((1,), (1,)), ((), ())), preferred_element_type=jnp.float32
+    )
+
+
+def matmul_tn(left_op, right_op):
+    return lax.dot_general(
+        left_op, right_op, (((0,), (0,)), ((), ())), preferred_element_type=jnp.float32
+    )
+
+
+def halves_swapped(values):
+    lane = lax.broadcasted_iota(jnp.int32, values.shape, 1)
+    half = HEAD // 2
+    later = pltpu.roll(values, 2 * HEAD - half, 1)
+    return jnp.where(lane % HEAD < half, later, pltpu.roll(values, half, 1))
+
+
+def attend_kernel(
+    group, places_ref, raw_ref, key_ref, value_ref, cosine_ref, sine_ref, out_ref, total_ref, query_ref, bias
+):
+    keys, tokens = bias.shape
+    for first in range(0, raw_ref.shape[1], 2 * HEAD):
+        raw = raw_ref[:, first : first + 2 * HEAD].astype(jnp.float32)
+        turned = raw * cosine_ref[...] + halves_swapped(raw) * sine_ref[...]
+        query_ref[:, first : first + 2 * HEAD] = turned.astype(query_ref.dtype)
+
+    @pl.when(pl.program_id(0) == 0)
+    def _():
+        bias[...] = mask_bias(places_ref, keys, tokens)
+
+    for k in range(key_ref.shape[1] // HEAD):
+        key = key_ref[:, k * HEAD : (k + 1) * HEAD]
+        value = value_ref[:, k * HEAD : (k + 1) * HEAD]
+        for h in range(k * group, (k + 1) * group):
+            query = query_ref[:, h * HEAD : (h + 1) * HEAD]
+            scores = matmul_nt(key, query) * HEAD**-0.5 + bias[...]
+            largest = jnp.max(scores, axis=0, keepdims=True)
+            weights = jnp.exp(scores - largest)
+            total = jnp.sum(weights, axis=0, keepdims=True)
+            probs = (weights * (1.0 / total)).astype(query.dtype)
+            out = matmul_tn(value, probs)
+            out_ref[:, h * HEAD : (h + 1) * HEAD] = out.T.astype(out_ref.dtype)
+            total_ref[0, h : h + 1, :] = largest + jnp.log(total)
+
+
+def attend_back_kernel(
+    group, places_ref, query_ref, key_ref, value_ref, cosine_ref, sine_ref, total_ref, grad_ref,
+    query_out, pair_out, bias, turned
+):
+    keys, tokens = bias.shape
+
+    @pl.when(pl.program_id(0) == 0)
+    def _():
+        bias[...] = mask_bias(places_ref, keys, tokens)
+
+    for k in range(key_ref.shape[1] // HEAD):
+        lanes = slice(k * HEAD, (k + 1) * HEAD)
+        key, value = key_ref[:, lanes], value_ref[:, lanes]
+        grad_key = grad_value = None
+        for h in range(k * group, (k + 1) * group):
+            query = query_ref[:, h * HEAD : (h + 1) * HEAD]
+            grad = grad_ref[:, h * HEAD : (h + 1) * HEAD]
+            scores = matmul_nt(key, query) * HEAD**-0.5 + bias[...]
+            probs = jnp.exp(scores - total_ref[0, h : h + 1, :])
+            grad_probs = matmul_nt(value, grad)
+            inner_sum = jnp.sum(probs * grad_probs, axis=0, keepdims=True)
+            grad_scores = (probs * (grad_probs - inner_sum)).astype(query.dtype)
+            out = matmul_tn(key, grad_scores) * HEAD**-0.5
+            turned[:, h * HEAD : (h + 1) * HEAD] = out.T
+            key_term = jnp.dot(grad_scores, query, preferred_element_type=jnp.float32)
+            value_term = jnp.dot(
+                probs.astype(query.dtype), grad, preferred_element_type=jnp.float32
+            )
+            grad_key = key_term if grad_key is None else grad_key + key_term
+            grad_value = value_term if grad_value is None else grad_value + value_term
+        pair_out[0, :, lanes] = (grad_key * HEAD**-0.5).astype(pair_out.dtype)
+        pair_out[1, :, lanes] = grad_value.astype(pair_out.dtype)
+    for first in range(0, turned.shape[1], 2 * HEAD):
+        grad = turned[:, first : first + 2 * HEAD]
+        raw = grad * cosine_ref[...] - halves_swapped(grad) * sine_ref[...]
+        query_out[:, first : first + 2 * HEAD] = raw.astype(query_out.dtype)
+
+
+def attention_call(kernel, places, queries, pairs, waves, extra, extra_specs, outs, out_specs, scratch):
+    tokens, keys = queries.shape[0], pairs.shape[0]
+    steps = KV_HEADS // 2
+    group = Q_HEADS // KV_HEADS
+    wide = 2 * group * HEAD
+    return pl.pallas_call(
+        functools.partial(kernel, group),
+        grid=(steps,),
+        in_specs=[
+            pl.BlockSpec(memory_space=pltpu.SMEM),
+            pl.BlockSpec((tokens, wide), lambda g: (0, g)),
+            pl.BlockSpec((keys, 2 * HEAD), lambda g: (0, g)),
+            pl.BlockSpec((keys, 2 * HEAD), lambda g: (0, steps + g)),
+            *[pl.BlockSpec((tokens, 2 * HEAD), lambda g: (0, 0))] * 2,
+            *extra_specs,
+        ],
+        out_shape=outs,
+        out_specs=out_specs,
+        scratch_shapes=[pltpu.VMEM((keys, tokens), jnp.float32), *scratch],
+        compiler_params=pltpu.CompilerParams(vmem_limit_bytes=VMEM_LIMIT),
+        cost_estimate=pl.CostEstimate(
+            flops=8 * Q_HEADS * tokens * keys * HEAD,
+            bytes_accessed=8 * keys * Q_HEADS * HEAD,
+            transcendentals=Q_HEADS * tokens * keys,
+        ),
+    )(places, queries, pairs, pairs, *waves, *extra)
+
+
+def attend(places, raw, pairs, waves):
+    tokens, width = raw.shape[0], Q_HEADS * HEAD
+    steps = KV_HEADS // 2
+    heads = Q_HEADS // steps
+    return attention_call(
+        attend_kernel, places, raw, pairs, waves, [], [],
+        [
+            jax.ShapeDtypeStruct((tokens, width), raw.dtype),
+            jax.ShapeDtypeStruct((steps, heads, tokens), jnp.float32),
+            jax.ShapeDtypeStruct((tokens, width), raw.dtype),
+        ],
+        [
+            pl.BlockSpec((tokens, width // steps), lambda g: (0, g)),
+            pl.BlockSpec((1, heads, tokens), lambda g: (g, 0, 0)),
+            pl.BlockSpec((tokens, width // steps), lambda g: (0, g)),
+        ],
+        [],
+    )
+
+
+def attend_back(places, queries, pairs, waves, totals, grad):
+    tokens, width = queries.shape
+    steps = KV_HEADS // 2
+    wide = pl.BlockSpec((tokens, width // steps), lambda g: (0, g))
+    keys, pair_width = pairs.shape
+    return attention_call(
+        attend_back_kernel, places, queries, pairs, waves, [totals, grad],
+        [pl.BlockSpec((1, Q_HEADS // steps, tokens), lambda g: (g, 0, 0)), wide],
+        [
+            jax.ShapeDtypeStruct((tokens, width), queries.dtype),
+            jax.ShapeDtypeStruct((2, keys, pair_width // 2), queries.dtype),
+        ],
+        [wide, pl.BlockSpec((2, keys, 2 * HEAD), lambda g: (0, 0, g))],
+        [pltpu.VMEM((tokens, width // steps), jnp.float32)],
+    )
 
 
 def outer_kernel(values_ref, left_ref, other_ref, *refs):
@@ -719,7 +888,7 @@
     )(ids, table, weight)
 
 
-def scatter_go(place, ids_ref, grad_ref, base_ref, out_ref, held, sems, row_sems):
+def reach_go(place, grad_ref, held, sems, row_sems):
     row, col, rows, cols = place
     row_peers = [((row + k) % rows, col) for k in range(1, rows)]
     held[col, row] = grad_ref[row]
@@ -727,6 +896,16 @@
         push(grad_ref.at[peer[0]], held.at[col, row], (row_sems.at[0], row_sems.at[1]), k, peer)
         for k, peer in enumerate(row_peers)
     ]
+    yield
+    for copy in started:
+        copy.wait_recv()
+    yield from line_spread((row, col, cols), lambda d: held.at[d], sems, 0)
+    for copy in started:
+        copy.wait_send()
+
+
+def scatter_go(place, ids_ref, held_ref, base_ref, out_ref):
+    row, col, rows, cols = place
     tiles = out_ref.shape[1] // VOCAB_TILE
 
     def tile_of(d, source_ref):
@@ -735,7 +914,7 @@
             total = source_ref[:, pl.ds(first, VOCAB_TILE)].astype(jnp.float32)
             for k in range(rows):
                 total = total + lax.dot_general(
-                    held[d, k],
+                    held_ref[d, k],
                     one_hot_tile(ids_ref[d, k], first, VOCAB_TILE),
                     (((1,), (0,)), ((), ())),
                     preferred_element_type=jnp.float32,
@@ -746,24 +925,11 @@
         return tile
 
     yield
-    for copy in started:
-        copy.wait_recv()
-    spreading = line_spread((row, col, cols), lambda d: held.at[d], sems, 0)
-    next(spreading)
-    for first in range(0, tiles, TILES_AT_ONCE):
-        lax.fori_loop(first, min(tiles, first + TILES_AT_ONCE), tile_of(col, base_ref), 0)
-        next(spreading, None)
-        yield
-    for unused in spreading:
-        yield
-    for k in range(1, cols):
+    for d in range(cols):
         for first in range(0, tiles, TILES_AT_ONCE):
-            lax.fori_loop(
-                first, min(tiles, first + TILES_AT_ONCE), tile_of((col + k) % cols, out_ref), 0
-            )
+            last = min(tiles, first + TILES_AT_ONCE)
+            lax.fori_loop(first, last, tile_of(d, out_ref if d else base_ref), 0)
             yield
-    for copy in started:
-        copy.wait_send()
 
 
 def share_go(place, x_ref, out_ref, sems, row_sems):
@@ -944,8 +1110,6 @@
     width = features * row_count
     query_width = Q_HEADS * HEAD
     kv_width = KV_HEADS * HEAD
-    group_size = Q_HEADS // KV_HEADS
-    scaling = HEAD ** (-0.5)
     qkv_cols, out_cols, ff_cols = qkv_weight.shape[1], output_weight.shape[1], mlp_weight.shape[2]
     vocab_part = -(-(vocab_shard + 1) // (128 * row_count)) * 128
     vocab_room = vocab_part * row_count
@@ -1008,13 +1172,11 @@
     def rotate_here(values):
         return rotary(values, positions)
 
-    queries_raw = project[:, :query_width].astype(jnp.float32).reshape(device_tokens, Q_HEADS, HEAD)
     keys_raw = (
         project[:, query_width : query_width + kv_width]
         .astype(jnp.float32)
         .reshape(device_tokens, KV_HEADS, HEAD)
     )
-    queries = rotate_here(queries_raw).astype(low).reshape(device_tokens, KV_HEADS, group_size, HEAD)
     keys_local = rotate_here(keys_raw).astype(low).reshape(device_tokens, kv_width)
     own_pairs = jnp.concatenate([keys_local, project[:, query_width + kv_width :]], axis=1)
     keys_values, table_part = gather(own_pairs, padded, 8)
@@ -1022,29 +1184,15 @@
     left_full = lax.all_gather(left_block, "row", axis=0, tiled=True)
     keys_values = keys_values.reshape(LEN, 2 * kv_width)
     table_part = table_part.reshape(width, vocab_part)
-    attn_keys = keys_values[:, :kv_width].reshape(LEN, KV_HEADS, HEAD)
-    attn_values = keys_values[:, kv_width:].reshape(LEN, KV_HEADS, HEAD)
-    key_positions = jnp.arange(LEN, dtype=jnp.int32)
-    allowed = (key_positions[None, :] <= positions[:, None]) | (key_positions[None, :] < seq_prefix)
-
-    raw_scores = (
-        jnp.einsum("qhgd,khd->hgqk", queries, attn_keys, preferred_element_type=jnp.float32)
-        * scaling
-    )
-    scores = jnp.where(allowed, raw_scores, MASK_VALUE)
-    largest = jnp.max(scores, axis=-1, keepdims=True)
-    weights = jnp.exp(scores - largest)
-    attn_probs = weights / jnp.sum(weights, axis=-1, keepdims=True)
-    attended = (
-        jnp.einsum(
-            "hgqk,khd->qhgd",
-            attn_probs.astype(low),
-            attn_values,
-            preferred_element_type=jnp.float32,
-        )
-        .astype(low)
-        .reshape(device_tokens, query_width)
-    )
+    places = jnp.stack([first_token, seq_prefix])
+    frequency = jnp.power(10000.0, -jnp.arange(HEAD // 2, dtype=jnp.float32) / (HEAD // 2))
+    angles = positions[:, None].astype(jnp.float32) * frequency[None, :]
+    sine = jnp.sin(angles)
+    waves = [
+        jnp.tile(jnp.cos(angles), (1, 4)),
+        jnp.tile(jnp.concatenate([-sine, sine], axis=1), (1, 2)),
+    ]
+    attended, totals, queries = attend(places, project, keys_values, waves)
     hidden_one = embedded + over_columns(attended, out_full)
     middle = rms_norm(hidden_one, norm_gains[1]).astype(low)
     gate_part = by_columns(middle, gate_full, matmul)
@@ -1105,49 +1253,25 @@
     attn_grad = outer(
         grad_one_low, left_full, 1, attended, SMALL_BLOCK, attn_width, 0, None
     )
-    grad_attended = by_columns(grad_one_low, out_full, matmul).astype(low).reshape(
-        device_tokens, KV_HEADS, group_size, HEAD
-    )
-    grad_probs = jnp.einsum(
-        "qhgd,khd->hgqk", grad_attended, attn_values, preferred_element_type=jnp.float32
-    )
-    inner_sum = jnp.sum(attn_probs * grad_probs, axis=-1, keepdims=True)
-    grad_scores = (attn_probs * (grad_probs - inner_sum)).astype(low)
-    grad_queries = (
-        jnp.einsum("hgqk,khd->qhgd", grad_scores, attn_keys, preferred_element_type=jnp.float32)
-        * scaling
-    )
-    grad_keys = (
-        jnp.einsum("hgqk,qhgd->khd", grad_scores, queries, preferred_element_type=jnp.float32)
-        * scaling
-    )
-    grad_values = jnp.einsum(
-        "hgqk,qhgd->khd",
-        attn_probs.astype(low),
-        grad_attended,
-        preferred_element_type=jnp.float32,
-    )
-    grad_pairs = (
-        jnp.concatenate([grad_keys.reshape(LEN, kv_width), grad_values.reshape(LEN, kv_width)], axis=1)
-        .astype(low)
-        .reshape(col_count, device_tokens, 2 * kv_width)
-    )
+    grad_attended = by_columns(grad_one_low, out_full, matmul).astype(low)
+    grad_query_raw, grad_pairs = attend_back(
+        places, queries, keys_values, waves, totals, grad_attended
+    )
+    grad_pairs = grad_pairs.reshape(2, col_count, device_tokens, kv_width)
     pair_pieces = [
-        pick_block(grad_pairs, (col_index + col_count - k) % col_count, 0) for k in range(col_count)
+        pick_block(grad_pairs, (col_index + col_count - k) % col_count, 1) for k in range(col_count)
     ]
     grad_pairs = summed(deliver(pair_pieces, "col", -1))
-    unused, pull_query = jax.vjp(rotate_here, queries_raw)
-    grad_query_raw = pull_query(grad_queries.reshape(device_tokens, Q_HEADS, HEAD))[0]
     unused, pull_key = jax.vjp(rotate_here, keys_raw)
-    grad_key_raw = pull_key(grad_pairs[:, :kv_width].reshape(device_tokens, KV_HEADS, HEAD))[0]
+    grad_key_raw = pull_key(grad_pairs[0].reshape(device_tokens, KV_HEADS, HEAD))[0]
     grad_project = jnp.concatenate(
         [
-            grad_query_raw.reshape(device_tokens, query_width),
-            grad_key_raw.reshape(device_tokens, kv_width),
-            grad_pairs[:, kv_width:],
+            grad_query_raw,
+            grad_key_raw.reshape(device_tokens, kv_width).astype(low),
+            grad_pairs[1].astype(low),
         ],
         axis=1,
-    ).astype(low)
+    )
     attn_grad = outer(
         normed, left_full, 0, grad_project, SMALL_BLOCK, attn_width,
         query_width // SMALL_BLOCK, attn_grad,
@@ -1159,39 +1283,31 @@
     by_feature = grad_embedded.T.reshape(row_count, features, device_tokens)
     mlp_mean_later, by_feature, attn_grad = lax.optimization_barrier((mlp_mean, by_feature, attn_grad))
     attn_rows = reduce_rows(attn_grad)
-    mlp_new = soap(
+    mlp_moment, mlp_scale, mlp_next, token_grads, table_base, all_gains = soap(
         [mlp_rows],
         [feedforward_bases],
-        [(mlp_mean_later[j], mlp_square[j], mlp_weight[j], bases_low[2 + j]) for j in range(3)],
+        [mlp_mean_later, mlp_square, mlp_weight],
+        [bases_low[2 + j] for j in range(3)],
         (True, True, True),
         (2, 0, 1),
-        (grad_parts,),
+        (by_feature, grad_parts, own_gains),
         4,
     )
-    mlp_new, table_base = mlp_new[:3], mlp_new[3]
-    mlp_next, mlp_moment, mlp_scale = (
-        jnp.stack([entry[k] for entry in mlp_new]) for k in range(3)
-    )
-
     attn_rows, mlp_next = lax.optimization_barrier((attn_rows, mlp_next))
 
     def blocks(values):
         return jnp.moveaxis(values.reshape(values.shape[0], col_count, -1), 1, 0)
 
-    out_new, qkv_new, table_grad, all_gains = soap(
+    out_moment, out_scale, out_update, qkv_moment, qkv_scale, qkv_next, table_grad = soap(
         [blocks(attn_rows[:, :query_width]), blocks(attn_rows[:, query_width:])],
         [blocks(out_bases.astype(low)), blocks(qkv_bases.astype(low))],
-        [
-            (out_mean, out_square, output_weight, bases_low[1]),
-            (qkv_mean, qkv_square, qkv_weight, bases_low[0]),
-        ],
+        [out_mean, out_square, output_weight, qkv_mean, qkv_square, qkv_weight],
+        [bases_low[1], bases_low[0]],
         (False, True),
         (),
-        (local_tokens[:, :, :, None], by_feature, table_base, own_gains),
+        (local_tokens[:, :, :, None], token_grads, table_base),
         5,
     )
-    out_update, out_moment, out_scale = out_new
-    qkv_next, qkv_moment, qkv_scale = qkv_new
     table_grad = table_grad[:, :vocab_shard]
     gain_grads = jnp.sum(all_gains.reshape(row_count * col_count, 3, width), axis=0)
     embed_change, embed_moment, embed_scale = adam_update(

time: 935 us -> 902 us (0.965)
  matrix products: 156 us -> 109 us
  Pallas kernels: 600 us -> 624 us
  other arithmetic: 71.2 us -> 50.1 us
  waiting for transfers between devices: 7.62 us -> 22.9 us
    dot_general x5 -> x0, matrix products: 41.7 us -> none  [the longest x1 12.8 us: per_device(): jnp.einsum('qhgd,khd->hgqk', grad_attended, attn_values, preferred_elemen...]
    pallas_call x0 -> x2, Pallas kernels: none -> 39 us  [attention_call(): pl.pallas_call(functools.partial(kernel, group), grid=(steps,), in_specs=...]
    pallas_call x2, Pallas kernels: 284 us -> 269 us  [soap(): pl.pallas_call(functools.partial(soap_kernel, rows, cols, adds, streamed)...]
    convert_element_type x1, other arithmetic: 13.9 us -> 0.03 us  [per_device(): grad_key_raw.reshape(device_tokens, kv_width).astype(low)]
    sub x1 -> x0, matrix products: 11.1 us -> none  [per_device(): weights = jnp.exp(scores - largest)]
    unnamed x264 -> x231, local copies, waits for them, and re-layouts: 21.7 us -> 22.4 us
  transfers between devices with their start and end apart: 7 -> 7, of which waited for: 1 -> 2; matrix products, arithmetic and copies ran while one was open for 27% -> 20% of each run, Pallas kernels for 50% -> 58%
where the time goes in v4:
time: 902 us; the launch traced here: 893 us
  Pallas kernels  624 us (69%)
  matrix products  109 us (12%)
  local copies, waits for them, and re-layouts  55.7 us (6%)
  other arithmetic  50.1 us (6%)
  waiting for transfers between devices  22.9 us (3%)
  between operations  16.5 us (2%)
  blocking collectives  10.6 us (1%)
    pallas_call x2, Pallas kernels, soap(): pl.pallas_call(functools.partial(soap_kernel, rows, cols, adds, streamed)...  269 us
    pallas_call x1, Pallas kernels, lookup(): pl.pallas_call(functools.partial(lookup_kernel, rows, cols), out_shape=[j...  136 us
    pallas_call x1, Pallas kernels, gather(): pl.pallas_call(functools.partial(gather_kernel, rows, cols), out_shape=[j...  60.5 us
    dot_general x21, matrix products, matmul_last(): lax.dot_general(left_op, right_op, (((1,), (1,)), ((), ())), preferred_el...  50.2 us
    dot_general x22, matrix products, matmul(): return jnp.dot(left_op, right_op, preferred_element_type=jnp.float32)  49.4 us
    pallas_call x5, Pallas kernels, outer(): pl.pallas_call(outer_kernel, grid=(other.shape[1] // block,), out_shape=j...  39.1 us
    pallas_call x2, Pallas kernels, attention_call(): pl.pallas_call(functools.partial(kernel, group), grid=(steps,), in_specs=...  39 us
    pallas_call x1, Pallas kernels, fold(): pl.pallas_call(functools.partial(fold_kernel, rows, cols), out_shape=jax....  35.4 us
  transfers between devices with their start and end apart: 7, of which 2 were waited for; matrix products, arithmetic and copies ran while one was open for 20% of the time, Pallas kernels for 58%

profile of v4, /device:TPU:0, one launch (start us, length us, event | category | flops | bytes accessed | tf_op | source)
XLA Modules:
  0.0 892.9 jit_solution(649888980422350040)
XLA Ops:
  9.7 10.6 %all-gather.1 = s32[8,1,1152]{2,1,0:T(1,128)S(1)} all-gather(s32[1,1,1152]{2,1,0:T(1,128)S(1)} %reshape.325), channel_id=2, replica_groups=mesh['row'=8,'col'=4] {'row'}, dimensions={0}, use_global_device_ids=true | all-gather | bytes 41472 | tf_op jit(solution)/shard_map/all_gather | solution.py:1117
  21.6 2.9 convert_bitcast_fusion
  27.0 136.0 %shard_map.351 = (bf16[8,144,256]{2,1,0:T(8,128)(2,1)}, bf16[4,8,144,768]{3,2,1,0:T(8,128)(2,1)}) custom-call(s32[8192]{0:T(1024)} %bitcast.314, bf16[144,8192]{1,0:T(8,128)(2,1)} %pad.10.table_ref, bf16[144,768]{1,0:T(8,128)(2,1)} %pad_maximum_fusion.10.weight_ref), custom_call_target="tpu_custom_call" | custom-call | tf_op jit(solution)/shard_map/pallas_call | solution.py:864
  164.6 2.2 convert_element_type.138
  167.2 2.1 convolution_convert_fusion.4
  169.4 1.9 convolution_convert_fusion.3
  173.0 1.9 copy.119
  181.6 60.5 %shard_map.352 = (bf16[4,256,768]{2,1,0:T(8,128)(2,1)}, bf16[8,144,1024]{2,1,0:T(8,128)(2,1)}) custom-call(bf16[256,768]{1,0:T(8,128)(2,1)} %pad_maximum_fusion.5.x_ref, bf16[144,8192]{1,0:T(8,128)(2,1)} %pad.10.table_ref), custom_call_target="tpu_custom_call" | custom-call | tf_op jit(solution)/shard_map/pallas_call | solution.py:971
  245.9 1.9 convolution_convert_fusion.6
  248.0 1.9 convolution_convert_fusion.5
  257.0 18.6 %shard_map.353 = (bf16[256,1152]{1,0:T(8,128)(2,1)}, f32[3,6,256]{2,1,0:T(8,128)}, bf16[256,1152]{1,0:T(8,128)(2,1)}) custom-call(s32[2]{0:T(128)} %pad_add_fusion.1.places_ref, bf16[256,1920]{1,0:T(8,128)(2,1)} %concatenate.53.raw_ref, bf16[1024,768]{1,0:T(8,128)(2,1)} %bitcast.321, bf16[1024,768]{1,0:T(8,128)(2,1)} %bitcast.322, ...), custom_call_target="tpu_custom_call" | custom-call | flops 2415919104 | bytes 9437184 | tf_op jit(solution)/shard_map/pallas_call | solution.py:668
  275.6 1.9 fusion.33
  279.3 2.0 convolution_add_fusion.13
  281.4 2.8 multiply_reduce_fusion.6
  285.1 2.4 fusion.16
  287.5 3.1 fusion.15
  290.6 3.3 fusion.14
  293.9 2.4 fusion.13
  296.4 2.4 fusion.11
  298.8 2.4 fusion.10
  309.7 30.2 %shard_map.354 = bf16[8,4,32,1152]{3,2,1,0:T(8,128)(2,1)} custom-call(bf16[4,32,1152]{2,1,0:T(8,128)(2,1)} %bitcast.307), custom_call_target="tpu_custom_call" | custom-call | tf_op jit(solution)/shard_map/pallas_call | solution.py:148
  340.0 4.7 select_reduce_fusion.1
  344.6 2.2 exponential_reduce_fusion
  348.8 15.1 %shard_map.355 = f32[8,4,24,128]{3,2,1,0:T(8,128)} custom-call(f32[24,128]{1,0:T(8,128)} %reshape.304.x_ref), custom_call_target="tpu_custom_call" | custom-call | tf_op jit(solution)/shard_map/pallas_call | solution.py:83
  363.9 1.9 reshape.305
  365.8 2.1 slice_reduce_fusion
  369.3 8.5 convolution_convert_fusion.1
  377.8 35.4 %shard_map.356 = bf16[4,32,1152]{2,1,0:T(8,128)(2,1)} custom-call(bf16[8,4,32,1152]{3,2,1,0:T(8,128)(2,1)} %bitcast.299), custom_call_target="tpu_custom_call" | custom-call | tf_op jit(solution)/shard_map/pallas_call | solution.py:227
  413.3 2.2 multiply_reduce_fusion
  415.7 2.5 fusion.21
  418.2 2.2 fusion.20
  420.4 2.2 fusion.19
  422.6 2.3 fusion.17
  427.4 2.1 fusion.4.other_ref
  429.5 8.0 shard_map.357.refs_0_
  437.5 8.5 shard_map.358.refs_0_
  445.9 8.1 shard_map.359
  454.1 2.4 fusion.7
  456.6 2.3 fusion.12
  458.9 2.7 convolution_add_fusion.5
  461.6 2.7 convolution_add_fusion.4
  464.3 2.6 convolution_add_fusion.3
  466.9 2.6 convolution_add_fusion.2
  469.6 2.6 convolution_add_fusion.1
  472.2 3.6 multiply_reduce_fusion.1
  477.6 2.4 convolution_convert_fusion.10
  480.2 2.8 convolution_convert_fusion.9
  483.2 2.2 convolution_convert_fusion.8
  485.5 2.1 convolution_convert_fusion.7
  489.2 20.4 %shard_map.360 = (bf16[256,1152]{1,0:T(8,128)(2,1)}, bf16[2,1024,384]{2,1,0:T(8,128)(2,1)}) custom-call(s32[2]{0:T(128)} %pad_add_fusion.1.places_ref, bf16[256,1152]{1,0:T(8,128)(2,1)} %get-tuple-element.61.query_ref, bf16[1024,768]{1,0:T(8,128)(2,1)} %bitcast.323, bf16[1024,768]{1,0:T(8,128)(2,1)} %bitcast.324, f32[256,128]{1,0:T(8,128)} %copy.121.cosine_ref, ...), custom_call_target="tpu_custom_call" | custom-call | flops 2415919104 | bytes 9437184 | tf_op jit(solution)/shard_map/pallas_call | solution.py:668
  509.6 2.2 dynamic-slice_bitcast_fusion.2
  513.0 3.0 collective-permute-start.1
  517.9 6.5 shard_map.361.refs_0_
  526.3 14.1 %collective-permute-done.1 = bf16[2,256,384]{2,1,0:T(8,128)(2,1)S(1)} collective-permute-done((bf16[2,256,384]{2,1,0:T(8,128)(2,1)S(1)}, bf16[2,256,384]{2,1,0:T(8,128)(2,1)S(1)}, u32[]{:S(2)}, u32[]{:S(2)}) %collective-permute-start.1) | collective-permute-done | bytes 393248 | tf_op jit(solution)/shard_map/ppermute | solution.py:988
  547.8 2.2 multiply_reduce_fusion.2
  553.4 8.1 shard_map.362
  564.6 3.3 copy.141
  568.0 2.4 copy.142
  570.4 2.7 copy.143.refs_12_
  575.5 6.9 convolution_convert_fusion
  583.0 8.6 reduce-scatter.5.cloned.1.call-done.refs_0_
  591.6 190.0 %shard_map.363 = (f32[3,144,768]{2,1,0:T(8,128)}, f32[3,144,768]{2,1,0:T(8,128)}, f32[3,144,768]{2,1,0:T(8,128)}, bf16[4,8,144,256]{3,2,1,0:T(8,128)(2,1)}, bf16...) custom-call(bf16[144,9216]{1,0:T(8,128)(2,1)} %reduce-scatter.5.cloned.1.call-done.refs_0_, f32[3,768,3072]{2,1,0:T(8,128)} %refs_1_.1, ...), custom_call_target="tpu_custom_call" | custom-call | tf_op jit(solution)/shard_map/pallas_call | solution.py:560
  785.6 78.9 %shard_map.364 = (f32[144,288]{1,0:T(8,128)}, f32[144,288]{1,0:T(8,128)}, f32[144,288]{1,0:T(8,128)}, f32[144,480]{1,0:T(8,128)}, f32[144,480]{1,0:T(8,128)}, /*index=5*/f32[144,480]{1,0:T(8,128)}, f32[144,8192]{1,0:T(8,128)}) custom-call(bf16[4,144,288]{2,1,0:T(8,128)(2,1)} %bitcast.301, bf16[4,144,480]{2,1,0:T(8,128)(2,1)} %bitcast.296, ...), custom_call_target="tpu_custom_call" | custom-call | tf_op jit(solution)/shard_map/pallas_call | solution.py:560
  864.5 12.8 %negate_add_fusion = (f32[8000,144]{0,1:T(8,128)}, f32[8000,144]{0,1:T(8,128)}, f32[8000,144]{0,1:T(8,128)}) fusion(f32[8000,144]{0,1:T(8,128)} %param.29, f32[144,8192]{1,0:T(8,128)} %get-tuple-element.73, f32[8000,144]{0,1:T(8,128)} %param.35, f32[8000,144]{0,1:T(8,128)} %param.34), kind=kLoop, calls=%fused_computation.4 | loop fusion | flops 14976000 | bytes 32256000 | tf_op jit(solution)/shard_map/add | solution.py:1316
  (343 shorter events, 82.4 us)
Async XLA Ops:
  7.2 277.9 %all-gather.5.cloned.1.call-start = ((), (), s32[]{:S(2)}) async-start(), calls=%async_computation.2 | async-start | bytes 21897216 | tf_op jit(solution)/shard_map/all_gather | solution.py:1122
  8.6 12.9 %copy-start.48 = (f32[144,288]{1,0:T(8,128)S(1)}, f32[144,288]{1,0:T(8,128)}, u32[]{:S(2)}) copy-start(f32[144,288]{1,0:T(8,128)} %refs_6_.1) | copy-start | bytes 497668
  8.7 12.9 %copy-start.45 = (f32[144,480]{1,0:T(8,128)S(1)}, f32[144,480]{1,0:T(8,128)}, u32[]{:S(2)}) copy-start(f32[144,480]{1,0:T(8,128)} %refs_9_.1) | copy-start | bytes 829444
  9.6 419.9 %all-gather.7.cloned.1.call-start = ((), (), s32[]{:S(2)}) async-start(), calls=%async_computation.3 | async-start | bytes 14929920 | tf_op jit(solution)/shard_map/all_gather | solution.py:1184
  166.7 78.4 %copy-start.3 = (bf16[5,144,1152]{2,1,0:T(8,128)(2,1)}, bf16[5,144,1152]{2,1,0:T(8,128)(2,1)S(1)}, u32[]{:S(2)}) copy-start(bf16[5,144,1152]{2,1,0:T(8,128)(2,1)S(1)} %convert_element_type.138) | copy-start | bytes 4976644
  167.2 80.8 %copy-start.37 = (bf16[256,1152]{1,0:T(8,128)(2,1)}, bf16[256,1152]{1,0:T(8,128)(2,1)S(1)}, u32[]{:S(2)}) copy-start(bf16[256,1152]{1,0:T(8,128)(2,1)S(1)} %multiply_convert_fusion.5.values_ref) | copy-start | bytes 1769476
  169.4 3.6 copy-start.46
  176.2 73.8 %copy-start.50 = (f32[256,32]{0,1:T(8,128)}, f32[256,32]{0,1:T(8,128)S(1)}, u32[]{:S(2)}) copy-start(f32[256,32]{0,1:T(8,128)S(1)} %get-tuple-element.133) | copy-start | bytes 98308
  176.2 74.6 %copy-start.52 = (f32[256,32]{0,1:T(8,128)}, f32[256,32]{0,1:T(8,128)S(1)}, u32[]{:S(2)}) copy-start(f32[256,32]{0,1:T(8,128)S(1)} %get-tuple-element.132) | copy-start | bytes 98308
  245.9 345.7 %reduce-scatter.5.cloned.1.call-start = ((), (), s32[]{:S(2)}) async-start(), calls=%async_computation.5 | async-start | bytes 23887872 | tf_op jit(solution)/shard_map/reduce_scatter | solution.py:1154
  247.9 2.9 copy-start.63
  248.0 3.7 copy-start.84
  248.0 5.0 copy-start.40
  248.0 5.0 copy-start.47
  249.9 4.7 copy-start.106
  284.2 3.2 copy-start.87
  284.2 3.2 copy-start.72
  285.0 16.9 %copy-start.19 = (bf16[256,1152]{1,0:T(8,128)(2,1)}, bf16[256,1152]{1,0:T(8,128)(2,1)S(1)}, u32[]{:S(2)}) copy-start(bf16[256,1152]{1,0:T(8,128)(2,1)S(1)} %multiply_convert_fusion.4.values_ref) | copy-start | bytes 1769476
  285.1 16.2 %copy-start.5 = (bf16[4608,2304]{1,0:T(8,128)(2,1)S(1)}, bf16[4608,2304]{1,0:T(8,128)(2,1)}, u32[]{:S(2)}) copy-start(bf16[4608,2304]{1,0:T(8,128)(2,1)} %all-gather.5.cloned.1.call-done) | copy-start | bytes 63700996
  287.5 15.2 %copy-start.25 = (f32[256,768]{1,0:T(8,128)}, f32[256,768]{1,0:T(8,128)S(1)}, u32[]{:S(2)}) copy-start(f32[256,768]{1,0:T(8,128)S(1)} %fusion.16) | copy-start | bytes 2359300
  290.6 12.0 %copy-start.27 = (f32[256,768]{1,0:T(8,128)}, f32[256,768]{1,0:T(8,128)S(1)}, u32[]{:S(2)}) copy-start(f32[256,768]{1,0:T(8,128)S(1)} %fusion.15) | copy-start | bytes 2359300
  293.9 8.8 copy-start.29
  296.4 6.3 copy-start.31
  298.8 3.9 copy-start.11
  308.7 31.3 %copy-start.102 = (pred[1024]{0:T(1024)(128)(4,1)S(1)}, pred[1024]{0:T(1024)(128)(4,1)}, u32[]{:S(2)}) copy-start(pred[1024]{0:T(1024)(128)(4,1)} %iota_compare_fusion.1) | copy-start | bytes 3076
  308.7 31.3 %copy-start.105 = (bf16[8,144,1024]{2,1,0:T(8,128)(2,1)S(1)}, bf16[8,144,1024]{2,1,0:T(8,128)(2,1)}, u32[]{:S(2)}) copy-start(bf16[8,144,1024]{2,1,0:T(8,128)(2,1)} %get-tuple-element.57) | copy-start | bytes 7077892
  339.9 4.7 copy-start.82
  369.3 8.5 copy-start.96
  369.3 8.5 copy-start.98
  377.8 35.4 %copy-start.67 = (f32[256]{0:T(256)S(1)}, f32[256]{0:T(256)}, u32[]{:S(2)}) copy-start(f32[256]{0:T(256)} %copy-done.66) | copy-start | bytes 3076
  377.8 35.4 %copy-start.92 = (s32[256]{0:T(256)S(1)}, s32[256]{0:T(256)}, u32[]{:S(2)}) copy-start(s32[256]{0:T(256)} %get-tuple-element.141) | copy-start | bytes 3076
  377.8 35.4 %copy-start.101 = (s32[128]{0:T(128)S(1)}, s32[128]{0:T(128)}, u32[]{:S(2)}) copy-start(s32[128]{0:T(128)} %param.26) | copy-start | bytes 1540
  415.4 2.8 copy-start
  415.4 2.8 copy-start.77
  415.7 6.8 copy-start.38
  454.0 327.6 %reduce-scatter.3.cloned.1.call-start = ((), (), s32[]{:S(2)}) async-start(), calls=%async_computation.4 | async-start | bytes 7962624 | tf_op jit(solution)/shard_map/reduce_scatter | solution.py:1154
  469.5 2.6 copy-start.73
  472.2 3.6 copy-start.88
  472.2 3.6 copy-start.1
  472.2 3.6 copy-start.68
  472.2 3.6 copy-start.78
  480.0 3.2 copy-start.36
  509.6 6.5 copy-start.20
  511.8 14.5 %collective-permute-start.2 = (bf16[2,256,384]{2,1,0:T(8,128)(2,1)}, bf16[2,256,384]{2,1,0:T(8,128)(2,1)S(1)}, u32[]{:S(2)}, u32[]{:S(2)}) collective-permute-start(bf16[2,256,384]{2,1,0:T(8,128)(2,1)} %get-tuple-element.116), channel_id=1, source_target_pairs={{0,1},{1,2},{2,3},{3,0},{4,5},{5,6},{6,7},{7,4},{8,9},{9,10},{10,1... | collective-permute-start | bytes 1179656 | tf_op jit(solution)/shard_map/ppermute | solution.py:988
  513.0 27.4 %collective-permute-start.1 = (bf16[2,256,384]{2,1,0:T(8,128)(2,1)S(1)}, bf16[2,256,384]{2,1,0:T(8,128)(2,1)S(1)}, u32[]{:S(2)}, u32[]{:S(2)}) collective-permute-start(bf16[2,256,384]{2,1,0:T(8,128)(2,1)S(1)} %get-tuple-element.117), channel_id=1, source_target_pairs={{0,2},{1,3},{2,0},{3,1},{4,6},{5,7},{6,4},{7,5},{8,10},{9,11},{10,... | collective-permute-start | bytes 1179656 | tf_op jit(solution)/shard_map/ppermute | solution.py:988
  516.0 24.3 %collective-permute-start = (bf16[2,256,384]{2,1,0:T(8,128)(2,1)S(1)}, bf16[2,256,384]{2,1,0:T(8,128)(2,1)}, u32[]{:S(2)}, u32[]{:S(2)}) collective-permute-start(bf16[2,256,384]{2,1,0:T(8,128)(2,1)S(1)} %get-tuple-element.115), channel_id=1, source_target_pairs={{0,3},{1,0},{2,1},{3,2},{4,7},{5,4},{6,5},{7,6},{8,11},{9,8},{10,9... | collective-permute-start | bytes 1179656 | tf_op jit(solution)/shard_map/ppermute | solution.py:988
  526.2 17.3 %copy-start.51 = (f32[256,32]{0,1:T(8,128)S(1)}, f32[256,32]{0,1:T(8,128)}, u32[]{:S(2)}) copy-start(f32[256,32]{0,1:T(8,128)} %copy-done.50) | copy-start | bytes 98308
  526.3 17.3 %copy-start.53 = (f32[256,32]{0,1:T(8,128)S(1)}, f32[256,32]{0,1:T(8,128)}, u32[]{:S(2)}) copy-start(f32[256,32]{0,1:T(8,128)} %copy-done.52) | copy-start | bytes 98308
  547.8 2.7 copy-start.22
  547.8 2.7 copy-start.69
  547.8 2.6 copy-start.74
  547.8 2.6 copy-start.79
  547.8 2.6 copy-start.86
  570.3 2.7 copy-start.4
  864.4 12.9 %copy-start.65 = (f32[3,1152]{1,0:T(4,128)S(1)}, f32[3,1152]{1,0:T(4,128)}, u32[]{:S(2)}) copy-start(f32[3,1152]{1,0:T(4,128)} %param.30) | copy-start | bytes 41476
  864.4 12.9 %copy-start.75 = (f32[3,1152]{1,0:T(4,128)S(1)}, f32[3,1152]{1,0:T(4,128)}, u32[]{:S(2)}) copy-start(f32[3,1152]{1,0:T(4,128)} %param.37) | copy-start | bytes 41476
  864.5 12.9 %copy-start.76 = (f32[3,1152]{1,0:T(4,128)S(1)}, f32[3,1152]{1,0:T(4,128)}, u32[]{:S(2)}) copy-start(f32[3,1152]{1,0:T(4,128)} %param.36) | copy-start | bytes 41476
  864.5 13.5 %copy-start.56 = (f32[144,480]{1,0:T(8,128)S(1)}, f32[144,480]{1,0:T(8,128)}, u32[]{:S(2)}) copy-start(f32[144,480]{1,0:T(8,128)} %get-tuple-element.166) | copy-start | bytes 829444
  864.5 14.2 %copy-start.55 = (f32[144,480]{1,0:T(8,128)S(1)}, f32[144,480]{1,0:T(8,128)}, u32[]{:S(2)}) copy-start(f32[144,480]{1,0:T(8,128)} %get-tuple-element.167) | copy-start | bytes 829444
  864.5 15.0 %copy-start.54 = (f32[144,480]{1,0:T(8,128)S(1)}, f32[144,480]{1,0:T(8,128)}, u32[]{:S(2)}) copy-start(f32[144,480]{1,0:T(8,128)} %get-tuple-element.168) | copy-start | bytes 829444
  864.5 15.7 %copy-start.59 = (f32[144,288]{1,0:T(8,128)S(1)}, f32[144,288]{1,0:T(8,128)}, u32[]{:S(2)}) copy-start(f32[144,288]{1,0:T(8,128)} %get-tuple-element.169) | copy-start | bytes 497668
  877.3 3.5 copy-start.58
  877.4 4.2 copy-start.57
  877.4 4.9 copy-start.44
  (52 other events, 98.4 us)
Sparse Core Ops, SparseCore 0:
  11.5 199.5 all-gather.4
  246.0 73.2 all-gather.6
  454.1 137.4 reduce-scatter.4
  595.0 75.2 reduce-scatter.2

commit v5 on v4

--- a/solution.py
+++ b/solution.py
@@ -538,13 +538,12 @@
     if streamed:
         width = kept[0].shape[2]
         grad, parts, own = others
-        specs += [vmem, anywhere, vmem]
+        specs += [vmem] * 3
         outs += [
             jax.ShapeDtypeStruct((cols, *grad.shape), grad.dtype),
             jax.ShapeDtypeStruct((parts.shape[1], parts.shape[0] * parts.shape[2]), parts.dtype),
             jax.ShapeDtypeStruct((rows, cols, *own.shape), own.dtype),
         ]
-        out_specs = [vmem] * (len(outs) - 2) + [anywhere, vmem]
         scratch += [
             pltpu.VMEM((len(adds), cols, width, width), low),
             pltpu.VMEM((2, width // 2, width), jnp.float32),
@@ -556,12 +555,11 @@
     else:
         specs += [vmem] * 3
         outs += [jax.ShapeDtypeStruct(others[2].shape, jnp.float32)]
-        out_specs = [vmem] * len(outs)
     return pl.pallas_call(
         functools.partial(soap_kernel, rows, cols, adds, streamed),
         out_shape=outs,
         in_specs=specs,
-        out_specs=out_specs,
+        out_specs=[vmem] * len(outs),
         scratch_shapes=scratch,
         compiler_params=pltpu.CompilerParams(
             collective_id=collective_id, has_side_effects=True, vmem_limit_bytes=SOAP_VMEM
@@ -732,10 +730,10 @@
     def _():
         turned[...] = jnp.dot(
             values_ref[...], left_ref[...], preferred_element_type=jnp.float32
-        ).astype(turned.dtype)
-
-    out_ref[...] = lax.dot_general(
-        turned[...], other_ref[...], (((0,), (0,)), ((), ())), preferred_element_type=jnp.float32
+        ).T.astype(turned.dtype)
+
+    out_ref[...] = jnp.dot(
+        turned[...], other_ref[...], preferred_element_type=jnp.float32
     ).astype(out_ref.dtype)
 
 
@@ -758,7 +756,7 @@
         out_shape=jax.ShapeDtypeStruct((width, total), values.dtype),
         in_specs=specs,
         out_specs=pl.BlockSpec((width, block), lambda j: (0, at + j)),
-        scratch_shapes=[pltpu.VMEM((tokens, width), values.dtype)],
+        scratch_shapes=[pltpu.VMEM((width, tokens), values.dtype)],
         input_output_aliases=aliases,
         compiler_params=pltpu.CompilerParams(vmem_limit_bytes=VMEM_LIMIT),
         cost_estimate=pl.CostEstimate(
@@ -774,20 +772,74 @@
     return jnp.where(ids - first == columns, 1.0, 0.0).astype(jnp.bfloat16)
 
 
+def line_up_kernel(rows, cols, *refs):
+    row, col = lax.axis_index("row"), lax.axis_index("col")
+    count = (len(refs) - 8) // 3
+    blocks, ids_ref, table_ref = refs[:count], refs[count], refs[count + 1]
+    wholes, all_ref, swapped_ref = refs[count + 2 : 2 * count + 2], refs[2 * count + 2], refs[2 * count + 3]
+    row_sems, local_sems, swap_sems, swap_local = refs[2 * count + 4 : 2 * count + 8]
+    greet(line_peers(row, col, cols) + [((row + k) % rows, col) for k in range(1, rows)])
+    all_ref[row] = ids_ref[...]
+    copies = [
+        push(all_ref.at[row], all_ref.at[row], (row_sems.at[0], row_sems.at[1]), k - 1, ((row + k) % rows, col))
+        for k in range(1, rows)
+    ]
+    running = []
+    for k, (block, whole) in enumerate(zip(blocks, wholes, strict=True)):
+        width = block.shape[1]
+
+        def lies_at(d, whole=whole, width=width):
+            return whole.at[:, pl.ds(pl.multiple_of(d * width, width), width)]
+
+        own = pltpu.make_async_copy(block, lies_at(col), local_sems.at[k])
+        own.start()
+        own.wait()
+        running.append(line_spread((row, col, cols), lies_at, refs[2 * count + 8 + k], 0))
+    span = swapped_ref.shape[2]
+
+    def part_of(k):
+        return table_ref.at[:, pl.ds(pl.multiple_of(k * span, span), span)]
+
+    place = (row, col, rows, cols)
+    running.append(swap_go(place, part_of, lambda k: swapped_ref.at[k], swap_sems, swap_local))
+    while running:
+        running = [m for m in running if next(m, "done") != "done"]
+    for copy in copies:
+        copy.wait()
+
+
+def line_up(blocks, ids, table, collective_id):
+    rows, cols = lax.axis_size("row"), lax.axis_size("col")
+    dma = pltpu.SemaphoreType.DMA
+    vmem = pl.BlockSpec(memory_space=pltpu.VMEM)
+    return pl.pallas_call(
+        functools.partial(line_up_kernel, rows, cols),
+        out_shape=[
+            jax.ShapeDtypeStruct((block.shape[0], cols * block.shape[1]), block.dtype)
+            for block in blocks
+        ]
+        + [
+            jax.ShapeDtypeStruct((rows, *ids.shape), ids.dtype),
+            jax.ShapeDtypeStruct((rows, table.shape[0], table.shape[1] // rows), table.dtype),
+        ],
+        in_specs=[vmem] * (len(blocks) + 2),
+        out_specs=[vmem] * (len(blocks) + 2),
+        scratch_shapes=[dma((2, rows - 1)), dma((len(blocks),)), dma((2, rows - 1)), dma]
+        + [dma((2, 2 * (cols - 1)))] * len(blocks),
+        compiler_params=pltpu.CompilerParams(
+            collective_id=collective_id, has_side_effects=True, vmem_limit_bytes=VMEM_LIMIT
+        ),
+    )(*blocks, ids, table)
+
+
 def lookup_kernel(
-    rows, cols, ids_ref, table_ref, weight_ref, out_ref, whole_ref,
-    table, taken, found, inbox, summed_ref, sems, row_sems, local_sem, col_sems, chip_sems, core_sems,
+    rows, cols, ids_ref, table_ref, out_ref,
+    table, taken, found, inbox, summed_ref, sems, row_sems,
 ):
     row, col = lax.axis_index("row"), lax.axis_index("col")
     row_peers = [((row + k) % rows, col) for k in range(1, rows)]
-    other = (row // 2 * 2 + 1 - row % 2, col)
     line = (row, col, cols)
     greet(line_peers(row, col, cols) + row_peers)
-    own = pltpu.make_async_copy(weight_ref, whole_ref.at[col, row], local_sem)
-    own.start()
-    own.wait()
-    spreading = line_spread(line, lambda d: whole_ref.at[d, row], col_sems, 0)
-    next(spreading)
     features, tokens = out_ref.shape[1:]
     planes = [(k, min(128, features - 128 * k)) for k in range(table.shape[1])]
 
@@ -827,15 +879,6 @@
             e = jnp.where(col == i, orders[i][k], e)
         look(e)
         next(summing)
-        next(spreading, None)
-    for unused in spreading:
-        pass
-    mine = whole_ref.at[:, row]
-    chips = [
-        push(mine, mine, (chip_sems.at[0], chip_sems.at[1]), k - 1, peer)
-        for k, peer in enumerate(same_core(row, col, rows), 1)
-    ]
-    core = [push(mine, mine, (core_sems.at[0], core_sems.at[1]), 0, other)]
     look(col)
     for unused in summing:
         pass
@@ -844,17 +887,11 @@
         push(summed_ref.at[peer[0]], out_ref.at[row], (row_sems.at[0], row_sems.at[1]), k, peer)
         for k, peer in enumerate(row_peers)
     ]
-    for k, arrived in enumerate(chips, 1):
-        arrived.wait_recv()
-        block = whole_ref.at[:, (row + rows - 2 * k) % rows]
-        core.append(push(block, block, (core_sems.at[0], core_sems.at[1]), k, other))
-    for copy in copies + core:
-        copy.wait_recv()
-    for copy in copies + core + chips:
-        copy.wait_send()
-
-
-def lookup(ids, table, weight, tokens, collective_id):
+    for copy in copies:
+        copy.wait()
+
+
+def lookup(ids, table, tokens, collective_id):
     rows, cols = lax.axis_size("row"), lax.axis_size("col")
     features, count = table.shape
     planes = -(-features // 128)
@@ -863,12 +900,9 @@
     block = (rows, features, tokens)
     return pl.pallas_call(
         functools.partial(lookup_kernel, rows, cols),
-        out_shape=[
-            jax.ShapeDtypeStruct(block, table.dtype),
-            jax.ShapeDtypeStruct((cols, rows, *weight.shape), weight.dtype),
-        ],
-        in_specs=[pl.BlockSpec(memory_space=pltpu.SMEM), vmem, pl.BlockSpec(memory_space=pl.ANY)],
-        out_specs=[vmem, pl.BlockSpec(memory_space=pl.ANY)],
+        out_shape=jax.ShapeDtypeStruct(block, table.dtype),
+        in_specs=[pl.BlockSpec(memory_space=pltpu.SMEM), vmem],
+        out_specs=vmem,
         scratch_shapes=[
             pltpu.VMEM((count, planes, 128), jnp.float32),
             pltpu.VMEM((tokens, planes, 128), jnp.float32),
@@ -877,15 +911,11 @@
             pltpu.VMEM(block, table.dtype),
             dma((2, 2 * (cols - 1))),
             dma((2, rows - 1)),
-            dma,
-            dma((2, 2 * (cols - 1))),
-            dma((2, rows // 2 - 1)),
-            dma((2, rows // 2)),
         ],
         compiler_params=pltpu.CompilerParams(
             collective_id=collective_id, has_side_effects=True, vmem_limit_bytes=VMEM_LIMIT
         ),
-    )(ids, table, weight)
+    )(ids, table)
 
 
 def reach_go(place, grad_ref, held, sems, row_sems):
@@ -945,42 +975,27 @@
         copy.wait()
 
 
-def gather_kernel(rows, cols, x_ref, table_ref, out_ref, swapped_ref, sems, row_sems, local_sem):
+def gather_kernel(rows, cols, x_ref, out_ref, sems):
     row, col = lax.axis_index("row"), lax.axis_index("col")
-    greet(line_peers(row, col, cols) + [((row + k) % rows, col) for k in range(1, rows)])
+    greet(line_peers(row, col, cols))
     out_ref[col] = x_ref[...]
-    spreading = line_spread((row, col, cols), lambda d: out_ref.at[d], sems, 0)
-    next(spreading)
-    count = swapped_ref.shape[2]
-
-    def part_of(k):
-        return table_ref.at[:, pl.ds(pl.multiple_of(k * count, count), count)]
-
-    swapping = swap_go((row, col, rows, cols), part_of, lambda k: swapped_ref.at[k], row_sems, local_sem)
-    next(swapping)
-    for unused in spreading:
+    for unused in line_spread((row, col, cols), lambda d: out_ref.at[d], sems, 0):
         pass
-    for unused in swapping:
-        pass
-
-
-def gather(value, table, collective_id):
+
+
+def gather(value, collective_id):
     rows, cols = lax.axis_size("row"), lax.axis_size("col")
-    dma = pltpu.SemaphoreType.DMA
-    vmem, anywhere = pl.BlockSpec(memory_space=pltpu.VMEM), pl.BlockSpec(memory_space=pl.ANY)
+    vmem = pl.BlockSpec(memory_space=pltpu.VMEM)
     return pl.pallas_call(
         functools.partial(gather_kernel, rows, cols),
-        out_shape=[
-            jax.ShapeDtypeStruct((cols, *value.shape), value.dtype),
-            jax.ShapeDtypeStruct((rows, table.shape[0], table.shape[1] // rows), table.dtype),
-        ],
-        in_specs=[vmem, anywhere],
-        out_specs=[vmem, anywhere],
-        scratch_shapes=[dma((2, 2 * (cols - 1))), dma((2, rows - 1)), dma],
+        out_shape=jax.ShapeDtypeStruct((cols, *value.shape), value.dtype),
+        in_specs=[vmem],
+        out_specs=vmem,
+        scratch_shapes=[pltpu.SemaphoreType.DMA((2, 2 * (cols - 1)))],
         compiler_params=pltpu.CompilerParams(
             collective_id=collective_id, has_side_effects=True, vmem_limit_bytes=VMEM_LIMIT
         ),
-    )(value, table)
+    )(value)
 
 
 def send(value, axis, shift):
@@ -1114,22 +1129,40 @@
     vocab_part = -(-(vocab_shard + 1) // (128 * row_count)) * 128
     vocab_room = vocab_part * row_count
 
-    ids_all = lax.all_gather(jnp.concatenate([token_ids, target_ids]), "row", axis=0)
-    table_first, ids_all = lax.optimization_barrier((embed_table, ids_all))
+    low_weights = [weight.astype(low) for weight in (qkv_weight, output_weight, *mlp_weight)]
+    own_ids = jnp.concatenate([token_ids, target_ids]).reshape(-1, 128)
+    table_low_t = embed_table.astype(low).T
+    padded = jnp.pad(table_low_t, ((0, 0), (0, vocab_room - vocab_shard)))
+    attn_line, mlp_line, ids_all, table_part = line_up(
+        [jnp.concatenate(low_weights[:2], axis=1), jnp.concatenate(low_weights[2:], axis=1)],
+        own_ids,
+        padded,
+        6,
+    )
+    ids_all = ids_all.reshape(row_count, group_tokens + pick_count)
+    tokens_all = ids_all[:, :group_tokens].reshape(row_count, col_count, device_tokens)
+    targets_all = ids_all[:, group_tokens:].reshape(row_count * pick_count)
+    local_tokens = jnp.moveaxis(tokens_all, 1, 0) - col_index * vocab_shard
+    inside = (local_tokens >= 0) & (local_tokens < vocab_shard)
+    local_tokens = jnp.where(inside, local_tokens, vocab_shard)
 
     qkv_width, ff_width = qkv_cols * col_count, ff_cols * col_count
-    mlp_low = mlp_weight.astype(low)
-    mlp_full = lax.all_gather(
-        jnp.concatenate([mlp_low[0], mlp_low[1], mlp_low[2]], axis=1),
-        ("col", "row"),
-        axis=0,
-        tiled=True,
-    ).reshape(col_count, width, 3 * ff_cols)
+    attn_full = lax.all_gather(attn_line, "row", axis=0, tiled=True)
+    mlp_line, ids_line = lax.optimization_barrier((mlp_line, local_tokens))
+    mlp_full = lax.all_gather(mlp_line, "row", axis=0, tiled=True)
     bases_low = left_bases.astype(low)
     left_block = jnp.concatenate([bases_low[k] for k in range(5)], axis=1)
-    columns = range(col_count)
+
+    def column_blocks(values, first, count):
+        span = values.shape[1] // col_count
+        return [
+            values[:, c * span + first : c * span + first + count] for c in range(col_count)
+        ]
+
+    qkv_full = column_blocks(attn_full, 0, qkv_cols)
+    out_full = column_blocks(attn_full, qkv_cols, out_cols)
     gate_full, up_full, down_full = (
-        [mlp_full[c, :, k * ff_cols : (k + 1) * ff_cols] for c in columns] for k in range(3)
+        column_blocks(mlp_full, k * ff_cols, ff_cols) for k in range(3)
     )
 
     def by_columns(values, weights, multiply):
@@ -1143,22 +1176,11 @@
         ]
         return functools.reduce(jnp.add, terms)
 
-    tokens_all = ids_all[:, :group_tokens].reshape(row_count, col_count, device_tokens)
-    targets_all = ids_all[:, group_tokens:].reshape(row_count * pick_count)
-    local_tokens = jnp.moveaxis(tokens_all, 1, 0) - col_index * vocab_shard
-    inside = (local_tokens >= 0) & (local_tokens < vocab_shard)
-    local_tokens = jnp.where(inside, local_tokens, vocab_shard)
-    table_low_t = table_first.astype(low).T
 
     def reduce_rows(values):
         return lax.psum_scatter(values, "row", scatter_dimension=0, tiled=True)
 
-    padded = jnp.pad(table_low_t, ((0, 0), (0, vocab_room - vocab_shard)))
-    attn_block = jnp.concatenate([qkv_weight.astype(low), output_weight.astype(low)], axis=1)
-    found, attn_full = lookup(local_tokens.reshape(-1), padded, attn_block, device_tokens, 6)
-    attn_full = attn_full.reshape(col_count, width, qkv_cols + out_cols)
-    qkv_full = [attn_full[c, :, :qkv_cols] for c in columns]
-    out_full = [attn_full[c, :, qkv_cols:] for c in columns]
+    found = lookup(local_tokens.reshape(-1), padded, device_tokens, 7)
     embedded = found.reshape(width, device_tokens).T.astype(jnp.float32)
 
     normed = rms_norm(embedded, norm_gains[0]).astype(low)
@@ -1179,7 +1201,7 @@
     )
     keys_local = rotate_here(keys_raw).astype(low).reshape(device_tokens, kv_width)
     own_pairs = jnp.concatenate([keys_local, project[:, query_width + kv_width :]], axis=1)
-    keys_values, table_part = gather(own_pairs, padded, 8)
+    keys_values = gather(own_pairs, 8)
     left_block, keys_values = lax.optimization_barrier((left_block, keys_values))
     left_full = lax.all_gather(left_block, "row", axis=0, tiled=True)
     keys_values = keys_values.reshape(LEN, 2 * kv_width)

time: 902 us -> 882 us (0.978)
  blocking collectives: 10.6 us -> 0 us
    pallas_call x2 -> x3, Pallas kernels: 196 us -> 174 us  [the longest x1 72.3 us: lookup(): pl.pallas_call(functools.partial(lookup_kernel, rows, cols), out_shape=ja...]
    pallas_call x1, Pallas kernels: 30.2 us -> 49.6 us  [spread(): pl.pallas_call(functools.partial(spread_kernel, rows, cols), out_shape=ja...]
    all_gather x1 -> x0, blocking collectives: 10.6 us -> none  [per_device(): lax.all_gather(jnp.concatenate([token_ids, target_ids]), 'row', axis=0)]
    unnamed x231 -> x228, local copies, waits for them, and re-layouts: 22.4 us -> 19.6 us
  transfers between devices with their start and end apart: 7 -> 8, of which waited for: 2 -> 4; matrix products, arithmetic and copies ran while one was open for 20% -> 19% of each run, Pallas kernels for 58% -> 51%
where the time goes in v5:
time: 882 us; the launch traced here: 873 us
  Pallas kernels  621 us (70%)
  matrix products  109 us (12%)
  other arithmetic  50.2 us (6%)
  local copies, waits for them, and re-layouts  48.9 us (6%)
  waiting for transfers between devices  24.1 us (3%)
  between operations  16.6 us (2%)
    pallas_call x2, Pallas kernels, soap(): pl.pallas_call(functools.partial(soap_kernel, rows, cols, adds, streamed)...  270 us
    pallas_call x1, Pallas kernels, lookup(): pl.pallas_call(functools.partial(lookup_kernel, rows, cols), out_shape=ja...  72.3 us
    pallas_call x1, Pallas kernels, line_up(): pl.pallas_call(functools.partial(line_up_kernel, rows, cols), out_shape=[...  68.5 us
    dot_general x21, matrix products, matmul_last(): lax.dot_general(left_op, right_op, (((1,), (1,)), ((), ())), preferred_el...  50.3 us
    pallas_call x1, Pallas kernels, spread(): pl.pallas_call(functools.partial(spread_kernel, rows, cols), out_shape=ja...  49.6 us
    dot_general x22, matrix products, matmul(): return jnp.dot(left_op, right_op, preferred_element_type=jnp.float32)  49.3 us
    pallas_call x5, Pallas kernels, outer(): pl.pallas_call(outer_kernel, grid=(other.shape[1] // block,), out_shape=j...  39.1 us
    pallas_call x2, Pallas kernels, attention_call(): pl.pallas_call(functools.partial(kernel, group), grid=(steps,), in_specs=...  39 us
  transfers between devices with their start and end apart: 8, of which 4 were waited for; matrix products, arithmetic and copies ran while one was open for 19% of the time, Pallas kernels for 51%

profile of v5, /device:TPU:0, one launch (start us, length us, event | category | flops | bytes accessed | tf_op | source)
XLA Modules:
  0.0 873.0 jit_solution(14537830104558069261)
XLA Ops:
  10.6 2.6 convert_bitcast_fusion
  17.2 68.5 %shard_map.351 = (bf16[144,3072]{1,0:T(8,128)(2,1)}, bf16[144,9216]{1,0:T(8,128)(2,1)}, s32[8,9,128]{2,1,0:T(8,128)}, bf16[8,144,1024]{2,1,0:T(8,128)(2,1)}) custom-call(bf16[144,768]{1,0:T(8,128)(2,1)} %pad_maximum_fusion.10.refs_0_, bf16[144,2304]{1,0:T(8,128)(2,1)} %pad_maximum_fusion.4.refs_1_, s32[9,128]{1,0:T(8,128)} %add_bitcast_fusion.refs_2_, ...), custom_call_target="tpu_custom_call" | custom-call | tf_op jit(solution)/shard_map/pallas_call | solution.py:815
  87.8 72.3 %shard_map.352 = bf16[8,144,256]{2,1,0:T(8,128)(2,1)} custom-call(s32[8192]{0:T(1024)} %bitcast.191, bf16[144,8192]{1,0:T(8,128)(2,1)} %pad.10.refs_3_.table_ref), custom_call_target="tpu_custom_call" | custom-call | tf_op jit(solution)/shard_map/pallas_call | solution.py:901
  161.6 2.1 convert_element_type.150
  166.8 2.0 convolution_convert_fusion.4
  168.8 1.9 convolution_convert_fusion.3
  172.8 33.7 %shard_map.353 = bf16[4,256,768]{2,1,0:T(8,128)(2,1)} custom-call(bf16[256,768]{1,0:T(8,128)(2,1)} %pad_maximum_fusion.5.x_ref), custom_call_target="tpu_custom_call" | custom-call | tf_op jit(solution)/shard_map/pallas_call | solution.py:989
  213.0 1.9 convolution_convert_fusion.6
  215.1 1.9 convolution_convert_fusion.5
  218.8 18.6 %shard_map.354 = (bf16[256,1152]{1,0:T(8,128)(2,1)}, f32[3,6,256]{2,1,0:T(8,128)}, bf16[256,1152]{1,0:T(8,128)(2,1)}) custom-call(s32[2]{0:T(128)} %pad_add_fusion.places_ref, bf16[256,1920]{1,0:T(8,128)(2,1)} %concatenate.54.raw_ref, bf16[1024,768]{1,0:T(8,128)(2,1)} %bitcast.179, bf16[1024,768]{1,0:T(8,128)(2,1)} %bitcast.180, ...), custom_call_target="tpu_custom_call" | custom-call | flops 2415919104 | bytes 9437184 | tf_op jit(solution)/shard_map/pallas_call | solution.py:666
  237.4 2.1 fusion.72
  239.5 1.9 convolution_add_fusion.14
  241.4 1.9 convolution_add_fusion.13
  243.3 2.8 multiply_reduce_fusion.6
  246.9 2.3 fusion.21
  249.2 3.0 fusion.24
  252.2 3.1 fusion.27
  255.3 2.7 fusion.31
  258.0 2.6 fusion.34
  260.6 2.4 fusion.37
  271.6 49.6 %shard_map.355 = bf16[8,4,32,1152]{3,2,1,0:T(8,128)(2,1)} custom-call(bf16[4,32,1152]{2,1,0:T(8,128)(2,1)} %bitcast.184), custom_call_target="tpu_custom_call" | custom-call | tf_op jit(solution)/shard_map/pallas_call | solution.py:148
  321.3 4.6 select_reduce_fusion.1
  326.0 2.2 exponential_reduce_fusion
  330.1 12.4 %shard_map.356 = f32[8,4,24,128]{3,2,1,0:T(8,128)} custom-call(f32[24,128]{1,0:T(8,128)} %reshape.307.x_ref), custom_call_target="tpu_custom_call" | custom-call | tf_op jit(solution)/shard_map/pallas_call | solution.py:83
  342.5 1.9 reshape.308
  344.5 2.1 slice_reduce_fusion
  347.9 8.5 convolution_convert_fusion.1
  356.5 35.7 %shard_map.357 = bf16[4,32,1152]{2,1,0:T(8,128)(2,1)} custom-call(bf16[8,4,32,1152]{3,2,1,0:T(8,128)(2,1)} %bitcast.172), custom_call_target="tpu_custom_call" | custom-call | tf_op jit(solution)/shard_map/pallas_call | solution.py:227
  392.2 2.2 multiply_reduce_fusion
  394.6 2.5 fusion.7
  397.1 2.2 fusion.10
  399.3 2.2 fusion.13
  401.5 2.3 fusion.16
  406.3 2.1 fusion.4.other_ref
  408.4 8.0 shard_map.358.refs_0_
  416.3 8.4 shard_map.359.refs_0_
  424.8 8.0 shard_map.360
  432.9 2.4 fusion.42
  435.4 2.3 fusion.29
  437.7 2.6 convolution_add_fusion.5
  440.4 2.7 convolution_add_fusion.4
  443.1 2.7 convolution_add_fusion.3
  445.7 2.6 convolution_add_fusion.2
  448.4 2.6 convolution_add_fusion.1
  451.0 3.5 multiply_reduce_fusion.1
  456.4 2.4 convolution_convert_fusion.10
  458.9 2.9 convolution_convert_fusion.9
  462.0 2.3 convolution_convert_fusion.8
  464.4 2.1 convolution_convert_fusion.7
  468.1 20.4 %shard_map.361 = (bf16[256,1152]{1,0:T(8,128)(2,1)}, bf16[2,1024,384]{2,1,0:T(8,128)(2,1)}) custom-call(s32[2]{0:T(128)} %pad_add_fusion.places_ref, bf16[256,1152]{1,0:T(8,128)(2,1)} %get-tuple-element.59.query_ref, bf16[1024,768]{1,0:T(8,128)(2,1)} %bitcast.181, bf16[1024,768]{1,0:T(8,128)(2,1)} %bitcast.182, f32[256,128]{1,0:T(8,128)} %copy.91.cosine_ref, ...), custom_call_target="tpu_custom_call" | custom-call | flops 2415919104 | bytes 9437184 | tf_op jit(solution)/shard_map/pallas_call | solution.py:666
  488.5 2.2 dynamic-slice_bitcast_fusion.2
  496.3 6.6 shard_map.362.refs_0_
  504.8 14.0 %collective-permute-done.1 = bf16[2,256,384]{2,1,0:T(8,128)(2,1)S(1)} collective-permute-done((bf16[2,256,384]{2,1,0:T(8,128)(2,1)S(1)}, bf16[2,256,384]{2,1,0:T(8,128)(2,1)S(1)}, u32[]{:S(2)}, u32[]{:S(2)}) %collective-permute-start.1) | collective-permute-done | bytes 393248 | tf_op jit(solution)/shard_map/ppermute | solution.py:1003
  524.3 1.8 convolution_add_fusion.10
  526.2 2.2 multiply_reduce_fusion.2
  531.8 8.1 shard_map.363
  543.1 3.3 copy.111
  546.4 2.4 copy.112
  548.8 2.7 copy.113.refs_12_
  553.9 6.9 convolution_convert_fusion
  561.4 8.6 reduce-scatter.5.cloned.1.call-done.refs_0_
  570.0 191.5 %shard_map.364 = (f32[3,144,768]{2,1,0:T(8,128)}, f32[3,144,768]{2,1,0:T(8,128)}, f32[3,144,768]{2,1,0:T(8,128)}, bf16[4,8,144,256]{3,2,1,0:T(8,128)(2,1)}, bf16...) custom-call(bf16[144,9216]{1,0:T(8,128)(2,1)} %reduce-scatter.5.cloned.1.call-done.refs_0_, f32[3,768,3072]{2,1,0:T(8,128)} %refs_1_.1, ...), custom_call_target="tpu_custom_call" | custom-call | tf_op jit(solution)/shard_map/pallas_call | solution.py:558
  765.6 79.0 %shard_map.365 = (f32[144,288]{1,0:T(8,128)}, f32[144,288]{1,0:T(8,128)}, f32[144,288]{1,0:T(8,128)}, f32[144,480]{1,0:T(8,128)}, f32[144,480]{1,0:T(8,128)}, /*index=5*/f32[144,480]{1,0:T(8,128)}, f32[144,8192]{1,0:T(8,128)}) custom-call(bf16[4,144,288]{2,1,0:T(8,128)(2,1)} %bitcast.174, bf16[4,144,480]{2,1,0:T(8,128)(2,1)} %bitcast.169, ...), custom_call_target="tpu_custom_call" | custom-call | tf_op jit(solution)/shard_map/pallas_call | solution.py:558
  844.6 12.8 %negate_add_fusion = (f32[8000,144]{0,1:T(8,128)}, f32[8000,144]{0,1:T(8,128)}, f32[8000,144]{0,1:T(8,128)}) fusion(f32[8000,144]{0,1:T(8,128)} %param.29, f32[144,8192]{1,0:T(8,128)} %get-tuple-element.71, f32[8000,144]{0,1:T(8,128)} %param.35, f32[8000,144]{0,1:T(8,128)} %param.34), kind=kLoop, calls=%fused_computation.4 | loop fusion | flops 14976000 | bytes 32256000 | tf_op jit(solution)/shard_map/add | solution.py:1338
  (344 shorter events, 78.2 us)
Async XLA Ops:
  7.2 159.6 %all-gather.4.cloned.1.call-start = ((), (), s32[]{:S(2)}) async-start(), calls=%async_computation.2 | async-start | bytes 7962624 | tf_op jit(solution)/shard_map/all_gather | solution.py:1150
  10.6 3.4 copy-start.92
  10.6 3.4 copy-start.103
  85.7 161.2 %all-gather.6.cloned.1.call-start = ((), (), s32[]{:S(2)}) async-start(), calls=%async_computation.3 | async-start | bytes 23887872 | tf_op jit(solution)/shard_map/all_gather | solution.py:1152
  86.5 321.9 %all-gather.8.cloned.1.call-start = ((), (), s32[]{:S(2)}) async-start(), calls=%async_computation.4 | async-start | bytes 14929920 | tf_op jit(solution)/shard_map/all_gather | solution.py:1206
  165.6 41.0 %copy-start.49 = (f32[256,32]{0,1:T(8,128)}, f32[256,32]{0,1:T(8,128)S(1)}, u32[]{:S(2)}) copy-start(f32[256,32]{0,1:T(8,128)S(1)} %get-tuple-element.131) | copy-start | bytes 98308
  165.6 41.8 %copy-start.51 = (f32[256,32]{0,1:T(8,128)}, f32[256,32]{0,1:T(8,128)S(1)}, u32[]{:S(2)}) copy-start(f32[256,32]{0,1:T(8,128)S(1)} %get-tuple-element.130) | copy-start | bytes 98308
  165.9 2.9 copy-start.34
  166.8 48.3 %copy-start.38 = (bf16[256,1152]{1,0:T(8,128)(2,1)}, bf16[256,1152]{1,0:T(8,128)(2,1)S(1)}, u32[]{:S(2)}) copy-start(bf16[256,1152]{1,0:T(8,128)(2,1)S(1)} %multiply_convert_fusion.5.values_ref) | copy-start | bytes 1769476
  168.8 2.8 copy-start.46
  172.8 34.6 %copy-start.62 = (f32[256,32]{0,1:T(8,128)S(1)}, f32[256,32]{0,1:T(8,128)}, u32[]{:S(2)}) copy-start(f32[256,32]{0,1:T(8,128)} %get-tuple-element.129) | copy-start | bytes 98308
  206.5 3.0 copy-start.105
  206.6 363.4 %reduce-scatter.5.cloned.1.call-start = ((), (), s32[]{:S(2)}) async-start(), calls=%async_computation.6 | async-start | bytes 23887872 | tf_op jit(solution)/shard_map/reduce_scatter | solution.py:1181
  246.2 3.1 copy-start.86
  246.2 3.1 copy-start.72
  246.4 17.4 %copy-start.19 = (bf16[256,1152]{1,0:T(8,128)(2,1)}, bf16[256,1152]{1,0:T(8,128)(2,1)S(1)}, u32[]{:S(2)}) copy-start(bf16[256,1152]{1,0:T(8,128)(2,1)S(1)} %multiply_convert_fusion.4.values_ref) | copy-start | bytes 1769476
  246.9 16.1 %copy-start.5 = (bf16[1152,9216]{1,0:T(8,128)(2,1)S(1)}, bf16[1152,9216]{1,0:T(8,128)(2,1)}, u32[]{:S(2)}) copy-start(bf16[1152,9216]{1,0:T(8,128)(2,1)} %all-gather.6.cloned.1.call-done) | copy-start | bytes 63700996
  249.2 15.2 %copy-start.25 = (f32[256,768]{1,0:T(8,128)}, f32[256,768]{1,0:T(8,128)S(1)}, u32[]{:S(2)}) copy-start(f32[256,768]{1,0:T(8,128)S(1)} %fusion.21) | copy-start | bytes 2359300
  252.2 12.2 %copy-start.27 = (f32[256,768]{1,0:T(8,128)}, f32[256,768]{1,0:T(8,128)S(1)}, u32[]{:S(2)}) copy-start(f32[256,768]{1,0:T(8,128)S(1)} %fusion.24) | copy-start | bytes 2359300
  255.3 9.1 %copy-start.29 = (f32[256,768]{1,0:T(8,128)}, f32[256,768]{1,0:T(8,128)S(1)}, u32[]{:S(2)}) copy-start(f32[256,768]{1,0:T(8,128)S(1)} %fusion.27) | copy-start | bytes 2359300
  258.0 6.5 copy-start.31
  260.6 3.9 copy-start.11
  270.6 50.7 %copy-start.101 = (pred[1024]{0:T(1024)(128)(4,1)S(1)}, pred[1024]{0:T(1024)(128)(4,1)}, u32[]{:S(2)}) copy-start(pred[1024]{0:T(1024)(128)(4,1)} %iota_compare_fusion.1) | copy-start | bytes 3076
  270.6 50.7 %copy-start.104 = (bf16[8,144,1024]{2,1,0:T(8,128)(2,1)S(1)}, bf16[8,144,1024]{2,1,0:T(8,128)(2,1)}, u32[]{:S(2)}) copy-start(bf16[8,144,1024]{2,1,0:T(8,128)(2,1)} %get-tuple-element.55) | copy-start | bytes 7077892
  321.3 4.7 copy-start.81
  347.9 8.5 copy-start.93
  347.9 8.5 copy-start.95
  356.4 35.7 %copy-start.67 = (f32[256]{0:T(256)S(1)}, f32[256]{0:T(256)}, u32[]{:S(2)}) copy-start(f32[256]{0:T(256)} %copy-done.66) | copy-start | bytes 3076
  356.4 35.7 %copy-start.98 = (s32[256]{0:T(256)S(1)}, s32[256]{0:T(256)}, u32[]{:S(2)}) copy-start(s32[256]{0:T(256)} %iota_add_fusion) | copy-start | bytes 3076
  356.4 35.7 %copy-start.100 = (s32[128]{0:T(128)S(1)}, s32[128]{0:T(128)}, u32[]{:S(2)}) copy-start(s32[128]{0:T(128)} %param.26) | copy-start | bytes 1540
  394.3 2.8 copy-start
  394.3 2.8 copy-start.77
  394.6 6.8 copy-start.39
  432.8 328.7 %reduce-scatter.3.cloned.1.call-start = ((), (), s32[]{:S(2)}) async-start(), calls=%async_computation.5 | async-start | bytes 7962624 | tf_op jit(solution)/shard_map/reduce_scatter | solution.py:1181
  448.3 2.6 copy-start.73
  451.0 3.6 copy-start.87
  451.0 3.6 copy-start.1
  451.0 3.6 copy-start.68
  451.0 3.6 copy-start.78
  458.8 3.2 copy-start.37
  488.5 6.0 copy-start.20
  490.7 14.2 %collective-permute-start.2 = (bf16[2,256,384]{2,1,0:T(8,128)(2,1)}, bf16[2,256,384]{2,1,0:T(8,128)(2,1)S(1)}, u32[]{:S(2)}, u32[]{:S(2)}) collective-permute-start(bf16[2,256,384]{2,1,0:T(8,128)(2,1)} %get-tuple-element.114), channel_id=1, source_target_pairs={{0,1},{1,2},{2,3},{3,0},{4,5},{5,6},{6,7},{7,4},{8,9},{9,10},{10,1... | collective-permute-start | bytes 1179656 | tf_op jit(solution)/shard_map/ppermute | solution.py:1003
  492.1 26.8 %collective-permute-start.1 = (bf16[2,256,384]{2,1,0:T(8,128)(2,1)S(1)}, bf16[2,256,384]{2,1,0:T(8,128)(2,1)S(1)}, u32[]{:S(2)}, u32[]{:S(2)}) collective-permute-start(bf16[2,256,384]{2,1,0:T(8,128)(2,1)S(1)} %get-tuple-element.115), channel_id=1, source_target_pairs={{0,2},{1,3},{2,0},{3,1},{4,6},{5,7},{6,4},{7,5},{8,10},{9,11},{10,... | collective-permute-start | bytes 1179656 | tf_op jit(solution)/shard_map/ppermute | solution.py:1003
  493.5 25.3 %collective-permute-start = (bf16[2,256,384]{2,1,0:T(8,128)(2,1)S(1)}, bf16[2,256,384]{2,1,0:T(8,128)(2,1)}, u32[]{:S(2)}, u32[]{:S(2)}) collective-permute-start(bf16[2,256,384]{2,1,0:T(8,128)(2,1)S(1)} %get-tuple-element.113), channel_id=1, source_target_pairs={{0,3},{1,0},{2,1},{3,2},{4,7},{5,4},{6,5},{7,6},{8,11},{9,8},{10,9... | collective-permute-start | bytes 1179656 | tf_op jit(solution)/shard_map/ppermute | solution.py:1003
  504.7 17.3 %copy-start.50 = (f32[256,32]{0,1:T(8,128)S(1)}, f32[256,32]{0,1:T(8,128)}, u32[]{:S(2)}) copy-start(f32[256,32]{0,1:T(8,128)} %copy-done.49) | copy-start | bytes 98308
  504.7 17.3 %copy-start.52 = (f32[256,32]{0,1:T(8,128)S(1)}, f32[256,32]{0,1:T(8,128)}, u32[]{:S(2)}) copy-start(f32[256,32]{0,1:T(8,128)} %copy-done.51) | copy-start | bytes 98308
  526.2 2.7 copy-start.22
  526.2 2.7 copy-start.69
  526.2 2.7 copy-start.74
  526.2 2.7 copy-start.79
  526.2 2.6 copy-start.85
  548.8 2.7 copy-start.4
  763.0 2.5 copy-start.48
  844.5 12.9 %copy-start.65 = (f32[3,1152]{1,0:T(4,128)S(1)}, f32[3,1152]{1,0:T(4,128)}, u32[]{:S(2)}) copy-start(f32[3,1152]{1,0:T(4,128)} %param.30) | copy-start | bytes 41476
  844.6 12.9 %copy-start.75 = (f32[3,1152]{1,0:T(4,128)S(1)}, f32[3,1152]{1,0:T(4,128)}, u32[]{:S(2)}) copy-start(f32[3,1152]{1,0:T(4,128)} %param.37) | copy-start | bytes 41476
  844.6 12.9 %copy-start.76 = (f32[3,1152]{1,0:T(4,128)S(1)}, f32[3,1152]{1,0:T(4,128)}, u32[]{:S(2)}) copy-start(f32[3,1152]{1,0:T(4,128)} %param.36) | copy-start | bytes 41476
  844.6 13.5 %copy-start.55 = (f32[144,480]{1,0:T(8,128)S(1)}, f32[144,480]{1,0:T(8,128)}, u32[]{:S(2)}) copy-start(f32[144,480]{1,0:T(8,128)} %get-tuple-element.162) | copy-start | bytes 829444
  844.6 14.2 %copy-start.54 = (f32[144,480]{1,0:T(8,128)S(1)}, f32[144,480]{1,0:T(8,128)}, u32[]{:S(2)}) copy-start(f32[144,480]{1,0:T(8,128)} %get-tuple-element.163) | copy-start | bytes 829444
  844.6 15.0 %copy-start.53 = (f32[144,480]{1,0:T(8,128)S(1)}, f32[144,480]{1,0:T(8,128)}, u32[]{:S(2)}) copy-start(f32[144,480]{1,0:T(8,128)} %get-tuple-element.164) | copy-start | bytes 829444
  844.6 15.7 %copy-start.58 = (f32[144,288]{1,0:T(8,128)S(1)}, f32[144,288]{1,0:T(8,128)}, u32[]{:S(2)}) copy-start(f32[144,288]{1,0:T(8,128)} %get-tuple-element.165) | copy-start | bytes 497668
  857.4 3.5 copy-start.57
  857.5 4.2 copy-start.56
  857.5 4.9 copy-start.45
  861.0 2.4 copy-start.44
  (52 other events, 97.3 us)
Sparse Core Ops, SparseCore 0:
  85.8 47.4 all-gather.3
  135.3 111.6 all-gather.5
  249.4 87.6 all-gather.7
  433.0 137.0 reduce-scatter.4
  573.4 75.8 reduce-scatter.2

commit v6 on v5

--- a/solution.py
+++ b/solution.py
@@ -24,7 +24,7 @@
 MESH = pl.DeviceIdType.MESH
 VMEM_LIMIT = 58 * 2**20
 VOCAB_TILE = 1024
-LOOK_STEP = 32
+LOOK_STEP = 64
 TILES_AT_ONCE = 3
 SKEW = 2
 SOAP_VMEM = 62 * 2**20
@@ -730,7 +730,7 @@
     def _():
         turned[...] = jnp.dot(
             values_ref[...], left_ref[...], preferred_element_type=jnp.float32
-        ).T.astype(turned.dtype)
+        ).astype(turned.dtype).T
 
     out_ref[...] = jnp.dot(
         turned[...], other_ref[...], preferred_element_type=jnp.float32

time: 882 us -> 882 us (level)
  no operation moved by 1% of the time
where the time goes in v6:
time: 882 us; the launch traced here: 874 us
  Pallas kernels  621 us (70%)
  matrix products  109 us (12%)
  other arithmetic  50.2 us (6%)
  local copies, waits for them, and re-layouts  48.9 us (6%)
  waiting for transfers between devices  24.5 us (3%)
  between operations  16.6 us (2%)
    pallas_call x2, Pallas kernels, soap(): pl.pallas_call(functools.partial(soap_kernel, rows, cols, adds, streamed)...  271 us
    pallas_call x1, Pallas kernels, lookup(): pl.pallas_call(functools.partial(lookup_kernel, rows, cols), out_shape=ja...  72 us
    pallas_call x1, Pallas kernels, line_up(): pl.pallas_call(functools.partial(line_up_kernel, rows, cols), out_shape=[...  68.5 us
    dot_general x21, matrix products, matmul_last(): lax.dot_general(left_op, right_op, (((1,), (1,)), ((), ())), preferred_el...  50.4 us
    dot_general x22, matrix products, matmul(): return jnp.dot(left_op, right_op, preferred_element_type=jnp.float32)  49.5 us
    pallas_call x1, Pallas kernels, spread(): pl.pallas_call(functools.partial(spread_kernel, rows, cols), out_shape=ja...  48.5 us
    pallas_call x2, Pallas kernels, attention_call(): pl.pallas_call(functools.partial(kernel, group), grid=(steps,), in_specs=...  39 us
    pallas_call x5, Pallas kernels, outer(): pl.pallas_call(outer_kernel, grid=(other.shape[1] // block,), out_shape=j...  38.9 us
  transfers between devices with their start and end apart: 8, of which 4 were waited for; matrix products, arithmetic and copies ran while one was open for 19% of the time, Pallas kernels for 51%

profile of v6, /device:TPU:0, one launch (start us, length us, event | category | flops | bytes accessed | tf_op | source)
XLA Modules:
  0.0 873.7 jit_solution(14727430102512862112)
XLA Ops:
  10.6 2.6 convert_bitcast_fusion
  17.2 68.5 %shard_map.351 = (bf16[144,3072]{1,0:T(8,128)(2,1)}, bf16[144,9216]{1,0:T(8,128)(2,1)}, s32[8,9,128]{2,1,0:T(8,128)}, bf16[8,144,1024]{2,1,0:T(8,128)(2,1)}) custom-call(bf16[144,768]{1,0:T(8,128)(2,1)} %pad_maximum_fusion.10.refs_0_, bf16[144,2304]{1,0:T(8,128)(2,1)} %pad_maximum_fusion.4.refs_1_, s32[9,128]{1,0:T(8,128)} %add_bitcast_fusion.refs_2_, ...), custom_call_target="tpu_custom_call" | custom-call | tf_op jit(solution)/shard_map/pallas_call | solution.py:815
  87.8 72.0 %shard_map.352 = bf16[8,144,256]{2,1,0:T(8,128)(2,1)} custom-call(s32[8192]{0:T(1024)} %bitcast.191, bf16[144,8192]{1,0:T(8,128)(2,1)} %pad.10.refs_3_.table_ref), custom_call_target="tpu_custom_call" | custom-call | tf_op jit(solution)/shard_map/pallas_call | solution.py:901
  161.4 2.1 convert_element_type.150
  166.6 2.0 convolution_convert_fusion.4
  168.6 1.9 convolution_convert_fusion.3
  172.6 33.7 %shard_map.353 = bf16[4,256,768]{2,1,0:T(8,128)(2,1)} custom-call(bf16[256,768]{1,0:T(8,128)(2,1)} %pad_maximum_fusion.5.x_ref), custom_call_target="tpu_custom_call" | custom-call | tf_op jit(solution)/shard_map/pallas_call | solution.py:989
  212.8 1.9 convolution_convert_fusion.6
  214.8 1.9 convolution_convert_fusion.5
  218.5 18.6 %shard_map.354 = (bf16[256,1152]{1,0:T(8,128)(2,1)}, f32[3,6,256]{2,1,0:T(8,128)}, bf16[256,1152]{1,0:T(8,128)(2,1)}) custom-call(s32[2]{0:T(128)} %pad_add_fusion.places_ref, bf16[256,1920]{1,0:T(8,128)(2,1)} %concatenate.54.raw_ref, bf16[1024,768]{1,0:T(8,128)(2,1)} %bitcast.179, bf16[1024,768]{1,0:T(8,128)(2,1)} %bitcast.180, ...), custom_call_target="tpu_custom_call" | custom-call | flops 2415919104 | bytes 9437184 | tf_op jit(solution)/shard_map/pallas_call | solution.py:666
  237.1 2.1 fusion.72
  239.2 1.9 convolution_add_fusion.14
  241.1 1.9 convolution_add_fusion.13
  243.0 2.8 multiply_reduce_fusion.6
  246.9 2.3 fusion.21
  249.2 3.0 fusion.24
  252.2 3.1 fusion.27
  255.3 2.7 fusion.31
  258.0 2.6 fusion.34
  260.6 2.4 fusion.37
  271.7 48.5 %shard_map.355 = bf16[8,4,32,1152]{3,2,1,0:T(8,128)(2,1)} custom-call(bf16[4,32,1152]{2,1,0:T(8,128)(2,1)} %bitcast.184), custom_call_target="tpu_custom_call" | custom-call | tf_op jit(solution)/shard_map/pallas_call | solution.py:148
  320.2 4.7 select_reduce_fusion.1
  324.9 2.2 exponential_reduce_fusion
  329.1 13.5 %shard_map.356 = f32[8,4,24,128]{3,2,1,0:T(8,128)} custom-call(f32[24,128]{1,0:T(8,128)} %reshape.307.x_ref), custom_call_target="tpu_custom_call" | custom-call | tf_op jit(solution)/shard_map/pallas_call | solution.py:83
  342.6 1.9 reshape.308
  344.5 2.1 slice_reduce_fusion
  347.9 8.5 convolution_convert_fusion.1
  356.5 35.7 %shard_map.357 = bf16[4,32,1152]{2,1,0:T(8,128)(2,1)} custom-call(bf16[8,4,32,1152]{3,2,1,0:T(8,128)(2,1)} %bitcast.172), custom_call_target="tpu_custom_call" | custom-call | tf_op jit(solution)/shard_map/pallas_call | solution.py:227
  392.2 2.2 multiply_reduce_fusion
  394.7 2.5 fusion.7
  397.2 2.2 fusion.10
  399.3 2.2 fusion.13
  401.5 2.3 fusion.16
  406.3 2.1 fusion.4.other_ref
  408.4 7.9 shard_map.358.refs_0_
  416.3 8.4 shard_map.359.refs_0_
  424.8 8.0 shard_map.360
  432.9 2.4 fusion.42
  435.3 2.3 fusion.29
  437.7 2.7 convolution_add_fusion.5
  440.4 2.7 convolution_add_fusion.4
  443.1 2.6 convolution_add_fusion.3
  445.7 2.6 convolution_add_fusion.2
  448.4 2.6 convolution_add_fusion.1
  451.0 3.6 multiply_reduce_fusion.1
  456.5 2.5 convolution_convert_fusion.10
  459.2 2.9 convolution_convert_fusion.9
  462.2 2.3 convolution_convert_fusion.8
  464.6 2.1 convolution_convert_fusion.7
  468.3 20.4 %shard_map.361 = (bf16[256,1152]{1,0:T(8,128)(2,1)}, bf16[2,1024,384]{2,1,0:T(8,128)(2,1)}) custom-call(s32[2]{0:T(128)} %pad_add_fusion.places_ref, bf16[256,1152]{1,0:T(8,128)(2,1)} %get-tuple-element.59.query_ref, bf16[1024,768]{1,0:T(8,128)(2,1)} %bitcast.181, bf16[1024,768]{1,0:T(8,128)(2,1)} %bitcast.182, f32[256,128]{1,0:T(8,128)} %copy.91.cosine_ref, ...), custom_call_target="tpu_custom_call" | custom-call | flops 2415919104 | bytes 9437184 | tf_op jit(solution)/shard_map/pallas_call | solution.py:666
  488.7 2.2 dynamic-slice_bitcast_fusion.2
  491.8 1.9 collective-permute-start.1
  496.5 6.5 shard_map.362.refs_0_
  505.1 14.1 %collective-permute-done.1 = bf16[2,256,384]{2,1,0:T(8,128)(2,1)S(1)} collective-permute-done((bf16[2,256,384]{2,1,0:T(8,128)(2,1)S(1)}, bf16[2,256,384]{2,1,0:T(8,128)(2,1)S(1)}, u32[]{:S(2)}, u32[]{:S(2)}) %collective-permute-start.1) | collective-permute-done | bytes 393248 | tf_op jit(solution)/shard_map/ppermute | solution.py:1003
  526.6 2.2 multiply_reduce_fusion.2
  532.2 8.0 shard_map.363
  543.4 3.3 copy.111
  546.7 2.4 copy.112
  549.1 2.7 copy.113.refs_12_
  554.2 6.9 convolution_convert_fusion
  561.7 8.6 reduce-scatter.5.cloned.1.call-done.refs_0_
  570.3 191.7 %shard_map.364 = (f32[3,144,768]{2,1,0:T(8,128)}, f32[3,144,768]{2,1,0:T(8,128)}, f32[3,144,768]{2,1,0:T(8,128)}, bf16[4,8,144,256]{3,2,1,0:T(8,128)(2,1)}, bf16...) custom-call(bf16[144,9216]{1,0:T(8,128)(2,1)} %reduce-scatter.5.cloned.1.call-done.refs_0_, f32[3,768,3072]{2,1,0:T(8,128)} %refs_1_.1, ...), custom_call_target="tpu_custom_call" | custom-call | tf_op jit(solution)/shard_map/pallas_call | solution.py:558
  766.0 79.2 %shard_map.365 = (f32[144,288]{1,0:T(8,128)}, f32[144,288]{1,0:T(8,128)}, f32[144,288]{1,0:T(8,128)}, f32[144,480]{1,0:T(8,128)}, f32[144,480]{1,0:T(8,128)}, /*index=5*/f32[144,480]{1,0:T(8,128)}, f32[144,8192]{1,0:T(8,128)}) custom-call(bf16[4,144,288]{2,1,0:T(8,128)(2,1)} %bitcast.174, bf16[4,144,480]{2,1,0:T(8,128)(2,1)} %bitcast.169, ...), custom_call_target="tpu_custom_call" | custom-call | tf_op jit(solution)/shard_map/pallas_call | solution.py:558
  845.3 12.8 %negate_add_fusion = (f32[8000,144]{0,1:T(8,128)}, f32[8000,144]{0,1:T(8,128)}, f32[8000,144]{0,1:T(8,128)}) fusion(f32[8000,144]{0,1:T(8,128)} %param.29, f32[144,8192]{1,0:T(8,128)} %get-tuple-element.71, f32[8000,144]{0,1:T(8,128)} %param.35, f32[8000,144]{0,1:T(8,128)} %param.34), kind=kLoop, calls=%fused_computation.4 | loop fusion | flops 14976000 | bytes 32256000 | tf_op jit(solution)/shard_map/add | solution.py:1338
  (344 shorter events, 78.5 us)
Async XLA Ops:
  7.2 159.4 %all-gather.4.cloned.1.call-start = ((), (), s32[]{:S(2)}) async-start(), calls=%async_computation.2 | async-start | bytes 7962624 | tf_op jit(solution)/shard_map/all_gather | solution.py:1150
  10.6 3.4 copy-start.92
  10.6 3.4 copy-start.103
  85.7 161.2 %all-gather.6.cloned.1.call-start = ((), (), s32[]{:S(2)}) async-start(), calls=%async_computation.3 | async-start | bytes 23887872 | tf_op jit(solution)/shard_map/all_gather | solution.py:1152
  86.5 321.9 %all-gather.8.cloned.1.call-start = ((), (), s32[]{:S(2)}) async-start(), calls=%async_computation.4 | async-start | bytes 14929920 | tf_op jit(solution)/shard_map/all_gather | solution.py:1206
  165.4 41.0 %copy-start.49 = (f32[256,32]{0,1:T(8,128)}, f32[256,32]{0,1:T(8,128)S(1)}, u32[]{:S(2)}) copy-start(f32[256,32]{0,1:T(8,128)S(1)} %get-tuple-element.131) | copy-start | bytes 98308
  165.4 41.8 %copy-start.51 = (f32[256,32]{0,1:T(8,128)}, f32[256,32]{0,1:T(8,128)S(1)}, u32[]{:S(2)}) copy-start(f32[256,32]{0,1:T(8,128)S(1)} %get-tuple-element.130) | copy-start | bytes 98308
  165.6 2.9 copy-start.34
  166.5 48.3 %copy-start.38 = (bf16[256,1152]{1,0:T(8,128)(2,1)}, bf16[256,1152]{1,0:T(8,128)(2,1)S(1)}, u32[]{:S(2)}) copy-start(bf16[256,1152]{1,0:T(8,128)(2,1)S(1)} %multiply_convert_fusion.5.values_ref) | copy-start | bytes 1769476
  168.6 2.8 copy-start.46
  172.6 34.6 %copy-start.62 = (f32[256,32]{0,1:T(8,128)S(1)}, f32[256,32]{0,1:T(8,128)}, u32[]{:S(2)}) copy-start(f32[256,32]{0,1:T(8,128)} %get-tuple-element.129) | copy-start | bytes 98308
  206.3 3.0 copy-start.105
  206.3 364.0 %reduce-scatter.5.cloned.1.call-start = ((), (), s32[]{:S(2)}) async-start(), calls=%async_computation.6 | async-start | bytes 23887872 | tf_op jit(solution)/shard_map/reduce_scatter | solution.py:1181
  245.9 3.4 copy-start.86
  245.9 3.4 copy-start.72
  246.1 17.7 %copy-start.19 = (bf16[256,1152]{1,0:T(8,128)(2,1)}, bf16[256,1152]{1,0:T(8,128)(2,1)S(1)}, u32[]{:S(2)}) copy-start(bf16[256,1152]{1,0:T(8,128)(2,1)S(1)} %multiply_convert_fusion.4.values_ref) | copy-start | bytes 1769476
  246.9 16.1 %copy-start.5 = (bf16[1152,9216]{1,0:T(8,128)(2,1)S(1)}, bf16[1152,9216]{1,0:T(8,128)(2,1)}, u32[]{:S(2)}) copy-start(bf16[1152,9216]{1,0:T(8,128)(2,1)} %all-gather.6.cloned.1.call-done) | copy-start | bytes 63700996
  249.2 15.2 %copy-start.25 = (f32[256,768]{1,0:T(8,128)}, f32[256,768]{1,0:T(8,128)S(1)}, u32[]{:S(2)}) copy-start(f32[256,768]{1,0:T(8,128)S(1)} %fusion.21) | copy-start | bytes 2359300
  252.2 12.3 %copy-start.27 = (f32[256,768]{1,0:T(8,128)}, f32[256,768]{1,0:T(8,128)S(1)}, u32[]{:S(2)}) copy-start(f32[256,768]{1,0:T(8,128)S(1)} %fusion.24) | copy-start | bytes 2359300
  255.3 9.2 %copy-start.29 = (f32[256,768]{1,0:T(8,128)}, f32[256,768]{1,0:T(8,128)S(1)}, u32[]{:S(2)}) copy-start(f32[256,768]{1,0:T(8,128)S(1)} %fusion.27) | copy-start | bytes 2359300
  258.0 6.5 copy-start.31
  260.6 3.9 copy-start.11
  270.6 49.6 %copy-start.101 = (pred[1024]{0:T(1024)(128)(4,1)S(1)}, pred[1024]{0:T(1024)(128)(4,1)}, u32[]{:S(2)}) copy-start(pred[1024]{0:T(1024)(128)(4,1)} %iota_compare_fusion.1) | copy-start | bytes 3076
  270.6 49.6 %copy-start.104 = (bf16[8,144,1024]{2,1,0:T(8,128)(2,1)S(1)}, bf16[8,144,1024]{2,1,0:T(8,128)(2,1)}, u32[]{:S(2)}) copy-start(bf16[8,144,1024]{2,1,0:T(8,128)(2,1)} %get-tuple-element.55) | copy-start | bytes 7077892
  320.2 4.7 copy-start.81
  347.9 8.5 copy-start.93
  347.9 8.5 copy-start.95
  356.5 35.7 %copy-start.67 = (f32[256]{0:T(256)S(1)}, f32[256]{0:T(256)}, u32[]{:S(2)}) copy-start(f32[256]{0:T(256)} %copy-done.66) | copy-start | bytes 3076
  356.5 35.7 %copy-start.98 = (s32[256]{0:T(256)S(1)}, s32[256]{0:T(256)}, u32[]{:S(2)}) copy-start(s32[256]{0:T(256)} %iota_add_fusion) | copy-start | bytes 3076
  356.5 35.7 %copy-start.100 = (s32[128]{0:T(128)S(1)}, s32[128]{0:T(128)}, u32[]{:S(2)}) copy-start(s32[128]{0:T(128)} %param.26) | copy-start | bytes 1540
  394.3 2.8 copy-start
  394.4 2.8 copy-start.77
  394.6 6.8 copy-start.39
  432.8 329.2 %reduce-scatter.3.cloned.1.call-start = ((), (), s32[]{:S(2)}) async-start(), calls=%async_computation.5 | async-start | bytes 7962624 | tf_op jit(solution)/shard_map/reduce_scatter | solution.py:1181
  448.4 2.6 copy-start.73
  451.0 3.7 copy-start.87
  451.0 3.7 copy-start.1
  451.0 3.7 copy-start.68
  451.0 3.7 copy-start.78
  459.0 3.2 copy-start.37
  488.7 6.0 copy-start.20
  490.9 14.2 %collective-permute-start.2 = (bf16[2,256,384]{2,1,0:T(8,128)(2,1)}, bf16[2,256,384]{2,1,0:T(8,128)(2,1)S(1)}, u32[]{:S(2)}, u32[]{:S(2)}) collective-permute-start(bf16[2,256,384]{2,1,0:T(8,128)(2,1)} %get-tuple-element.114), channel_id=1, source_target_pairs={{0,1},{1,2},{2,3},{3,0},{4,5},{5,6},{6,7},{7,4},{8,9},{9,10},{10,1... | collective-permute-start | bytes 1179656 | tf_op jit(solution)/shard_map/ppermute | solution.py:1003
  491.8 27.4 %collective-permute-start.1 = (bf16[2,256,384]{2,1,0:T(8,128)(2,1)S(1)}, bf16[2,256,384]{2,1,0:T(8,128)(2,1)S(1)}, u32[]{:S(2)}, u32[]{:S(2)}) collective-permute-start(bf16[2,256,384]{2,1,0:T(8,128)(2,1)S(1)} %get-tuple-element.115), channel_id=1, source_target_pairs={{0,2},{1,3},{2,0},{3,1},{4,6},{5,7},{6,4},{7,5},{8,10},{9,11},{10,... | collective-permute-start | bytes 1179656 | tf_op jit(solution)/shard_map/ppermute | solution.py:1003
  493.7 25.5 %collective-permute-start = (bf16[2,256,384]{2,1,0:T(8,128)(2,1)S(1)}, bf16[2,256,384]{2,1,0:T(8,128)(2,1)}, u32[]{:S(2)}, u32[]{:S(2)}) collective-permute-start(bf16[2,256,384]{2,1,0:T(8,128)(2,1)S(1)} %get-tuple-element.113), channel_id=1, source_target_pairs={{0,3},{1,0},{2,1},{3,2},{4,7},{5,4},{6,5},{7,6},{8,11},{9,8},{10,9... | collective-permute-start | bytes 1179656 | tf_op jit(solution)/shard_map/ppermute | solution.py:1003
  504.9 17.4 %copy-start.50 = (f32[256,32]{0,1:T(8,128)S(1)}, f32[256,32]{0,1:T(8,128)}, u32[]{:S(2)}) copy-start(f32[256,32]{0,1:T(8,128)} %copy-done.49) | copy-start | bytes 98308
  504.9 17.4 %copy-start.52 = (f32[256,32]{0,1:T(8,128)S(1)}, f32[256,32]{0,1:T(8,128)}, u32[]{:S(2)}) copy-start(f32[256,32]{0,1:T(8,128)} %copy-done.51) | copy-start | bytes 98308
  526.6 2.7 copy-start.22
  526.6 2.7 copy-start.69
  526.6 2.7 copy-start.74
  526.6 2.7 copy-start.79
  526.6 2.6 copy-start.85
  549.1 2.7 copy-start.4
  763.4 2.5 copy-start.48
  845.2 12.9 %copy-start.65 = (f32[3,1152]{1,0:T(4,128)S(1)}, f32[3,1152]{1,0:T(4,128)}, u32[]{:S(2)}) copy-start(f32[3,1152]{1,0:T(4,128)} %param.30) | copy-start | bytes 41476
  845.2 12.9 %copy-start.75 = (f32[3,1152]{1,0:T(4,128)S(1)}, f32[3,1152]{1,0:T(4,128)}, u32[]{:S(2)}) copy-start(f32[3,1152]{1,0:T(4,128)} %param.37) | copy-start | bytes 41476
  845.2 12.9 %copy-start.76 = (f32[3,1152]{1,0:T(4,128)S(1)}, f32[3,1152]{1,0:T(4,128)}, u32[]{:S(2)}) copy-start(f32[3,1152]{1,0:T(4,128)} %param.36) | copy-start | bytes 41476
  845.2 13.5 %copy-start.55 = (f32[144,480]{1,0:T(8,128)S(1)}, f32[144,480]{1,0:T(8,128)}, u32[]{:S(2)}) copy-start(f32[144,480]{1,0:T(8,128)} %get-tuple-element.162) | copy-start | bytes 829444
  845.2 14.2 %copy-start.54 = (f32[144,480]{1,0:T(8,128)S(1)}, f32[144,480]{1,0:T(8,128)}, u32[]{:S(2)}) copy-start(f32[144,480]{1,0:T(8,128)} %get-tuple-element.163) | copy-start | bytes 829444
  845.3 15.0 %copy-start.53 = (f32[144,480]{1,0:T(8,128)S(1)}, f32[144,480]{1,0:T(8,128)}, u32[]{:S(2)}) copy-start(f32[144,480]{1,0:T(8,128)} %get-tuple-element.164) | copy-start | bytes 829444
  845.3 15.7 %copy-start.58 = (f32[144,288]{1,0:T(8,128)S(1)}, f32[144,288]{1,0:T(8,128)}, u32[]{:S(2)}) copy-start(f32[144,288]{1,0:T(8,128)} %get-tuple-element.165) | copy-start | bytes 497668
  858.1 3.5 copy-start.57
  858.1 4.2 copy-start.56
  858.1 4.9 copy-start.45
  861.6 2.4 copy-start.44
  (52 other events, 97.3 us)
Sparse Core Ops, SparseCore 0:
  85.8 47.4 all-gather.3
  135.3 111.5 all-gather.5
  249.4 87.6 all-gather.7
  432.9 137.3 reduce-scatter.4
  573.7 75.8 reduce-scatter.2
